TPU v7x, 512 devices: a whole 4x4x16 slice. The times are simulated.
512 devices in a mesh: gx: 64 (over x, z_lo, core), gy: 8 (over z_hi, y).
Axes of the slice: x: 4, y: 4, z: 16 (z_hi: 2, z_lo: 8; z = z_hi * 8 + z_lo), core: 2. Of those that a mesh axis runs over, the one named last changes fastest.
Arguments:
- ensemble: float32 [32, 2, 2, 256, 1024], P(None, None, None, 'gx', 'gy')
- courant: float32 [2], replicated, may hold values from 0.25 to 0.5
- target_spread: float32 [2, 2], replicated, may hold values from 0.5 to 2
- obs_error: float32 [2], replicated, may hold values from 0.2 to 1
- obs_value: float32 [3, 512], replicated, may hold values from -8 to 8
- obs_owner: int32 [3, 512], replicated, may hold values from 0 to 511, as said below
- obs_cell: int32 [3, 512], replicated, may hold values from 0 to 511
- obs_kind: int32 [3, 512], replicated, may hold values from 0 to 1
- tile_mask: int32 [3, 64, 8, 512], P(None, 'gx', 'gy'), may hold values from 0 to 1, as said below
- batch_order: int32 [3], replicated, may hold values from 0 to 2, each once
Outputs:
- analysis: float32 [32, 2, 2, 256, 1024], P(None, None, None, 'gx', 'gy')
Inputs may be any that keep to these rules, and one draw needn't show every extreme that they name: obs_owner[b, j] is the tile tx * 8 + ty whose cells hold observation j; every batch names the first and the last tile. tile_mask[b, tx, ty, j] is 0 wherever the periodic distance between tx and obs_owner[b, j] // 8 exceeds 2 tiles.
All inputs are finite; a program needn't handle non-finite values.
Results may differ from a plain program's by a relative error of at most 0.00011.
Values sent between devices are 32-bit elements; how exact they have to be, the bound alone decides.
No kernel may reach another device: no remote copies, remote signals or barrier semaphores. Data moves between devices by JAX's collectives and lax.ppermute only.
A program may use at most 64 MiB of HBM per device.

v0:
```python
import jax
import jax.numpy as jnp
from jax import lax
from jax.sharding import PartitionSpec as P

BATCHES = 3
STEPS = 2
RX = 2
LOC_X = 12


diffuse_rate = 0.1
mixing_rate = 0.05
spread_floor = 1e-05


def extended(block, sides, width, periodic):
    for axis, dim in sides:
        count = lax.axis_size(axis)
        forward = [(i, i + 1) for i in range(count - 1)]
        if periodic:
            forward.append((count - 1, 0))
        backward = [(target, source) for source, target in forward]
        low = lax.ppermute(
            lax.slice_in_dim(block, block.shape[dim] - width, None, axis=dim), axis, forward
        )
        high = lax.ppermute(lax.slice_in_dim(block, 0, width, axis=dim), axis, backward)
        block = jnp.concatenate([low, block, high], axis=dim)
    return block


def from_behind(value, axis, steps):
    count = lax.axis_size(axis)
    pairs = [(source, (source + steps) % count) for source in range(count)]
    return lax.ppermute(value, axis, pairs)


def advance(padded, courant):
    centre = padded[..., 1:-1, 1:-1]
    upwind = padded[..., :-2, 1:-1]
    downwind = padded[..., 2:, 1:-1]
    lower = padded[..., 1:-1, :-2]
    upper = padded[..., 1:-1, 2:]
    below = jnp.concatenate([centre[:, :, :1], centre[:, :, :-1]], axis=2)
    above = jnp.concatenate([centre[:, :, 1:], centre[:, :, -1:]], axis=2)
    speed = courant[None, None, :, None, None]
    return (
        centre
        + speed * (upwind - centre)
        + diffuse_rate * (upwind + downwind + lower + upper - 4.0 * centre)
        + mixing_rate * (below + above - 2.0 * centre)
    )


def taper_of(xs, ys, ox, oy, width_x, loc_x, loc_y):
    gap_x = jnp.abs(xs[:, None, None] - ox[None, None, :])
    gap_x = jnp.minimum(gap_x, width_x - gap_x).astype(jnp.float32) / loc_x
    gap_y = jnp.abs(ys[None, :, None] - oy[None, None, :]).astype(jnp.float32) / loc_y
    room = jnp.maximum(1.0 - gap_x * gap_x - gap_y * gap_y, 0.0)
    return room * room


def local(
    ensemble,
    courant,
    target_spread,
    obs_error,
    obs_value,
    obs_owner,
    obs_cell,
    obs_kind,
    tile_mask,
    batch_order,
):
    members, fields, levels, rows_x, rows_y = ensemble.shape
    tiles_x = lax.axis_size("gx")
    tiles_y = lax.axis_size("gy")
    place_x = lax.axis_index("gx")
    place_y = lax.axis_index("gy")
    width_x = rows_x * tiles_x
    width_y = rows_y * tiles_y
    state = ensemble
    for step in range(STEPS):
        wide = extended(state, (("gx", 3),), 1, True)
        wide = extended(wide, (("gy", 4),), 1, False)
        state = advance(wide, courant)
    cells_all = float(width_x * width_y)
    centre = jnp.mean(state, axis=0)
    deviation = state - centre
    cell_var = jnp.sum(deviation * deviation, axis=0) / (members - 1)
    local_var = jnp.sum(cell_var, axis=(2, 3))
    totals = lax.psum(local_var, ("gx", "gy"))
    stretch = jnp.sqrt(target_spread / (totals / cells_all + spread_floor))
    state = centre + stretch[None, :, :, None, None] * deviation
    owner_me = place_x * tiles_y + place_y
    scale = 1.0 / (members - 1)
    loc_x = float(LOC_X)
    loc_y = float(width_y // 2)
    xs = place_x * rows_x + jnp.arange(rows_x, dtype=jnp.int32)
    ys = place_y * rows_y + jnp.arange(rows_y, dtype=jnp.int32)
    field_ids = jnp.arange(fields, dtype=jnp.int32)
    for turn in range(BATCHES):
        batch = batch_order[turn]
        owner = obs_owner[batch]
        cell = obs_cell[batch]
        kind = obs_kind[batch]
        value = obs_value[batch]
        kind_onehot = (kind[None, :] == field_ids[:, None]).astype(jnp.float32)
        ground = state[:, :, 0].reshape(members, fields * rows_x * rows_y)
        picked = jnp.take(ground, kind * (rows_x * rows_y) + cell, axis=1)
        contrib = jnp.where((owner == owner_me)[None, :], picked, 0.0)
        column = lax.psum(contrib, "gy")
        prior = column
        for reach in range(1, RX + 1):
            for sign in (1, -1):
                prior = prior + from_behind(column, "gx", sign * reach)
        error = jnp.sum(kind_onehot * obs_error[:, None], axis=0)
        prior_mean = jnp.mean(prior, axis=0)
        prior_dev = prior - prior_mean
        prior_var = jnp.sum(prior_dev * prior_dev, axis=0) / (members - 1)
        gain = (value - prior_mean) / (prior_var + error)
        shrink = -1.0 / (jnp.sqrt(error * (error + prior_var)) + error + prior_var)
        drive = gain[None, :] + shrink[None, :] * prior_dev
        ox = owner // tiles_y * rows_x + cell // rows_y
        oy = owner % tiles_y * rows_y + cell % rows_y
        own_mask = tile_mask[batch, 0, 0].astype(jnp.float32)
        weight = taper_of(xs, ys, ox, oy, width_x, loc_x, loc_y) * own_mask[None, None, :]
        weight = weight.reshape(rows_x * rows_y, -1)
        state_dev = state - jnp.mean(state, axis=0)
        blocks = []
        for field in range(fields):
            for level in range(levels):
                flat = state_dev[:, field, level].reshape(members, rows_x * rows_y)
                covariance = (
                    lax.dot_general(
                        flat, prior_dev, (((0,), (0,)), ((), ())), precision=lax.Precision.HIGHEST
                    )
                    * scale
                )
                increment = lax.dot_general(
                    drive,
                    covariance * weight,
                    (((1,), (1,)), ((), ())),
                    precision=lax.Precision.HIGHEST,
                )
                blocks.append(increment.reshape(members, rows_x, rows_y))
        state = state + jnp.stack(blocks, axis=1).reshape(members, fields, levels, rows_x, rows_y)
    return state


def solution(mesh):
    in_specs = (
        P(None, None, None, "gx", "gy"),
        P(),
        P(),
        P(),
        P(),
        P(),
        P(),
        P(),
        P(None, "gx", "gy", None),
        P(),
    )
    out_specs = P(None, None, None, "gx", "gy")
    return jax.shard_map(local, mesh=mesh, in_specs=in_specs, out_specs=out_specs, check_vma=False)
```

profile of v0, /device:TPU:1, one launch (start us, length us, event | category | flops | bytes accessed | tf_op | source)
XLA Modules:
  0.0 865.7 jit_solution(13704922205044798056)
XLA Ops:
  6.5 1.9 fusion.155
  8.4 4.9 collective-permute-start
  13.3 5.8 collective-permute-start.1
  32.5 1.3 collective-permute-start.2
  33.9 1.3 collective-permute-start.3
  35.2 4.8 collective-permute-done.2
  40.0 3.8 collective-permute-done.3
  44.5 2.1 fusion.26
  46.7 7.8 collective-permute-start.4
  54.5 7.6 collective-permute-start.5
  63.4 2.5 collective-permute-start.6
  65.9 1.3 collective-permute-start.7
  67.2 4.7 collective-permute-done.6
  71.9 12.4 %collective-permute-done.7 = f32[32,2,2,6,1]{4,3,2,1,0:T(8,128)S(1)} collective-permute-done((f32[32,2,2,6,1]{4,3,2,1,0:T(8,128)S(1)}, f32[32,2,2,6,1]{4,3,2,1,0:T(8,128)S(1)}, u32[]{:S(2)}, u32[]{:S(2)}) %collective-permute-start.7) | collective-permute-done | bytes 3104 | tf_op jit(solution)/shard_map/ppermute | solution.py:27
  86.4 185.8 %psum.28 = f32[2,2]{1,0:T(2,128)S(1)} all-reduce(f32[2,2]{1,0:T(2,128)S(1)} %multiply_reduce_fusion.4), channel_id=1, replica_groups=mesh['gx'=64,'gy'=8] {'gx','gy'}, use_global_device_ids=true, to_apply=%region_3.0 | all-reduce | flops 4 | bytes 32 | tf_op jit(solution)/shard_map/psum | solution.py:92
  272.1 1.1 fusion.143
  274.3 2.7 gather_fusion
  277.6 1.8 bitcast_select_fusion.2
  280.3 137.4 %all-reduce.4.cloned.1.call-done = f32[32,512]{0,1:T(8,128)} async-done(((f32[32,512]{0,1:T(8,128)}), f32[32,512]{0,1:T(8,128)}) %all-reduce.4.cloned.1.call-update) | async-done | bytes 65552 | tf_op jit(solution)/shard_map/psum | solution.py:112
  417.7 2.2 collective-permute-start.10
  419.9 11.8 %collective-permute-start.11 = (f32[32,512]{0,1:T(8,128)}, f32[32,512]{0,1:T(8,128)S(1)}, u32[]{:S(2)}, u32[]{:S(2)}) collective-permute-start(f32[32,512]{0,1:T(8,128)} %all-reduce.4.cloned.1.call-done), channel_id=1, source_target_pairs={{0,496},{8,504},{16,0},{24,8},{32,16},{40,24},{48,32},{56,40},{64,... | collective-permute-start | bytes 196616 | tf_op jit(solution)/shard_map/ppermute | solution.py:35
  431.7 1.9 collective-permute-start.8
  433.6 9.1 %collective-permute-start.9 = (f32[32,512]{0,1:T(8,128)}, f32[32,512]{0,1:T(8,128)S(1)}, u32[]{:S(2)}, u32[]{:S(2)}) collective-permute-start(f32[32,512]{0,1:T(8,128)} %all-reduce.4.cloned.1.call-done), channel_id=1, source_target_pairs={{0,504},{8,0},{16,8},{24,16},{32,24},{40,32},{48,40},{56,48},{64,5... | collective-permute-start | bytes 196616 | tf_op jit(solution)/shard_map/ppermute | solution.py:35
  442.8 1.6 fusion.151
  444.8 1.1 fusion.11
  446.7 2.0 fusion.130
  448.7 1.5 stack_reshape.36
  450.2 2.0 fusion.10
  452.2 2.0 fusion.129
  454.1 1.5 stack_reshape.37
  455.6 1.1 fusion.9
  456.7 2.0 fusion.128
  459.6 1.1 fusion.8
  460.7 1.4 fusion.127
  467.5 154.3 %all-reduce.6.cloned.1.call-done = f32[32,512]{0,1:T(8,128)} async-done(((f32[32,512]{0,1:T(8,128)}), f32[32,512]{0,1:T(8,128)}) %all-reduce.6.cloned.1.call-update) | async-done | bytes 65552 | tf_op jit(solution)/shard_map/psum | solution.py:112
  621.9 8.2 collective-permute-start.12
  630.1 1.9 collective-permute-start.13
  632.0 2.3 collective-permute-start.14
  634.3 11.9 %collective-permute-start.15 = (f32[32,512]{0,1:T(8,128)}, f32[32,512]{0,1:T(8,128)S(1)}, u32[]{:S(2)}, u32[]{:S(2)}) collective-permute-start(f32[32,512]{0,1:T(8,128)} %all-reduce.6.cloned.1.call-done), channel_id=1, source_target_pairs={{0,496},{8,504},{16,0},{24,8},{32,16},{40,24},{48,32},{56,40},{64,... | collective-permute-start | bytes 196616 | tf_op jit(solution)/shard_map/ppermute | solution.py:35
  646.3 2.1 collective-permute-done.14
  648.4 3.2 collective-permute-done.15
  652.0 1.1 fusion.7
  653.9 1.4 fusion.134
  655.3 1.1 fusion.6
  656.4 1.4 fusion.133
  657.8 1.1 fusion.5
  658.9 1.4 fusion.132
  660.3 1.1 fusion.4
  661.5 1.4 fusion.131
  666.0 151.7 %all-reduce.8.cloned.1.call-done = f32[32,512]{0,1:T(8,128)} async-done(((f32[32,512]{0,1:T(8,128)}), f32[32,512]{0,1:T(8,128)}) %all-reduce.8.cloned.1.call-update) | async-done | bytes 65552 | tf_op jit(solution)/shard_map/psum | solution.py:112
  817.7 8.2 collective-permute-start.16
  826.0 1.9 collective-permute-start.17
  827.9 2.3 collective-permute-start.18
  830.2 11.9 %collective-permute-start.19 = (f32[32,512]{0,1:T(8,128)}, f32[32,512]{0,1:T(8,128)S(1)}, u32[]{:S(2)}, u32[]{:S(2)}) collective-permute-start(f32[32,512]{0,1:T(8,128)} %all-reduce.8.cloned.1.call-done), channel_id=1, source_target_pairs={{0,496},{8,504},{16,0},{24,8},{32,16},{40,24},{48,32},{56,40},{64,... | collective-permute-start | bytes 196616 | tf_op jit(solution)/shard_map/ppermute | solution.py:35
  842.2 2.1 collective-permute-done.18
  844.3 3.2 collective-permute-done.19
  847.9 1.1 fusion.3
  849.1 1.4 fusion.138
  850.5 1.1 fusion.2
  851.6 1.4 fusion.137
  853.0 1.1 fusion.1
  854.2 1.4 fusion.136
  855.5 1.1 fusion
  856.7 1.4 fusion.135
  (163 shorter events, 27.3 us)
Async XLA Ops:
  6.5 12.6 %copy-start = (f32[32,2,2,4,128]{4,3,2,1,0:T(4,128)S(1)}, f32[32,2,2,4,128]{4,3,2,1,0:T(4,128)}, u32[]{:S(2)}) copy-start(f32[32,2,2,4,128]{4,3,2,1,0:T(4,128)} %param.12) | copy-start | bytes 786436
  6.5 411.1 %all-reduce.4.cloned.1.call-start = ((), (), s32[]{:S(2)}) async-start(), calls=%async_computation | async-start | bytes 524288 | tf_op jit(solution)/shard_map/psum | solution.py:112
  8.4 22.9 %collective-permute-start = (f32[32,2,2,1,128]{4,3,2,1,0:T(1,128)}, f32[32,2,2,1,128]{4,3,2,1,0:T(1,128)}, u32[]{:S(2)}, u32[]{:S(2)}) collective-permute-start(f32[32,2,2,1,128]{4,3,2,1,0:T(1,128)} %get-tuple-element.57), channel_id=1, source_target_pairs={{0,8},{8,16},{16,24},{24,32},{32,40},{40,48},{48,56},{56,64},{64,7... | collective-permute-start | bytes 196616 | tf_op jit(solution)/shard_map/ppermute | solution.py:24
  13.3 17.9 %collective-permute-start.1 = (f32[32,2,2,1,128]{4,3,2,1,0:T(1,128)}, f32[32,2,2,1,128]{4,3,2,1,0:T(1,128)}, u32[]{:S(2)}, u32[]{:S(2)}) collective-permute-start(f32[32,2,2,1,128]{4,3,2,1,0:T(1,128)} %get-tuple-element.58), channel_id=1, source_target_pairs={{8,0},{16,8},{24,16},{32,24},{40,32},{48,40},{56,48},{64,56},{72,6... | collective-permute-start | bytes 196616 | tf_op jit(solution)/shard_map/ppermute | solution.py:27
  19.1 0.7 copy-start.18
  22.9 3.2 copy-start.15
  25.5 0.7 copy-start.16
  26.2 0.7 copy-start.14
  26.9 0.7 copy-start.19
  29.9 0.7 copy-start.28
  32.3 11.5 %copy-start.4 = (f32[32,2,1,4,128]{4,3,2,1,0:T(4,128)S(1)}, f32[32,2,1,4,128]{4,3,2,1,0:T(4,128)}, u32[]{:S(2)}) copy-start(f32[32,2,1,4,128]{4,3,2,1,0:T(4,128)} %get-tuple-element.56) | copy-start | bytes 393220
  32.5 7.4 collective-permute-start.2
  33.9 9.9 %collective-permute-start.3 = (f32[32,2,2,6,1]{4,3,2,1,0:T(8,128)S(1)}, f32[32,2,2,6,1]{4,3,2,1,0:T(8,128)S(1)}, u32[]{:S(2)}, u32[]{:S(2)}) collective-permute-start(f32[32,2,2,6,1]{4,3,2,1,0:T(8,128)S(1)} %get-tuple-element.38), channel_id=1, source_target_pairs={{1,0},{2,1},{3,2},{4,3},{5,4},{6,5},{7,6},{9,8},{10,9},{11,10},{12... | collective-permute-start | bytes 9224 | tf_op jit(solution)/shard_map/ppermute | solution.py:27
  43.8 0.7 copy-start.20
  46.7 16.0 %collective-permute-start.4 = (f32[32,2,2,1,128]{4,3,2,1,0:T(1,128)S(1)}, f32[32,2,2,1,128]{4,3,2,1,0:T(1,128)S(1)}, u32[]{:S(2)}, u32[]{:S(2)}) collective-permute-start(f32[32,2,2,1,128]{4,3,2,1,0:T(1,128)S(1)} %get-tuple-element.51), channel_id=1, source_target_pairs={{0,8},{8,16},{16,24},{24,32},{32,40},{40,48},{48,56},{56,64},{64,7... | collective-permute-start | bytes 196616 | tf_op jit(solution)/shard_map/ppermute | solution.py:24
  54.5 8.5 collective-permute-start.5
  63.4 8.5 collective-permute-start.6
  65.9 18.5 %collective-permute-start.7 = (f32[32,2,2,6,1]{4,3,2,1,0:T(8,128)S(1)}, f32[32,2,2,6,1]{4,3,2,1,0:T(8,128)S(1)}, u32[]{:S(2)}, u32[]{:S(2)}) collective-permute-start(f32[32,2,2,6,1]{4,3,2,1,0:T(8,128)S(1)} %get-tuple-element.36), channel_id=1, source_target_pairs={{1,0},{2,1},{3,2},{4,3},{5,4},{6,5},{7,6},{9,8},{10,9},{11,10},{12... | collective-permute-start | bytes 9224 | tf_op jit(solution)/shard_map/ppermute | solution.py:27
  85.4 0.7 copy-start.3
  86.3 185.8 %copy-start.27 = (f32[2,2]{1,0:T(2,128)S(1)}, f32[2,2]{1,0:T(2,128)}, u32[]{:S(2)}) copy-start(f32[2,2]{1,0:T(2,128)} %param.14) | copy-start | bytes 52
  273.3 6.3 copy-start.1
  277.0 0.6 copy-start.23
  277.0 0.6 copy-start.24
  279.5 342.4 %all-reduce.6.cloned.1.call-start = ((), (), s32[]{:S(2)}) async-start(), calls=%async_computation.1 | async-start | bytes 524288 | tf_op jit(solution)/shard_map/psum | solution.py:112
  417.7 26.7 %collective-permute-start.10 = (f32[32,512]{0,1:T(8,128)}, f32[32,512]{0,1:T(8,128)S(1)}, u32[]{:S(2)}, u32[]{:S(2)}) collective-permute-start(f32[32,512]{0,1:T(8,128)} %all-reduce.4.cloned.1.call-done), channel_id=1, source_target_pairs={{0,16},{8,24},{16,32},{24,40},{32,48},{40,56},{48,64},{56,72},{64,... | collective-permute-start | bytes 196616 | tf_op jit(solution)/shard_map/ppermute | solution.py:35
  419.9 24.5 %collective-permute-start.11 = (f32[32,512]{0,1:T(8,128)}, f32[32,512]{0,1:T(8,128)S(1)}, u32[]{:S(2)}, u32[]{:S(2)}) collective-permute-start(f32[32,512]{0,1:T(8,128)} %all-reduce.4.cloned.1.call-done), channel_id=1, source_target_pairs={{0,496},{8,504},{16,0},{24,8},{32,16},{40,24},{48,32},{56,40},{64,... | collective-permute-start | bytes 196616 | tf_op jit(solution)/shard_map/ppermute | solution.py:35
  431.7 12.7 %collective-permute-start.8 = (f32[32,512]{0,1:T(8,128)}, f32[32,512]{0,1:T(8,128)S(1)}, u32[]{:S(2)}, u32[]{:S(2)}) collective-permute-start(f32[32,512]{0,1:T(8,128)} %all-reduce.4.cloned.1.call-done), channel_id=1, source_target_pairs={{0,8},{8,16},{16,24},{24,32},{32,40},{40,48},{48,56},{56,64},{64,7... | collective-permute-start | bytes 196616 | tf_op jit(solution)/shard_map/ppermute | solution.py:35
  433.6 10.8 %collective-permute-start.9 = (f32[32,512]{0,1:T(8,128)}, f32[32,512]{0,1:T(8,128)S(1)}, u32[]{:S(2)}, u32[]{:S(2)}) collective-permute-start(f32[32,512]{0,1:T(8,128)} %all-reduce.4.cloned.1.call-done), channel_id=1, source_target_pairs={{0,504},{8,0},{16,8},{24,16},{32,24},{40,32},{48,40},{56,48},{64,5... | collective-permute-start | bytes 196616 | tf_op jit(solution)/shard_map/ppermute | solution.py:35
  442.8 1.7 copy-start.5
  444.8 1.1 copy-start.13
  462.1 0.8 copy-start.8
  462.1 0.9 copy-start.9
  463.0 1.0 copy-start.2
  464.1 0.7 copy-start.10
  465.8 0.6 copy-start.22
  465.8 0.7 copy-start.26
  467.5 350.3 %all-reduce.8.cloned.1.call-start = ((), (), s32[]{:S(2)}) async-start(), calls=%async_computation.2 | async-start | bytes 524288 | tf_op jit(solution)/shard_map/psum | solution.py:112
  621.9 24.4 %collective-permute-start.12 = (f32[32,512]{0,1:T(8,128)}, f32[32,512]{0,1:T(8,128)S(1)}, u32[]{:S(2)}, u32[]{:S(2)}) collective-permute-start(f32[32,512]{0,1:T(8,128)} %all-reduce.6.cloned.1.call-done), channel_id=1, source_target_pairs={{0,8},{8,16},{16,24},{24,32},{32,40},{40,48},{48,56},{56,64},{64,7... | collective-permute-start | bytes 196616 | tf_op jit(solution)/shard_map/ppermute | solution.py:35
  630.1 16.2 %collective-permute-start.13 = (f32[32,512]{0,1:T(8,128)}, f32[32,512]{0,1:T(8,128)S(1)}, u32[]{:S(2)}, u32[]{:S(2)}) collective-permute-start(f32[32,512]{0,1:T(8,128)} %all-reduce.6.cloned.1.call-done), channel_id=1, source_target_pairs={{0,504},{8,0},{16,8},{24,16},{32,24},{40,32},{48,40},{56,48},{64,5... | collective-permute-start | bytes 196616 | tf_op jit(solution)/shard_map/ppermute | solution.py:35
  632.0 16.4 %collective-permute-start.14 = (f32[32,512]{0,1:T(8,128)}, f32[32,512]{0,1:T(8,128)S(1)}, u32[]{:S(2)}, u32[]{:S(2)}) collective-permute-start(f32[32,512]{0,1:T(8,128)} %all-reduce.6.cloned.1.call-done), channel_id=1, source_target_pairs={{0,16},{8,24},{16,32},{24,40},{32,48},{40,56},{48,64},{56,72},{64,... | collective-permute-start | bytes 196616 | tf_op jit(solution)/shard_map/ppermute | solution.py:35
  634.3 17.3 %collective-permute-start.15 = (f32[32,512]{0,1:T(8,128)}, f32[32,512]{0,1:T(8,128)S(1)}, u32[]{:S(2)}, u32[]{:S(2)}) collective-permute-start(f32[32,512]{0,1:T(8,128)} %all-reduce.6.cloned.1.call-done), channel_id=1, source_target_pairs={{0,496},{8,504},{16,0},{24,8},{32,16},{40,24},{48,32},{56,40},{64,... | collective-permute-start | bytes 196616 | tf_op jit(solution)/shard_map/ppermute | solution.py:35
  646.2 5.4 copy-start.6
  652.0 1.2 copy-start.12
  653.2 0.7 copy-start.17
  664.4 0.6 copy-start.21
  664.4 0.7 copy-start.25
  817.7 24.5 %collective-permute-start.16 = (f32[32,512]{0,1:T(8,128)}, f32[32,512]{0,1:T(8,128)S(1)}, u32[]{:S(2)}, u32[]{:S(2)}) collective-permute-start(f32[32,512]{0,1:T(8,128)} %all-reduce.8.cloned.1.call-done), channel_id=1, source_target_pairs={{0,8},{8,16},{16,24},{24,32},{32,40},{40,48},{48,56},{56,64},{64,7... | collective-permute-start | bytes 196616 | tf_op jit(solution)/shard_map/ppermute | solution.py:35
  826.0 16.2 %collective-permute-start.17 = (f32[32,512]{0,1:T(8,128)}, f32[32,512]{0,1:T(8,128)S(1)}, u32[]{:S(2)}, u32[]{:S(2)}) collective-permute-start(f32[32,512]{0,1:T(8,128)} %all-reduce.8.cloned.1.call-done), channel_id=1, source_target_pairs={{0,504},{8,0},{16,8},{24,16},{32,24},{40,32},{48,40},{56,48},{64,5... | collective-permute-start | bytes 196616 | tf_op jit(solution)/shard_map/ppermute | solution.py:35
  827.9 16.4 %collective-permute-start.18 = (f32[32,512]{0,1:T(8,128)}, f32[32,512]{0,1:T(8,128)S(1)}, u32[]{:S(2)}, u32[]{:S(2)}) collective-permute-start(f32[32,512]{0,1:T(8,128)} %all-reduce.8.cloned.1.call-done), channel_id=1, source_target_pairs={{0,16},{8,24},{16,32},{24,40},{32,48},{40,56},{48,64},{56,72},{64,... | collective-permute-start | bytes 196616 | tf_op jit(solution)/shard_map/ppermute | solution.py:35
  830.2 17.3 %collective-permute-start.19 = (f32[32,512]{0,1:T(8,128)}, f32[32,512]{0,1:T(8,128)S(1)}, u32[]{:S(2)}, u32[]{:S(2)}) collective-permute-start(f32[32,512]{0,1:T(8,128)} %all-reduce.8.cloned.1.call-done), channel_id=1, source_target_pairs={{0,496},{8,504},{16,0},{24,8},{32,16},{40,24},{48,32},{56,40},{64,... | collective-permute-start | bytes 196616 | tf_op jit(solution)/shard_map/ppermute | solution.py:35
  842.1 5.4 copy-start.7
  847.9 1.1 copy-start.11
Sparse Core Ops, SparseCore 0:
  279.6 138.0 all-reduce.3
  467.6 154.2 all-reduce.5
  666.1 151.5 all-reduce.7
where the time goes:
time: 878 us; the launch traced here: 866 us
  waiting for transfers between devices  480 us (55%)
  blocking collectives  186 us (21%)
  starting transfers between devices  106 us (12%)
  matrix products  32.5 us (4%)
  local copies, waits for them, and re-layouts  23.4 us (3%)
  between operations  20 us (2%)
  other arithmetic  17.6 us (2%)
    psum x3, waiting for transfers between devices, local(): column = lax.psum(contrib, 'gy')  443 us
    psum x1, blocking collectives, local(): totals = lax.psum(local_var, ('gx', 'gy'))  186 us
    ppermute x12, starting transfers between devices, from_behind(): return lax.ppermute(value, axis, pairs)  73.7 us
    dot_general x12, matrix products, local(): lax.dot_general(drive, covariance * weight, (((1,), (1,)), ((), ())), pre...  18.2 us
  transfers between devices with their start and end apart: 23, of which 12 were waited for; matrix products, arithmetic and copies ran while one was open for 1% of the time, Pallas kernels for 0%

commit v1 on v0

v1 whole, which is shorter than its diff:
```python
import jax
import jax.numpy as jnp
from jax import lax
from jax.experimental import pallas as pl
from jax.experimental.pallas import tpu as pltpu
from jax.sharding import PartitionSpec as P

MEMBERS = 32
GROUPS = 4
CX = 4
CY = 128
CELLS = CX * CY
OBS = 512
BATCHES = 3
STEPS = 2
TILES_X = 64
TILES_Y = 8
TILES = TILES_X * TILES_Y
NX = TILES_X * CX
NY = TILES_Y * CY
LOC_X = 12.0
LOC_Y = 512.0
REACH = 2
SPAN = 2 * REACH + 1
WINDOW = SPAN * TILES_Y
CHUNK = 256
AHEAD = GROUPS * CELLS

diffuse_rate = 0.1
mixing_rate = 0.05
spread_floor = 1e-05

F32 = jnp.float32
BF16 = jnp.bfloat16
I32 = jnp.int32

VMEM = pl.BlockSpec(memory_space=pltpu.VMEM)
SMEM = pl.BlockSpec(memory_space=pltpu.SMEM)


def rows_of(group, x):
    return pl.ds(group * CX + x, MEMBERS, stride=GROUPS * CX)


def mm(a, b):
    return lax.dot_general(a, b, (((1,), (0,)), ((), ())), preferred_element_type=F32)


def halves(value):
    high = value.astype(BF16)
    return high, (value - high.astype(F32)).astype(BF16)


def thirds(value):
    high = value.astype(BF16)
    rest = value - high.astype(F32)
    middle = rest.astype(BF16)
    return high, middle, (rest - middle.astype(F32)).astype(BF16)


def edges_kernel(ens_ref, low_ref, high_ref):
    turned = ens_ref[...].T
    low_ref[...] = turned[0:2]
    high_ref[...] = turned[CY - 2 : CY]


def advance(rows, courant_ref, keep):
    lowest = min(x for _, x in rows) - 1
    highest = max(x for _, x in rows) + 1
    width = 2 * CY
    after = {}
    for group in range(GROUPS):
        speed = courant_ref[group % 2]
        stay = 1.0 - speed - 4.0 * diffuse_rate - mixing_rate
        for x in range(lowest, highest + 1):
            terms = []
            if (group, x) in rows:
                here = rows[group, x]
                beside = pltpu.roll(here, 1, 1) + pltpu.roll(here, width - 1, 1)
                terms.append(stay * here + diffuse_rate * beside + mixing_rate * rows[group ^ 1, x])
            if (group, x - 1) in rows:
                terms.append((speed + diffuse_rate) * rows[group, x - 1])
            if (group, x + 1) in rows:
                terms.append(diffuse_rate * rows[group, x + 1])
            total = terms[0]
            for term in terms[1:]:
                total = total + term
            after[group, x] = total if keep is None else total * keep
    return after


def spread_kernel(
    order_ref,
    place_ref,
    courant_ref,
    ens_ref,
    before_ref,
    behind_ref,
    owner_ref,
    cell_ref,
    kind_ref,
    mask_ref,
    own_ref,
    left_ref,
    right_ref,
    send_ref,
    outer_ref,
):
    place_x = place_ref[0]
    place_y = place_ref[1]
    rim = jnp.concatenate(
        [behind_ref[...], jnp.zeros((CY - 4, OBS), F32), before_ref[...]], axis=0
    )
    outer_ref[...] = rim.T
    rows = {}
    for group in range(GROUPS):
        for x in range(CX):
            rows[group, x] = jnp.concatenate(
                [ens_ref[rows_of(group, x), :], outer_ref[rows_of(group, x), :]], axis=1
            )
    lane = lax.broadcasted_iota(I32, (1, 2 * CY), 1)
    below = (lane >= 3 * CY // 2) & (place_y == 0)
    above = (lane >= CY) & (lane < 3 * CY // 2) & (place_y == TILES_Y - 1)
    keep = jnp.where(below | above, 0.0, 1.0).astype(F32)
    rows = advance(rows, courant_ref, keep)
    rows = advance(rows, courant_ref, None)
    tile = {at: value[:, :CY] for at, value in rows.items()}
    for group in range(GROUPS):
        for x in range(CX):
            own_ref[group, :, x * CY : (x + 1) * CY] = tile[group, x]
        for x in range(2):
            left_ref[group, :, x * CY : (x + 1) * CY] = tile[group, x - 2]
            right_ref[group, :, x * CY : (x + 1) * CY] = tile[group, x + CX]
    ground = jnp.concatenate(
        [
            jnp.concatenate([tile[2 * field, x] for x in range(-2, CX + 2)], axis=1)
            for field in range(2)
        ],
        axis=0,
    )
    parts = jnp.concatenate(thirds(ground), axis=0)
    blocks = []
    masks = []
    for turn in range(BATCHES):
        batch = order_ref[turn]
        owner = owner_ref[pl.ds(batch, 1), :]
        cell = cell_ref[pl.ds(batch, 1), :]
        kind = kind_ref[pl.ds(batch, 1), :]
        masks.append(mask_ref[pl.ds(batch, 1), :].astype(F32))
        at_x = ((owner >> 3) - place_x) * CX + (cell >> 7) + 2
        at_x = at_x & (NX - 1)
        seen = (at_x < CX + 4) & ((owner & (TILES_Y - 1)) == place_y)
        index = jnp.where(seen, at_x * CY + (cell & (CY - 1)), -1)
        picked = jnp.zeros((parts.shape[0], OBS), F32)
        for start in range(0, (CX + 4) * CY, CHUNK):
            spot = lax.broadcasted_iota(I32, (CHUNK, OBS), 0) + start
            hot = jnp.where(spot == index, 1.0, 0.0).astype(BF16)
            picked = picked + mm(parts[:, start : start + CHUNK], hot)
        picked = picked[0:64] + picked[64:128] + picked[128:192]
        blocks.append(jnp.where(kind == 0, picked[0:32], picked[32:64]))
    sub = lax.broadcasted_iota(I32, (MEMBERS, OBS), 0)
    blocks.append(jnp.where(sub == 0, masks[0], jnp.where(sub == 1, masks[1], 0.0)))
    send_ref[...] = jnp.concatenate(blocks, axis=0).T


def merge_kernel(
    order_ref,
    place_ref,
    relay_ref,
    own_ref,
    from_left_ref,
    from_right_ref,
    recv_ref,
    forecast_ref,
    send_ref,
):
    place = place_ref[0] * TILES_Y + place_ref[1]
    lane = lax.broadcasted_iota(I32, (1, CY), 1)
    top = jnp.sum(recv_ref[...], axis=0, keepdims=True)
    top = jnp.where(lane < BATCHES * MEMBERS, top, 0.0)
    for group in range(GROUPS):
        own = own_ref[group]
        value = jnp.concatenate(
            [
                own[:, : 2 * CY] + from_left_ref[group],
                own[:, 2 * CY :] + from_right_ref[group],
            ],
            axis=1,
        )
        forecast_ref[group] = value
        centre = jnp.sum(value, axis=0, keepdims=True) * (1.0 / MEMBERS)
        deviation = value - centre
        total = jnp.sum(jnp.sum(deviation * deviation, axis=0, keepdims=True), axis=1, keepdims=True)
        top = jnp.where(lane == BATCHES * MEMBERS + group, total, top)
    pieces = []
    for turn in range(2):
        column = relay_ref[order_ref[turn], place] >> 3
        for step in range(SPAN):
            at = (column + (step - REACH)) & (TILES_X - 1)
            start = pl.multiple_of(at * TILES_Y, TILES_Y)
            pieces.append(recv_ref[pl.ds(start, TILES_Y), :])
    pieces.append(jnp.zeros((CY - 2 * WINDOW, CY), F32))
    turned = jnp.concatenate(pieces, axis=0).T
    first = turned[BATCHES * MEMBERS : BATCHES * MEMBERS + 1]
    second = turned[BATCHES * MEMBERS + 1 : BATCHES * MEMBERS + 2]
    bottom = jnp.where(lane < WINDOW, first, jnp.where(lane < 2 * WINDOW, second, 0.0))
    pair = jnp.concatenate([top, bottom] * 4, axis=0)
    send_ref[...] = jnp.concatenate([pair] * (2 * TILES // 8), axis=0)


def assimilate_kernel(
    order_ref,
    place_ref,
    spread_ref,
    error_ref,
    forecast_ref,
    recv_ref,
    owner_ref,
    cell_ref,
    kind_ref,
    value_ref,
    mask_ref,
    out_ref,
    state_ref,
    pack_ref,
    left_ref,
    drive_ref,
    table_ref,
    spots_ref,
    weight_ref,
):
    place_x = place_ref[0]
    place_y = place_ref[1]
    upper = recv_ref[pl.ds(0, TILES, stride=2), :].T
    stretch = []
    for group in range(GROUPS):
        row = BATCHES * MEMBERS + group
        total = jnp.sum(upper[row : row + 1], axis=1, keepdims=True)
        mean_var = total * (1.0 / ((MEMBERS - 1) * float(NX * NY)))
        stretch.append(jnp.sqrt(spread_ref[group // 2, group % 2] / (mean_var + spread_floor)))
    for group in range(GROUPS):
        value = forecast_ref[group]
        centre = jnp.sum(value, axis=0, keepdims=True) * (1.0 / MEMBERS)
        state_ref[:, group * CELLS : (group + 1) * CELLS] = centre + stretch[group] * (value - centre)

    kinds, xs, ys, values = [], [], [], []
    sub = lax.broadcasted_iota(I32, (CY, OBS), 0)
    table_ref[...] = jnp.zeros_like(table_ref)
    table = jnp.zeros((CY, OBS), F32)
    near = 4 * REACH + 1
    for turn in range(BATCHES):
        batch = order_ref[turn]
        owner = owner_ref[pl.ds(batch, 1), :]
        cell = cell_ref[pl.ds(batch, 1), :]
        kinds.append(kind_ref[pl.ds(batch, 1), :])
        values.append(value_ref[pl.ds(batch, 1), :])
        mask = mask_ref[pl.ds(batch, 1), :].astype(F32)
        xs.append(((owner >> 3) * CX + (cell >> 7)).astype(F32))
        ys.append(((owner & (TILES_Y - 1)) * CY + (cell & (CY - 1))).astype(F32))
        offset = ((owner >> 3) - place_x + REACH) & (TILES_X - 1)
        offset = jnp.where(offset >= TILES_X // 2, offset - TILES_X, offset).astype(F32)
        for row, value in enumerate((xs[turn], ys[turn], mask, offset)):
            table = jnp.where(sub == turn * 4 + row, value, table)
        prior = upper[turn * MEMBERS : (turn + 1) * MEMBERS]
        centre = jnp.sum(prior, axis=0, keepdims=True) * (1.0 / MEMBERS)
        factor = jnp.where(kinds[turn] == 0, stretch[0], stretch[2])
        state_ref[:, AHEAD + turn * OBS : AHEAD + (turn + 1) * OBS] = centre + factor * (prior - centre)
        at = ((owner >> 3) - place_x + 2 * REACH) & (TILES_X - 1)
        index = jnp.where(at < near, at * TILES_Y + (owner & (TILES_Y - 1)), -1)
        spots_ref[:, turn * OBS : (turn + 1) * OBS] = jnp.where(sub == index, 1.0, 0.0).astype(BF16)
    table_ref[...] = table.T

    lane = lax.broadcasted_iota(I32, (1, CY), 1)
    cell_x = (place_x * CX).astype(F32)
    cell_y = (place_y * CY + lane).astype(F32)

    for turn in range(BATCHES):
        prior = state_ref[:, AHEAD + turn * OBS : AHEAD + (turn + 1) * OBS]
        error = jnp.where(kinds[turn] == 0, error_ref[0], error_ref[1])
        centre = jnp.sum(prior, axis=0, keepdims=True) * (1.0 / MEMBERS)
        deviation = prior - centre
        variance = jnp.sum(deviation * deviation, axis=0, keepdims=True) / (MEMBERS - 1)
        gain = (values[turn] - centre) / (variance + error)
        shrink = -1.0 / (jnp.sqrt(error * (error + variance)) + error + variance)
        drive_high, drive_low = halves(gain + shrink * deviation)
        drive_ref[:MEMBERS] = drive_high
        drive_ref[MEMBERS:] = drive_low
        scaled = deviation * (1.0 / (MEMBERS - 1))
        scaled_high = scaled.astype(BF16).astype(F32)
        scaled_low = scaled - scaled_high
        packed = jnp.concatenate(
            [scaled_high, scaled_high, scaled_low, jnp.zeros_like(scaled)], axis=0
        )
        left_ref[...] = packed.T.astype(BF16)

        later = list(range(turn + 1, BATCHES))
        blocks = [slice(group * CELLS, (group + 1) * CELLS) for group in range(GROUPS)]
        blocks += [slice(AHEAD + other * OBS, AHEAD + (other + 1) * OBS) for other in later]
        for cols in blocks:
            state = state_ref[:, cols]
            state_dev = state - jnp.sum(state, axis=0, keepdims=True) * (1.0 / MEMBERS)
            high, low = halves(state_dev)
            pack_ref[0:32, cols] = high
            pack_ref[32:64, cols] = low
            pack_ref[64:96, cols] = high
            pack_ref[96:128, cols] = jnp.zeros_like(high)

        @pl.loop(0, OBS // CHUNK)
        def _(step):
            start = pl.multiple_of(step * CHUNK, CHUNK)
            part = pl.ds(start, CHUNK)
            table = table_ref[part, :]
            x_col = table[:, turn * 4 : turn * 4 + 1]
            y_col = table[:, turn * 4 + 1 : turn * 4 + 2]
            mask_col = table[:, turn * 4 + 2 : turn * 4 + 3]
            gap_y = y_col - cell_y
            drop_y = gap_y * gap_y * (1.0 / (LOC_Y * LOC_Y))
            for x in range(CX):
                gap_x = jnp.abs(x_col - (cell_x + x))
                gap_x = jnp.minimum(gap_x, NX - gap_x)
                room = jnp.maximum((1.0 - gap_x * gap_x * (1.0 / (LOC_X * LOC_X))) - drop_y, 0.0)
                weight_ref[:, x * CY : (x + 1) * CY] = room * room * mask_col
            if later:
                offset = table[:, turn * 4 + 3 : turn * 4 + 4]
                seen = recv_ref[pl.ds(2 * start + 1, CHUNK, stride=2), :]
                if turn == 1:
                    seen = pltpu.roll(seen, CY - WINDOW, 1)
                seen = jnp.where(lane < WINDOW, seen, 0.0)
                reach = jnp.zeros_like(seen)
                for hop in range(-(SPAN - 1), near):
                    moved = pltpu.roll(seen, (hop * TILES_Y) % CY, 1) if hop else seen
                    reach = jnp.where(offset == float(hop), moved, reach)
                reach = reach.astype(BF16)
                for place, other in enumerate(later):
                    allowed = mm(reach, spots_ref[:, other * OBS : (other + 1) * OBS])
                    gap_x = jnp.abs(x_col - xs[other])
                    gap_x = jnp.minimum(gap_x, NX - gap_x)
                    gap_y = y_col - ys[other]
                    room = 1.0 - gap_x * gap_x * (1.0 / (LOC_X * LOC_X))
                    room = jnp.maximum(room - gap_y * gap_y * (1.0 / (LOC_Y * LOC_Y)), 0.0)
                    weight_ref[:, (place + 1) * OBS : (place + 2) * OBS] = room * room * allowed

            left = left_ref[part, :]
            drive = drive_ref[:, part]
            for number, cols in enumerate(blocks):
                at = max(0, number - GROUPS + 1) * OBS
                covariance = mm(left, pack_ref[:, cols]) * weight_ref[:, at : at + OBS]
                high, low = halves(covariance)
                both = mm(drive, high)
                rest = mm(drive[:MEMBERS], low)
                state_ref[:, cols] += both[:MEMBERS] + both[MEMBERS:] + rest

    for group in range(GROUPS):
        for x in range(CX):
            at = group * CELLS + x * CY
            out_ref[rows_of(group, x), :] = state_ref[:, at : at + CY]


def call(kernel, specs, outs, scratch=()):
    return pl.pallas_call(
        kernel,
        in_specs=specs,
        out_specs=[VMEM] * len(outs) if len(outs) > 1 else VMEM,
        out_shape=outs if len(outs) > 1 else outs[0],
        scratch_shapes=list(scratch),
        compiler_params=pltpu.CompilerParams(vmem_limit_bytes=48 * 1024 * 1024),
    )


def shape(*dims):
    return jax.ShapeDtypeStruct(dims, F32)


def shifted(value, axis, step, periodic):
    count = lax.axis_size(axis)
    pairs = [
        (source, (source + step) % count)
        for source in range(count)
        if periodic or 0 <= source + step < count
    ]
    return lax.ppermute(value, axis, pairs)


def local(
    ensemble,
    courant,
    target_spread,
    obs_error,
    obs_value,
    obs_owner,
    obs_cell,
    obs_kind,
    tile_mask,
    batch_order,
):
    place = jnp.stack([lax.axis_index("gx"), lax.axis_index("gy")]).astype(I32)
    ens = ensemble.reshape(MEMBERS * GROUPS * CX, CY)
    mask = tile_mask.reshape(BATCHES, OBS)
    low, high = call(edges_kernel, [VMEM], [shape(2, OBS)] * 2)(ens)
    before = shifted(high, "gy", 1, False)
    behind = shifted(low, "gy", -1, False)
    own, left, right, send = call(
        spread_kernel,
        [SMEM] * 3 + [VMEM] * 7,
        [
            shape(GROUPS, MEMBERS, CELLS),
            shape(GROUPS, MEMBERS, 2 * CY),
            shape(GROUPS, MEMBERS, 2 * CY),
            shape(OBS, CY),
        ],
        [pltpu.VMEM((MEMBERS * GROUPS * CX, CY), F32)],
    )(
        batch_order,
        place,
        courant,
        ens,
        before,
        behind,
        obs_owner,
        obs_cell,
        obs_kind,
        mask,
    )
    from_left = shifted(right, "gx", 1, True)
    from_right = shifted(left, "gx", -1, True)
    recv = lax.all_to_all(send.reshape(TILES, 1, CY), ("gx", "gy"), 0, 0)
    forecast, send = call(
        merge_kernel,
        [SMEM] * 3 + [VMEM] * 4,
        [shape(GROUPS, MEMBERS, CELLS), shape(2 * TILES, CY)],
    )(batch_order, place, obs_owner, own, from_left, from_right, recv.reshape(TILES, CY))
    recv = lax.all_to_all(send.reshape(TILES, 2, CY), ("gx", "gy"), 0, 0)
    out = call(
        assimilate_kernel,
        [SMEM] * 4 + [VMEM] * 7,
        [shape(MEMBERS * GROUPS * CX, CY)],
        [
            pltpu.VMEM((MEMBERS, AHEAD + BATCHES * OBS), F32),
            pltpu.VMEM((CY, AHEAD + BATCHES * OBS), BF16),
            pltpu.VMEM((OBS, CY), BF16),
            pltpu.VMEM((2 * MEMBERS, OBS), BF16),
            pltpu.VMEM((OBS, CY), F32),
            pltpu.VMEM((CY, BATCHES * OBS), BF16),
            pltpu.VMEM((CHUNK, BATCHES * OBS), F32),
        ],
    )(
        batch_order,
        place,
        target_spread,
        obs_error,
        forecast,
        recv.reshape(2 * TILES, CY),
        obs_owner,
        obs_cell,
        obs_kind,
        obs_value,
        mask,
    )
    return out.reshape(ensemble.shape)


def solution(mesh):
    in_specs = (
        P(None, None, None, "gx", "gy"),
        P(),
        P(),
        P(),
        P(),
        P(),
        P(),
        P(),
        P(None, "gx", "gy", None),
        P(),
    )
    out_specs = P(None, None, None, "gx", "gy")
    return jax.shard_map(local, mesh=mesh, in_specs=in_specs, out_specs=out_specs, check_vma=False)
```

time: 878 us -> 142 us (0.16); the launches traced: 866 us -> 141 us
  waiting for transfers between devices: 480 us -> 19.1 us
  blocking collectives: 186 us -> 49.6 us
  starting transfers between devices: 106 us -> 50.8 us
  matrix products: 32.5 us -> 0 us
  local copies, waits for them, and re-layouts: 23.4 us -> 2.25 us
  between operations: 20 us -> 0.14 us
  Pallas kernels: 0 us -> 19.2 us
  other arithmetic: 17.6 us -> 0.08 us
    psum x3 -> x0, waiting for transfers between devices: 443 us -> none  [local(): column = lax.psum(contrib, 'gy')]
    psum x1 -> x0, blocking collectives: 186 us -> none  [local(): totals = lax.psum(local_var, ('gx', 'gy'))]
    ppermute x20 -> x4, starting transfers between devices: 106 us -> 13.5 us  [shifted(): return lax.ppermute(value, axis, pairs)]
    all_to_all x0 -> x1, blocking collectives: none -> 49.6 us  [local(): recv = lax.all_to_all(send.reshape(TILES, 2, CY), ('gx', 'gy'), 0, 0)]
    all_to_all x0 -> x1, starting transfers between devices: none -> 37.4 us  [local(): recv = lax.all_to_all(send.reshape(TILES, 1, CY), ('gx', 'gy'), 0, 0)]
    dot_general x24 -> x0, matrix products: 32.5 us -> none  [the longest x12 18.2 us: local(): lax.dot_general(drive, covariance * weight, (((1,), (1,)), ((), ())), pre...]
    ppermute x20 -> x4, waiting for transfers between devices: 36.6 us -> 6.2 us  [shifted(): return lax.ppermute(value, axis, pairs)]
    pallas_call x0 -> x4, Pallas kernels: none -> 19.2 us  [the longest x1 15.4 us: local(): call(assimilate_kernel, [SMEM] * 4 + [VMEM] * 7, [shape(MEMBERS * GROUPS...]
  transfers between devices with their start and end apart: 23 -> 5, of which waited for: 12 -> 3; matrix products, arithmetic and copies ran while one was open for 1% -> 0% of each run, Pallas kernels for 0% -> 0%
where the time goes in v1:
time: 142 us; the launch traced here: 141 us
  starting transfers between devices  50.8 us (36%)
  blocking collectives  49.6 us (35%)
  Pallas kernels  19.2 us (14%)
  waiting for transfers between devices  19.1 us (13%)
  local copies, waits for them, and re-layouts  2.25 us (2%)
    all_to_all x1, blocking collectives, local(): recv = lax.all_to_all(send.reshape(TILES, 2, CY), ('gx', 'gy'), 0, 0)  49.6 us
    all_to_all x1, starting transfers between devices, local(): recv = lax.all_to_all(send.reshape(TILES, 1, CY), ('gx', 'gy'), 0, 0)  37.4 us
    pallas_call x1, Pallas kernels, local(): call(assimilate_kernel, [SMEM] * 4 + [VMEM] * 7, [shape(MEMBERS * GROUPS...  15.4 us
    ppermute x4, starting transfers between devices, shifted(): return lax.ppermute(value, axis, pairs)  13.5 us
    all_to_all x1, waiting for transfers between devices, local(): recv = lax.all_to_all(send.reshape(TILES, 1, CY), ('gx', 'gy'), 0, 0)  12.9 us
    ppermute x4, waiting for transfers between devices, shifted(): return lax.ppermute(value, axis, pairs)  6.2 us
  transfers between devices with their start and end apart: 5, of which 3 were waited for; matrix products, arithmetic and copies ran while one was open for 0% of the time, Pallas kernels for 0%

profile of v1, /device:TPU:1, one launch (start us, length us, event | category | flops | bytes accessed | tf_op | source)
XLA Modules:
  0.0 141.2 jit_solution(12792012176887551723)
XLA Ops:
  0.0 0.0 copy-start
  0.0 0.9 copy-done
  1.0 0.0 copy-start.1
  1.0 0.1 shard_map.100
  1.1 4.0 %collective-permute-start = (f32[2,512]{1,0:T(2,128)S(1)}, f32[2,512]{1,0:T(2,128)S(1)}, u32[]{:S(2)}, u32[]{:S(2)}) collective-permute-start(f32[2,512]{1,0:T(2,128)S(1)} %get-tuple-element.13), channel_id=1, source_target_pairs={{0,1},{1,2},{2,3},{3,4},{4,5},{5,6},{6,7},{8,9},{9,10},{10,11},{11... | collective-permute-start | bytes 12296 | tf_op jit(solution)/shard_map/ppermute | solution.py:381
  5.1 1.3 collective-permute-start.1
  6.4 0.0 copy-start.10
  6.4 0.0 copy-start.4
  6.4 0.0 copy-start.3
  6.5 0.1 pad_add_fusion.place_ref
  6.5 0.6 copy-done.10
  7.1 0.0 copy-start.2
  7.1 0.0 copy-start.6
  7.1 0.0 copy-start.8
  7.1 0.0 collective-permute-done.before_ref
  7.1 2.3 %collective-permute-done.1.behind_ref = f32[2,512]{1,0:T(2,128)S(1)} collective-permute-done((f32[2,512]{1,0:T(2,128)S(1)}, f32[2,512]{1,0:T(2,128)S(1)}, u32[]{:S(2)}, u32[]{:S(2)}) %collective-permute-start.1) | collective-permute-done | bytes 4128 | tf_op jit(solution)/shard_map/ppermute | solution.py:381
  9.5 0.0 copy-done.1
  9.5 0.0 copy-done.4
  9.5 0.0 copy-done.3
  9.5 0.0 copy-done.2
  9.5 0.0 copy-done.6
  9.5 0.0 copy-done.8
  9.5 2.8 %shard_map.101 = (f32[4,32,512]{2,1,0:T(8,128)S(1)}, f32[4,32,256]{2,1,0:T(8,128)S(1)}, f32[4,32,256]{2,1,0:T(8,128)S(1)}, f32[512,128]{1,0:T(8,128)}) custom-call(s32[3]{0:T(128)S(1)} %copy-done.6, s32[2]{0:T(128)S(1)} %pad_add_fusion.place_ref, f32[2]{0:T(128)S(1)} %copy-done.8, f32[512,128]{1,0:T(8,128)S(1)} %bitcast.15, ...), custom_call_target="tpu_custom_call" | custom-call | tf_op jit(solution)/shard_map/pallas_call | solution.py:402
  12.3 37.4 %all-to-all-start = ((f32[512,1,128]{2,1,0:T(1,128)}), f32[512,1,128]{2,1,0:T(1,128)S(1)}, u32[]{:S(2)}, u32[]{:S(2)}) async-start(f32[512,1,128]{2,1,0:T(1,128)} %bitcast.4), calls=%async_computation | async-start | bytes 524288 | tf_op jit(solution)/shard_map/all_to_all | solution.py:426
  49.7 3.7 %collective-permute-start.2 = (f32[4,32,256]{2,1,0:T(8,128)S(1)}, f32[4,32,256]{2,1,0:T(8,128)S(1)}, u32[]{:S(2)}, u32[]{:S(2)}) collective-permute-start(f32[4,32,256]{2,1,0:T(8,128)S(1)} %get-tuple-element.16), channel_id=1, source_target_pairs={{0,8},{8,16},{16,24},{24,32},{32,40},{40,48},{48,56},{56,64},{64,7... | collective-permute-start | bytes 393224 | tf_op jit(solution)/shard_map/ppermute | solution.py:381
  53.3 4.5 %collective-permute-start.3 = (f32[4,32,256]{2,1,0:T(8,128)S(1)}, f32[4,32,256]{2,1,0:T(8,128)S(1)}, u32[]{:S(2)}, u32[]{:S(2)}) collective-permute-start(f32[4,32,256]{2,1,0:T(8,128)S(1)} %get-tuple-element.17), channel_id=1, source_target_pairs={{0,504},{8,0},{16,8},{24,16},{32,24},{40,32},{48,40},{56,48},{64,5... | collective-permute-start | bytes 393224 | tf_op jit(solution)/shard_map/ppermute | solution.py:381
  57.8 3.9 %collective-permute-done.2.from_left_ref = f32[4,32,256]{2,1,0:T(8,128)S(1)} collective-permute-done((f32[4,32,256]{2,1,0:T(8,128)S(1)}, f32[4,32,256]{2,1,0:T(8,128)S(1)}, u32[]{:S(2)}, u32[]{:S(2)}) %collective-permute-start.2) | collective-permute-done | bytes 131104 | tf_op jit(solution)/shard_map/ppermute | solution.py:381
  61.7 0.0 collective-permute-done.3.from_right_ref
  61.7 12.9 %all-to-all-done = f32[512,1,128]{2,1,0:T(1,128)S(1)} async-done(((f32[512,1,128]{2,1,0:T(1,128)}), f32[512,1,128]{2,1,0:T(1,128)S(1)}, u32[]{:S(2)}, u32[]{:S(2)}) %all-to-all-start) | async-done | bytes 262176 | tf_op jit(solution)/shard_map/all_to_all | solution.py:426
  74.6 0.9 shard_map.102
  75.5 0.0 copy-start.5
  75.5 49.6 %all_to_all.10 = f32[512,2,128]{2,1,0:T(2,128)S(1)} all-to-all(f32[512,2,128]{2,1,0:T(2,128)S(1)} %bitcast.17), channel_id=1, replica_groups=mesh['gx'=64,'gy'=8] {'gx','gy'}, dimensions={0} | all-to-all | bytes 1048576 | tf_op jit(solution)/shard_map/all_to_all | solution.py:432
  125.1 0.0 copy-start.7
  125.1 0.0 copy-start.9
  125.1 0.0 copy-done.5
  125.1 0.7 copy-done.7
  125.8 0.0 copy-done.9
  125.8 15.4 %shard_map.103 = f32[512,128]{1,0:T(8,128)} custom-call(s32[3]{0:T(128)S(1)} %copy-done.6, s32[2]{0:T(128)S(1)} %pad_add_fusion.place_ref, f32[2,2]{1,0:T(2,128)S(1)} %copy-done.7, f32[2]{0:T(128)S(1)} %copy-done.9, f32[4,32,512]{2,1,0:T(8,128)S(1)} %get-tuple-element.19.forecast_ref, f32[1024,128]{1,0:T(8,128)S(1)} %bitcast.13, s32[3,512]{1,0:T(4,128)S(1)} %copy-done.2, ...), custom_call_target="tpu_custom_call" | custom-call | tf_op jit(solution)/shard_map/pallas_call | solution.py:433
  (1 shorter events, 0.0 us)
Async XLA Ops:
  0.0 0.9 copy-start
  1.0 8.5 %copy-start.1 = (f32[32,2,2,4,128]{4,3,2,1,0:T(4,128)S(1)}, f32[32,2,2,4,128]{4,3,2,1,0:T(4,128)}, u32[]{:S(2)}) copy-start(f32[32,2,2,4,128]{4,3,2,1,0:T(4,128)} %param.10) | copy-start | bytes 786436
  1.1 6.1 %collective-permute-start = (f32[2,512]{1,0:T(2,128)S(1)}, f32[2,512]{1,0:T(2,128)S(1)}, u32[]{:S(2)}, u32[]{:S(2)}) collective-permute-start(f32[2,512]{1,0:T(2,128)S(1)} %get-tuple-element.13), channel_id=1, source_target_pairs={{0,1},{1,2},{2,3},{3,4},{4,5},{5,6},{6,7},{8,9},{9,10},{10,11},{11... | collective-permute-start | bytes 12296 | tf_op jit(solution)/shard_map/ppermute | solution.py:381
  5.1 4.4 %collective-permute-start.1 = (f32[2,512]{1,0:T(2,128)S(1)}, f32[2,512]{1,0:T(2,128)S(1)}, u32[]{:S(2)}, u32[]{:S(2)}) collective-permute-start(f32[2,512]{1,0:T(2,128)S(1)} %get-tuple-element.14), channel_id=1, source_target_pairs={{1,0},{2,1},{3,2},{4,3},{5,4},{6,5},{7,6},{9,8},{10,9},{11,10},{12... | collective-permute-start | bytes 12296 | tf_op jit(solution)/shard_map/ppermute | solution.py:381
  6.4 0.7 copy-start.10
  6.4 3.0 %copy-start.4 = (s32[3,512]{1,0:T(4,128)S(1)}, s32[3,512]{1,0:T(4,128)}, u32[]{:S(2)}) copy-start(s32[3,512]{1,0:T(4,128)} %kind_ref.3) | copy-start | bytes 18436
  6.4 3.0 %copy-start.3 = (s32[3,512]{1,0:T(4,128)S(1)}, s32[3,512]{1,0:T(4,128)}, u32[]{:S(2)}) copy-start(s32[3,512]{1,0:T(4,128)} %cell_ref.3) | copy-start | bytes 18436
  7.1 2.4 %copy-start.2 = (s32[3,512]{1,0:T(4,128)S(1)}, s32[3,512]{1,0:T(4,128)}, u32[]{:S(2)}) copy-start(s32[3,512]{1,0:T(4,128)} %owner_ref.3) | copy-start | bytes 18436
  7.1 2.4 %copy-start.6 = (s32[3]{0:T(128)S(1)}, s32[3]{0:T(128)}, u32[]{:S(2)}) copy-start(s32[3]{0:T(128)} %order_ref.5) | copy-start | bytes 40
  7.1 2.4 %copy-start.8 = (f32[2]{0:T(128)S(1)}, f32[2]{0:T(128)}, u32[]{:S(2)}) copy-start(f32[2]{0:T(128)} %courant_ref.1) | copy-start | bytes 28
  12.3 62.3 %all-to-all-start = ((f32[512,1,128]{2,1,0:T(1,128)}), f32[512,1,128]{2,1,0:T(1,128)S(1)}, u32[]{:S(2)}, u32[]{:S(2)}) async-start(f32[512,1,128]{2,1,0:T(1,128)} %bitcast.4), calls=%async_computation | async-start | bytes 524288 | tf_op jit(solution)/shard_map/all_to_all | solution.py:426
  49.7 12.0 %collective-permute-start.2 = (f32[4,32,256]{2,1,0:T(8,128)S(1)}, f32[4,32,256]{2,1,0:T(8,128)S(1)}, u32[]{:S(2)}, u32[]{:S(2)}) collective-permute-start(f32[4,32,256]{2,1,0:T(8,128)S(1)} %get-tuple-element.16), channel_id=1, source_target_pairs={{0,8},{8,16},{16,24},{24,32},{32,40},{40,48},{48,56},{56,64},{64,7... | collective-permute-start | bytes 393224 | tf_op jit(solution)/shard_map/ppermute | solution.py:381
  53.3 8.3 %collective-permute-start.3 = (f32[4,32,256]{2,1,0:T(8,128)S(1)}, f32[4,32,256]{2,1,0:T(8,128)S(1)}, u32[]{:S(2)}, u32[]{:S(2)}) collective-permute-start(f32[4,32,256]{2,1,0:T(8,128)S(1)} %get-tuple-element.17), channel_id=1, source_target_pairs={{0,504},{8,0},{16,8},{24,16},{32,24},{40,32},{48,40},{56,48},{64,5... | collective-permute-start | bytes 393224 | tf_op jit(solution)/shard_map/ppermute | solution.py:381
  75.5 49.6 %copy-start.5 = (f32[3,512]{1,0:T(4,128)S(1)}, f32[3,512]{1,0:T(4,128)}, u32[]{:S(2)}) copy-start(f32[3,512]{1,0:T(4,128)} %value_ref.1) | copy-start | bytes 18436
  125.1 0.7 copy-start.7
  125.1 0.7 copy-start.9

commit v2 on v1

--- a/solution.py
+++ b/solution.py
@@ -3,6 +3,7 @@
 from jax import lax
 from jax.experimental import pallas as pl
 from jax.experimental.pallas import tpu as pltpu
+from jax.sharding import Mesh
 from jax.sharding import PartitionSpec as P
 
 MEMBERS = 32
@@ -22,9 +23,16 @@
 LOC_Y = 512.0
 REACH = 2
 SPAN = 2 * REACH + 1
-WINDOW = SPAN * TILES_Y
+PLANES = 32
+LAYERS = 16
+HALF = CY // 2
+GX = ("x", "z_lo", "core")
+GY = ("z_hi", "y")
+PLANE = ("x", "core", "y")
+LAYER = ("z_lo", "z_hi")
 CHUNK = 256
 AHEAD = GROUPS * CELLS
+PAIRS = ((0, 1), (0, 2), (1, 2))
 
 diffuse_rate = 0.1
 mixing_rate = 0.05
@@ -163,6 +171,20 @@
     send_ref[...] = jnp.concatenate(blocks, axis=0).T
 
 
+def collect_kernel(recv_ref, send_ref):
+    lane = lax.broadcasted_iota(I32, (LAYERS, CY), 1)
+    total = jnp.zeros((LAYERS, CY), F32)
+    marks = jnp.zeros((LAYERS, CY), F32)
+    for plane in range(PLANES):
+        rows = recv_ref[plane * LAYERS : (plane + 1) * LAYERS, :]
+        total = total + rows
+        for turn in range(2):
+            at = BATCHES * MEMBERS + turn
+            marks = jnp.where(lane == turn * PLANES + plane, rows[:, at : at + 1], marks)
+    send_ref[pl.ds(0, LAYERS, stride=2), :] = total
+    send_ref[pl.ds(1, LAYERS, stride=2), :] = marks
+
+
 def merge_kernel(
     order_ref,
     place_ref,
@@ -174,9 +196,9 @@
     forecast_ref,
     send_ref,
 ):
-    place = place_ref[0] * TILES_Y + place_ref[1]
+    relay = place_ref[2]
     lane = lax.broadcasted_iota(I32, (1, CY), 1)
-    top = jnp.sum(recv_ref[...], axis=0, keepdims=True)
+    top = jnp.sum(recv_ref[pl.ds(0, LAYERS, stride=2), :], axis=0, keepdims=True)
     top = jnp.where(lane < BATCHES * MEMBERS, top, 0.0)
     for group in range(GROUPS):
         own = own_ref[group]
@@ -192,20 +214,31 @@
         deviation = value - centre
         total = jnp.sum(jnp.sum(deviation * deviation, axis=0, keepdims=True), axis=1, keepdims=True)
         top = jnp.where(lane == BATCHES * MEMBERS + group, total, top)
-    pieces = []
-    for turn in range(2):
-        column = relay_ref[order_ref[turn], place] >> 3
-        for step in range(SPAN):
-            at = (column + (step - REACH)) & (TILES_X - 1)
-            start = pl.multiple_of(at * TILES_Y, TILES_Y)
-            pieces.append(recv_ref[pl.ds(start, TILES_Y), :])
-    pieces.append(jnp.zeros((CY - 2 * WINDOW, CY), F32))
-    turned = jnp.concatenate(pieces, axis=0).T
-    first = turned[BATCHES * MEMBERS : BATCHES * MEMBERS + 1]
-    second = turned[BATCHES * MEMBERS + 1 : BATCHES * MEMBERS + 2]
-    bottom = jnp.where(lane < WINDOW, first, jnp.where(lane < 2 * WINDOW, second, 0.0))
+
+    marks = recv_ref[pl.ds(1, LAYERS, stride=2), :]
+    lanes = lax.broadcasted_iota(I32, (LAYERS, CY), 1)
+    subs = lax.broadcasted_iota(I32, (LAYERS, CY), 0)
+    tile_x = ((lanes >> 3) & 3) * 16 + (subs >> 1) * 2 + ((lanes >> 2) & 1)
+    first = relay_ref[order_ref[0], relay] >> 3
+    second = relay_ref[order_ref[1], relay] >> 3
+    column = jnp.where(lanes < PLANES, first, second)
+    near = ((tile_x - column + REACH) & (TILES_X - 1)) < SPAN
+    marks = jnp.where(near & (lanes < 2 * PLANES), marks, 0.0)
+    marks = marks[:8] + marks[8:]
+    folded = marks
+    for step in (8, 16, 24):
+        folded = folded + pltpu.roll(marks, CY - step, 1)
+    lanes = lax.broadcasted_iota(I32, (8, CY), 1)
+    subs = lax.broadcasted_iota(I32, (8, CY), 0)
+    bottom = jnp.zeros((8, CY), F32)
+    for row in range(8):
+        for turn in range(2):
+            moved = pltpu.roll(folded, (turn * PLANES + row * 8) % CY, 1)
+            there = (subs == row) & ((lanes >> 3) == turn * 8 + row)
+            bottom = jnp.where(there, moved, bottom)
+    bottom = jnp.sum(bottom, axis=0, keepdims=True)
     pair = jnp.concatenate([top, bottom] * 4, axis=0)
-    send_ref[...] = jnp.concatenate([pair] * (2 * TILES // 8), axis=0)
+    send_ref[...] = jnp.concatenate([pair] * (2 * LAYERS // 8), axis=0)
 
 
 def assimilate_kernel(
@@ -247,7 +280,7 @@
     sub = lax.broadcasted_iota(I32, (CY, OBS), 0)
     table_ref[...] = jnp.zeros_like(table_ref)
     table = jnp.zeros((CY, OBS), F32)
-    near = 4 * REACH + 1
+    columns, spots = [], []
     for turn in range(BATCHES):
         batch = order_ref[turn]
         owner = owner_ref[pl.ds(batch, 1), :]
@@ -257,17 +290,19 @@
         mask = mask_ref[pl.ds(batch, 1), :].astype(F32)
         xs.append(((owner >> 3) * CX + (cell >> 7)).astype(F32))
         ys.append(((owner & (TILES_Y - 1)) * CY + (cell & (CY - 1))).astype(F32))
-        offset = ((owner >> 3) - place_x + REACH) & (TILES_X - 1)
-        offset = jnp.where(offset >= TILES_X // 2, offset - TILES_X, offset).astype(F32)
-        for row, value in enumerate((xs[turn], ys[turn], mask, offset)):
+        tile_x = owner >> 3
+        columns.append(tile_x + REACH)
+        for row, value in enumerate((xs[turn], ys[turn], mask, tile_x.astype(F32))):
             table = jnp.where(sub == turn * 4 + row, value, table)
         prior = upper[turn * MEMBERS : (turn + 1) * MEMBERS]
         centre = jnp.sum(prior, axis=0, keepdims=True) * (1.0 / MEMBERS)
         factor = jnp.where(kinds[turn] == 0, stretch[0], stretch[2])
         state_ref[:, AHEAD + turn * OBS : AHEAD + (turn + 1) * OBS] = centre + factor * (prior - centre)
-        at = ((owner >> 3) - place_x + 2 * REACH) & (TILES_X - 1)
-        index = jnp.where(at < near, at * TILES_Y + (owner & (TILES_Y - 1)), -1)
-        spots_ref[:, turn * OBS : (turn + 1) * OBS] = jnp.where(sub == index, 1.0, 0.0).astype(BF16)
+        strip = ((tile_x >> 1) & 3) * 2 + ((owner >> 2) & 1)
+        spots.append(strip * 8 + (tile_x & 1) * 4 + (owner & 3))
+    for number, (turn, other) in enumerate(PAIRS):
+        hot = jnp.where(sub == spots[other] + turn * HALF, 1.0, 0.0)
+        spots_ref[:, number * OBS : (number + 1) * OBS] = hot.astype(BF16)
     table_ref[...] = table.T
 
     lane = lax.broadcasted_iota(I32, (1, CY), 1)
@@ -321,18 +356,13 @@
                 room = jnp.maximum((1.0 - gap_x * gap_x * (1.0 / (LOC_X * LOC_X))) - drop_y, 0.0)
                 weight_ref[:, x * CY : (x + 1) * CY] = room * room * mask_col
             if later:
-                offset = table[:, turn * 4 + 3 : turn * 4 + 4]
-                seen = recv_ref[pl.ds(2 * start + 1, CHUNK, stride=2), :]
-                if turn == 1:
-                    seen = pltpu.roll(seen, CY - WINDOW, 1)
-                seen = jnp.where(lane < WINDOW, seen, 0.0)
-                reach = jnp.zeros_like(seen)
-                for hop in range(-(SPAN - 1), near):
-                    moved = pltpu.roll(seen, (hop * TILES_Y) % CY, 1) if hop else seen
-                    reach = jnp.where(offset == float(hop), moved, reach)
-                reach = reach.astype(BF16)
+                column = table[:, turn * 4 + 3 : turn * 4 + 4].astype(I32)
+                marks = recv_ref[pl.ds(2 * start + 1, CHUNK, stride=2), :].astype(BF16)
                 for place, other in enumerate(later):
-                    allowed = mm(reach, spots_ref[:, other * OBS : (other + 1) * OBS])
+                    number = PAIRS.index((turn, other))
+                    allowed = mm(marks, spots_ref[:, number * OBS : (number + 1) * OBS])
+                    apart = (columns[other] - column) & (TILES_X - 1)
+                    allowed = jnp.where(apart < SPAN, allowed, 0.0)
                     gap_x = jnp.abs(x_col - xs[other])
                     gap_x = jnp.minimum(gap_x, NX - gap_x)
                     gap_y = y_col - ys[other]
@@ -393,12 +423,15 @@
     tile_mask,
     batch_order,
 ):
-    place = jnp.stack([lax.axis_index("gx"), lax.axis_index("gy")]).astype(I32)
+    place_x = lax.axis_index(GX)
+    place_y = lax.axis_index(GY)
+    relay = lax.axis_index(PLANE) * LAYERS + lax.axis_index(LAYER)
+    place = jnp.stack([place_x, place_y, relay]).astype(I32)
     ens = ensemble.reshape(MEMBERS * GROUPS * CX, CY)
     mask = tile_mask.reshape(BATCHES, OBS)
     low, high = call(edges_kernel, [VMEM], [shape(2, OBS)] * 2)(ens)
-    before = shifted(high, "gy", 1, False)
-    behind = shifted(low, "gy", -1, False)
+    before = shifted(high, GY, 1, False)
+    behind = shifted(low, GY, -1, False)
     own, left, right, send = call(
         spread_kernel,
         [SMEM] * 3 + [VMEM] * 7,
@@ -421,15 +454,19 @@
         obs_kind,
         mask,
     )
-    from_left = shifted(right, "gx", 1, True)
-    from_right = shifted(left, "gx", -1, True)
-    recv = lax.all_to_all(send.reshape(TILES, 1, CY), ("gx", "gy"), 0, 0)
+    from_left = shifted(right, GX, 1, True)
+    from_right = shifted(left, GX, -1, True)
+    recv = lax.all_to_all(send.reshape(PLANES, LAYERS, CY), PLANE, 0, 0)
+    send = call(collect_kernel, [VMEM], [shape(2 * LAYERS, CY)])(recv.reshape(TILES, CY))
+    recv = lax.all_to_all(send.reshape(LAYERS, 2, CY), LAYER, 0, 0)
     forecast, send = call(
         merge_kernel,
         [SMEM] * 3 + [VMEM] * 4,
-        [shape(GROUPS, MEMBERS, CELLS), shape(2 * TILES, CY)],
-    )(batch_order, place, obs_owner, own, from_left, from_right, recv.reshape(TILES, CY))
-    recv = lax.all_to_all(send.reshape(TILES, 2, CY), ("gx", "gy"), 0, 0)
+        [shape(GROUPS, MEMBERS, CELLS), shape(2 * LAYERS, CY)],
+    )(batch_order, place, obs_owner, own, from_left, from_right, recv.reshape(2 * LAYERS, CY))
+    recv = lax.all_to_all(send.reshape(LAYERS, 2, CY), LAYER, 0, 0)
+    send = jnp.broadcast_to(recv.reshape(1, 2 * LAYERS, CY), (PLANES, 2 * LAYERS, CY))
+    recv = lax.all_to_all(send, PLANE, 0, 0)
     out = call(
         assimilate_kernel,
         [SMEM] * 4 + [VMEM] * 7,
@@ -460,17 +497,18 @@
 
 
 def solution(mesh):
+    fine = Mesh(mesh.devices.reshape(4, 8, 2, 2, 4), ("x", "z_lo", "core", "z_hi", "y"))
     in_specs = (
-        P(None, None, None, "gx", "gy"),
-        P(),
-        P(),
-        P(),
-        P(),
-        P(),
-        P(),
-        P(),
-        P(None, "gx", "gy", None),
+        P(None, None, None, GX, GY),
+        P(),
+        P(),
+        P(),
+        P(),
+        P(),
+        P(),
+        P(),
+        P(None, GX, GY, None),
         P(),
     )
-    out_specs = P(None, None, None, "gx", "gy")
-    return jax.shard_map(local, mesh=mesh, in_specs=in_specs, out_specs=out_specs, check_vma=False)
+    out_specs = P(None, None, None, GX, GY)
+    return jax.shard_map(local, mesh=fine, in_specs=in_specs, out_specs=out_specs, check_vma=False)

time: 142 us -> 122 us (0.86)
  blocking collectives: 49.6 us -> 36.1 us
  starting transfers between devices: 50.8 us -> 47.6 us
  Pallas kernels: 19.2 us -> 17.5 us
    all_to_all x1 -> x2, blocking collectives: 49.6 us -> 36.1 us  [the longest x1 22.3 us: local(): recv = lax.all_to_all(send, PLANE, 0, 0)]
    ppermute x4, waiting for transfers between devices: 6.2 us -> 2.33 us  [shifted(): return lax.ppermute(value, axis, pairs)]
    ppermute x4, starting transfers between devices: 13.5 us -> 10 us  [shifted(): return lax.ppermute(value, axis, pairs)]
    pallas_call x1, Pallas kernels: 15.4 us -> 12.9 us  [local(): call(assimilate_kernel, [SMEM] * 4 + [VMEM] * 7, [shape(MEMBERS * GROUPS...]
    all_to_all x1 -> x2, waiting for transfers between devices: 12.9 us -> 15.4 us  [the longest x1 11.3 us: local(): recv = lax.all_to_all(send.reshape(LAYERS, 2, CY), LAYER, 0, 0)]
    all_to_all x1 -> x2, starting transfers between devices: 37.4 us -> 37.6 us  [the longest x1 31.7 us: local(): recv = lax.all_to_all(send.reshape(PLANES, LAYERS, CY), PLANE, 0, 0)]
  transfers between devices with their start and end apart: 5 -> 6, of which waited for: 3 -> 3; matrix products, arithmetic and copies ran while one was open for 0% -> 0% of each run, Pallas kernels for 0% -> 1%
where the time goes in v2:
time: 122 us; the launch traced here: 121 us
  starting transfers between devices  47.6 us (39%)
  blocking collectives  36.1 us (30%)
  waiting for transfers between devices  17.7 us (15%)
  Pallas kernels  17.5 us (14%)
  local copies, waits for them, and re-layouts  2.3 us (2%)
    all_to_all x1, starting transfers between devices, local(): recv = lax.all_to_all(send.reshape(PLANES, LAYERS, CY), PLANE, 0, 0)  31.7 us
    all_to_all x1, blocking collectives, local(): recv = lax.all_to_all(send, PLANE, 0, 0)  22.3 us
    all_to_all x1, blocking collectives, local(): recv = lax.all_to_all(send.reshape(LAYERS, 2, CY), LAYER, 0, 0)  13.8 us
    pallas_call x1, Pallas kernels, local(): call(assimilate_kernel, [SMEM] * 4 + [VMEM] * 7, [shape(MEMBERS * GROUPS...  12.9 us
    all_to_all x1, waiting for transfers between devices, local(): recv = lax.all_to_all(send.reshape(LAYERS, 2, CY), LAYER, 0, 0)  11.3 us
    ppermute x4, starting transfers between devices, shifted(): return lax.ppermute(value, axis, pairs)  10 us
    all_to_all x1, starting transfers between devices, local(): recv = lax.all_to_all(send.reshape(LAYERS, 2, CY), LAYER, 0, 0)  5.85 us
    all_to_all x1, waiting for transfers between devices, local(): recv = lax.all_to_all(send.reshape(PLANES, LAYERS, CY), PLANE, 0, 0)  4.1 us
  transfers between devices with their start and end apart: 6, of which 3 were waited for; matrix products, arithmetic and copies ran while one was open for 0% of the time, Pallas kernels for 1%

profile of v2, /device:TPU:1, one launch (start us, length us, event | category | flops | bytes accessed | tf_op | source)
XLA Modules:
  0.0 121.5 jit_solution(2620609913440123528)
XLA Ops:
  0.0 0.0 copy-start
  0.0 0.9 copy-done
  1.0 0.0 copy-start.1
  1.0 0.1 shard_map.100
  1.1 4.0 %collective-permute-start = (f32[2,512]{1,0:T(2,128)S(1)}, f32[2,512]{1,0:T(2,128)S(1)}, u32[]{:S(2)}, u32[]{:S(2)}) collective-permute-start(f32[2,512]{1,0:T(2,128)S(1)} %get-tuple-element.13), channel_id=1, source_target_pairs={{0,1},{1,2},{2,3},{3,4},{4,5},{5,6},{6,7},{8,9},{9,10},{10,11},{11... | collective-permute-start | bytes 12296 | tf_op jit(solution)/shard_map/ppermute | solution.py:411
  5.1 1.3 %collective-permute-start.1 = (f32[2,512]{1,0:T(2,128)S(1)}, f32[2,512]{1,0:T(2,128)S(1)}, u32[]{:S(2)}, u32[]{:S(2)}) collective-permute-start(f32[2,512]{1,0:T(2,128)S(1)} %get-tuple-element.14), channel_id=1, source_target_pairs={{1,0},{2,1},{3,2},{4,3},{5,4},{6,5},{7,6},{9,8},{10,9},{11,10},{12... | collective-permute-start | bytes 12296 | tf_op jit(solution)/shard_map/ppermute | solution.py:411
  6.4 0.0 copy-start.10
  6.4 0.0 copy-start.4
  6.5 0.0 copy-start.3
  6.5 0.1 pad_add_fusion.place_ref
  6.6 0.6 copy-done.10
  7.1 0.0 copy-start.2
  7.1 0.0 copy-start.6
  7.1 0.0 copy-start.8
  7.1 0.0 collective-permute-done.before_ref
  7.2 2.3 %collective-permute-done.1.behind_ref = f32[2,512]{1,0:T(2,128)S(1)} collective-permute-done((f32[2,512]{1,0:T(2,128)S(1)}, f32[2,512]{1,0:T(2,128)S(1)}, u32[]{:S(2)}, u32[]{:S(2)}) %collective-permute-start.1) | collective-permute-done | bytes 4128 | tf_op jit(solution)/shard_map/ppermute | solution.py:411
  9.5 0.0 copy-done.1
  9.5 0.0 copy-done.4
  9.5 0.0 copy-done.3
  9.5 0.0 copy-done.2
  9.5 0.0 copy-done.6
  9.5 0.0 copy-done.8
  9.5 2.8 %shard_map.101 = (f32[4,32,512]{2,1,0:T(8,128)S(1)}, f32[4,32,256]{2,1,0:T(8,128)S(1)}, f32[4,32,256]{2,1,0:T(8,128)S(1)}, f32[512,128]{1,0:T(8,128)}) custom-call(s32[3]{0:T(128)S(1)} %copy-done.6, s32[3]{0:T(128)S(1)} %pad_add_fusion.place_ref, f32[2]{0:T(128)S(1)} %copy-done.8, f32[512,128]{1,0:T(8,128)S(1)} %bitcast.17, ...), custom_call_target="tpu_custom_call" | custom-call | tf_op jit(solution)/shard_map/pallas_call | solution.py:435
  12.3 31.7 %all-to-all-start = ((f32[32,16,128]{2,1,0:T(8,128)}), f32[32,16,128]{2,1,0:T(8,128)S(1)}, u32[]{:S(2)}, u32[]{:S(2)}) async-start(f32[32,16,128]{2,1,0:T(8,128)} %bitcast.4), calls=%async_computation | async-start | bytes 524288 | tf_op jit(solution)/shard_map/all_to_all | solution.py:459
  44.0 2.8 %collective-permute-start.2 = (f32[4,32,256]{2,1,0:T(8,128)S(1)}, f32[4,32,256]{2,1,0:T(8,128)S(1)}, u32[]{:S(2)}, u32[]{:S(2)}) collective-permute-start(f32[4,32,256]{2,1,0:T(8,128)S(1)} %get-tuple-element.16), channel_id=1, source_target_pairs={{0,8},{8,16},{16,24},{24,32},{32,40},{40,48},{48,56},{56,64},{64,7... | collective-permute-start | bytes 393224 | tf_op jit(solution)/shard_map/ppermute | solution.py:411
  46.8 1.9 %collective-permute-start.3 = (f32[4,32,256]{2,1,0:T(8,128)S(1)}, f32[4,32,256]{2,1,0:T(8,128)S(1)}, u32[]{:S(2)}, u32[]{:S(2)}) collective-permute-start(f32[4,32,256]{2,1,0:T(8,128)S(1)} %get-tuple-element.17), channel_id=1, source_target_pairs={{0,504},{8,0},{16,8},{24,16},{32,24},{40,32},{48,40},{56,48},{64,5... | collective-permute-start | bytes 393224 | tf_op jit(solution)/shard_map/ppermute | solution.py:411
  48.7 4.1 %all-to-all-done = f32[32,16,128]{2,1,0:T(8,128)S(1)} async-done(((f32[32,16,128]{2,1,0:T(8,128)}), f32[32,16,128]{2,1,0:T(8,128)S(1)}, u32[]{:S(2)}, u32[]{:S(2)}) %all-to-all-start) | async-done | bytes 262176 | tf_op jit(solution)/shard_map/all_to_all | solution.py:459
  52.8 0.9 shard_map.102
  53.7 5.9 %all-to-all-start.1 = ((f32[16,2,128]{2,1,0:T(2,128)}), f32[16,2,128]{2,1,0:T(2,128)S(1)}, u32[]{:S(2)}, u32[]{:S(2)}) async-start(f32[16,2,128]{2,1,0:T(2,128)} %bitcast.6), calls=%async_computation.1 | async-start | bytes 32768 | tf_op jit(solution)/shard_map/all_to_all | solution.py:461
  59.6 0.0 collective-permute-done.2.from_left_ref
  59.6 0.0 collective-permute-done.3.from_right_ref
  59.6 11.3 %all-to-all-done.1 = f32[16,2,128]{2,1,0:T(2,128)S(1)} async-done(((f32[16,2,128]{2,1,0:T(2,128)}), f32[16,2,128]{2,1,0:T(2,128)S(1)}, u32[]{:S(2)}, u32[]{:S(2)}) %all-to-all-start.1) | async-done | bytes 16416 | tf_op jit(solution)/shard_map/all_to_all | solution.py:461
  70.9 0.9 shard_map.103
  71.7 13.8 %all_to_all.20 = f32[16,2,128]{2,1,0:T(2,128)S(1)} all-to-all(f32[16,2,128]{2,1,0:T(2,128)S(1)} %bitcast.22), channel_id=1, replica_groups=mesh['x'=4,'z_lo'=8,'core'=2,'z_hi'=2,'y'=4] {'z_lo','z_hi'}, dimensions={0} | all-to-all | bytes 32768 | tf_op jit(solution)/shard_map/all_to_all | solution.py:467
  85.6 0.0 copy-start.5
  85.6 22.3 %all_to_all.21 = f32[32,32,128]{2,1,0:T(8,128)S(1)} all-to-all(f32[32,32,128]{2,1,0:T(8,128)S(1)} %broadcast_in_dim.8), channel_id=1, replica_groups=mesh['x'=4,'z_lo'=8,'core'=2,'z_hi'=2,'y'=4] {'x','core','y'}, dimensions={0} | all-to-all | bytes 1048576 | tf_op jit(solution)/shard_map/all_to_all | solution.py:469
  107.9 0.0 copy-start.7
  107.9 0.0 copy-start.9
  107.9 0.0 copy-done.5
  107.9 0.7 copy-done.7
  108.6 0.0 copy-done.9
  108.6 12.9 %shard_map.104 = f32[512,128]{1,0:T(8,128)} custom-call(s32[3]{0:T(128)S(1)} %copy-done.6, s32[3]{0:T(128)S(1)} %pad_add_fusion.place_ref, f32[2,2]{1,0:T(2,128)S(1)} %copy-done.7, f32[2]{0:T(128)S(1)} %copy-done.9, f32[4,32,512]{2,1,0:T(8,128)S(1)} %get-tuple-element.19.forecast_ref, f32[1024,128]{1,0:T(8,128)S(1)} %bitcast.15, s32[3,512]{1,0:T(4,128)S(1)} %copy-done.2, ...), custom_call_target="tpu_custom_call" | custom-call | tf_op jit(solution)/shard_map/pallas_call | solution.py:470
  (2 shorter events, 0.1 us)
Async XLA Ops:
  0.0 0.9 copy-start
  1.0 8.5 %copy-start.1 = (f32[32,2,2,4,128]{4,3,2,1,0:T(4,128)S(1)}, f32[32,2,2,4,128]{4,3,2,1,0:T(4,128)}, u32[]{:S(2)}) copy-start(f32[32,2,2,4,128]{4,3,2,1,0:T(4,128)} %param.10) | copy-start | bytes 786436
  1.1 6.1 %collective-permute-start = (f32[2,512]{1,0:T(2,128)S(1)}, f32[2,512]{1,0:T(2,128)S(1)}, u32[]{:S(2)}, u32[]{:S(2)}) collective-permute-start(f32[2,512]{1,0:T(2,128)S(1)} %get-tuple-element.13), channel_id=1, source_target_pairs={{0,1},{1,2},{2,3},{3,4},{4,5},{5,6},{6,7},{8,9},{9,10},{10,11},{11... | collective-permute-start | bytes 12296 | tf_op jit(solution)/shard_map/ppermute | solution.py:411
  5.1 4.4 %collective-permute-start.1 = (f32[2,512]{1,0:T(2,128)S(1)}, f32[2,512]{1,0:T(2,128)S(1)}, u32[]{:S(2)}, u32[]{:S(2)}) collective-permute-start(f32[2,512]{1,0:T(2,128)S(1)} %get-tuple-element.14), channel_id=1, source_target_pairs={{1,0},{2,1},{3,2},{4,3},{5,4},{6,5},{7,6},{9,8},{10,9},{11,10},{12... | collective-permute-start | bytes 12296 | tf_op jit(solution)/shard_map/ppermute | solution.py:411
  6.4 0.7 copy-start.10
  6.4 3.0 %copy-start.4 = (s32[3,512]{1,0:T(4,128)S(1)}, s32[3,512]{1,0:T(4,128)}, u32[]{:S(2)}) copy-start(s32[3,512]{1,0:T(4,128)} %kind_ref.3) | copy-start | bytes 18436
  6.5 3.0 %copy-start.3 = (s32[3,512]{1,0:T(4,128)S(1)}, s32[3,512]{1,0:T(4,128)}, u32[]{:S(2)}) copy-start(s32[3,512]{1,0:T(4,128)} %cell_ref.3) | copy-start | bytes 18436
  7.1 2.4 %copy-start.2 = (s32[3,512]{1,0:T(4,128)S(1)}, s32[3,512]{1,0:T(4,128)}, u32[]{:S(2)}) copy-start(s32[3,512]{1,0:T(4,128)} %owner_ref.3) | copy-start | bytes 18436
  7.1 2.4 %copy-start.6 = (s32[3]{0:T(128)S(1)}, s32[3]{0:T(128)}, u32[]{:S(2)}) copy-start(s32[3]{0:T(128)} %order_ref.5) | copy-start | bytes 40
  7.1 2.4 %copy-start.8 = (f32[2]{0:T(128)S(1)}, f32[2]{0:T(128)}, u32[]{:S(2)}) copy-start(f32[2]{0:T(128)} %courant_ref.1) | copy-start | bytes 28
  12.3 40.6 %all-to-all-start = ((f32[32,16,128]{2,1,0:T(8,128)}), f32[32,16,128]{2,1,0:T(8,128)S(1)}, u32[]{:S(2)}, u32[]{:S(2)}) async-start(f32[32,16,128]{2,1,0:T(8,128)} %bitcast.4), calls=%async_computation | async-start | bytes 524288 | tf_op jit(solution)/shard_map/all_to_all | solution.py:459
  44.0 15.5 %collective-permute-start.2 = (f32[4,32,256]{2,1,0:T(8,128)S(1)}, f32[4,32,256]{2,1,0:T(8,128)S(1)}, u32[]{:S(2)}, u32[]{:S(2)}) collective-permute-start(f32[4,32,256]{2,1,0:T(8,128)S(1)} %get-tuple-element.16), channel_id=1, source_target_pairs={{0,8},{8,16},{16,24},{24,32},{32,40},{40,48},{48,56},{56,64},{64,7... | collective-permute-start | bytes 393224 | tf_op jit(solution)/shard_map/ppermute | solution.py:411
  46.8 12.8 %collective-permute-start.3 = (f32[4,32,256]{2,1,0:T(8,128)S(1)}, f32[4,32,256]{2,1,0:T(8,128)S(1)}, u32[]{:S(2)}, u32[]{:S(2)}) collective-permute-start(f32[4,32,256]{2,1,0:T(8,128)S(1)} %get-tuple-element.17), channel_id=1, source_target_pairs={{0,504},{8,0},{16,8},{24,16},{32,24},{40,32},{48,40},{56,48},{64,5... | collective-permute-start | bytes 393224 | tf_op jit(solution)/shard_map/ppermute | solution.py:411
  53.7 17.2 %all-to-all-start.1 = ((f32[16,2,128]{2,1,0:T(2,128)}), f32[16,2,128]{2,1,0:T(2,128)S(1)}, u32[]{:S(2)}, u32[]{:S(2)}) async-start(f32[16,2,128]{2,1,0:T(2,128)} %bitcast.6), calls=%async_computation.1 | async-start | bytes 32768 | tf_op jit(solution)/shard_map/all_to_all | solution.py:461
  85.6 22.3 %copy-start.5 = (f32[3,512]{1,0:T(4,128)S(1)}, f32[3,512]{1,0:T(4,128)}, u32[]{:S(2)}) copy-start(f32[3,512]{1,0:T(4,128)} %value_ref.1) | copy-start | bytes 18436
  107.9 0.7 copy-start.7
  107.9 0.7 copy-start.9

commit v3 on v2

--- a/solution.py
+++ b/solution.py
@@ -26,6 +26,10 @@
 PLANES = 32
 LAYERS = 16
 HALF = CY // 2
+RIM = 16
+SLOT = TILES_X + RIM
+VALUES = BATCHES * MEMBERS
+WIDE = (CX + 4) * CY
 GX = ("x", "z_lo", "core")
 GY = ("z_hi", "y")
 PLANE = ("x", "core", "y")
@@ -64,12 +68,6 @@
     rest = value - high.astype(F32)
     middle = rest.astype(BF16)
     return high, middle, (rest - middle.astype(F32)).astype(BF16)
-
-
-def edges_kernel(ens_ref, low_ref, high_ref):
-    turned = ens_ref[...].T
-    low_ref[...] = turned[0:2]
-    high_ref[...] = turned[CY - 2 : CY]
 
 
 def advance(rows, courant_ref, keep):
@@ -102,43 +100,38 @@
     place_ref,
     courant_ref,
     ens_ref,
-    before_ref,
-    behind_ref,
     owner_ref,
     cell_ref,
     kind_ref,
     mask_ref,
-    own_ref,
-    left_ref,
-    right_ref,
+    tile_ref,
     send_ref,
-    outer_ref,
 ):
     place_x = place_ref[0]
     place_y = place_ref[1]
-    rim = jnp.concatenate(
-        [behind_ref[...], jnp.zeros((CY - 4, OBS), F32), before_ref[...]], axis=0
-    )
-    outer_ref[...] = rim.T
     rows = {}
     for group in range(GROUPS):
         for x in range(CX):
-            rows[group, x] = jnp.concatenate(
-                [ens_ref[rows_of(group, x), :], outer_ref[rows_of(group, x), :]], axis=1
-            )
+            own = ens_ref[rows_of(group, x), :]
+            rows[group, x] = jnp.concatenate([own, jnp.zeros_like(own)], axis=1)
     lane = lax.broadcasted_iota(I32, (1, 2 * CY), 1)
     below = (lane >= 3 * CY // 2) & (place_y == 0)
     above = (lane >= CY) & (lane < 3 * CY // 2) & (place_y == TILES_Y - 1)
     keep = jnp.where(below | above, 0.0, 1.0).astype(F32)
     rows = advance(rows, courant_ref, keep)
     rows = advance(rows, courant_ref, None)
-    tile = {at: value[:, :CY] for at, value in rows.items()}
-    for group in range(GROUPS):
-        for x in range(CX):
-            own_ref[group, :, x * CY : (x + 1) * CY] = tile[group, x]
-        for x in range(2):
-            left_ref[group, :, x * CY : (x + 1) * CY] = tile[group, x - 2]
-            right_ref[group, :, x * CY : (x + 1) * CY] = tile[group, x + CX]
+    lane = lax.broadcasted_iota(I32, (MEMBERS, CY), 1)
+    low = jnp.zeros((MEMBERS, CY), F32)
+    high = jnp.zeros((MEMBERS, CY), F32)
+    tile = {}
+    for (group, x), value in rows.items():
+        tile[group, x] = value[:, :CY]
+        tile_ref[group, :, (x + 2) * CY : (x + 3) * CY] = tile[group, x]
+        rim = value[:, CY:]
+        at = group * 16 + (x + 2) * 2
+        there = (lane >> 1) == at // 2
+        low = jnp.where(there, pltpu.roll(rim, at + 2, 1), low)
+        high = jnp.where(there, pltpu.roll(rim, at, 1) if at else rim, high)
     ground = jnp.concatenate(
         [
             jnp.concatenate([tile[2 * field, x] for x in range(-2, CX + 2)], axis=1)
@@ -147,6 +140,7 @@
         axis=0,
     )
     parts = jnp.concatenate(thirds(ground), axis=0)
+    rims = jnp.concatenate(thirds(low + pltpu.roll(high, HALF, 1)), axis=0)
     blocks = []
     masks = []
     for turn in range(BATCHES):
@@ -157,32 +151,69 @@
         masks.append(mask_ref[pl.ds(batch, 1), :].astype(F32))
         at_x = ((owner >> 3) - place_x) * CX + (cell >> 7) + 2
         at_x = at_x & (NX - 1)
-        seen = (at_x < CX + 4) & ((owner & (TILES_Y - 1)) == place_y)
-        index = jnp.where(seen, at_x * CY + (cell & (CY - 1)), -1)
+        at_y = ((owner & (TILES_Y - 1)) - place_y) * CY + (cell & (CY - 1))
+        seen = at_x < CX + 4
+        index = jnp.where(seen & (at_y >= 0) & (at_y < CY), at_x * CY + at_y, -1)
+        corner = kind * 32 + at_x * 2
+        edge = jnp.where(seen & (at_y >= -2) & (at_y < 0), corner + at_y + 2, -1)
+        edge = jnp.where(seen & (at_y >= CY) & (at_y < CY + 2), corner + at_y - CY + HALF, edge)
         picked = jnp.zeros((parts.shape[0], OBS), F32)
-        for start in range(0, (CX + 4) * CY, CHUNK):
+        for start in range(0, WIDE, CHUNK):
             spot = lax.broadcasted_iota(I32, (CHUNK, OBS), 0) + start
             hot = jnp.where(spot == index, 1.0, 0.0).astype(BF16)
             picked = picked + mm(parts[:, start : start + CHUNK], hot)
         picked = picked[0:64] + picked[64:128] + picked[128:192]
-        blocks.append(jnp.where(kind == 0, picked[0:32], picked[32:64]))
+        spot = lax.broadcasted_iota(I32, (CY, OBS), 0)
+        found = mm(rims, jnp.where(spot == edge, 1.0, 0.0).astype(BF16))
+        found = found[0:32] + found[32:64] + found[64:96]
+        blocks.append(jnp.where(kind == 0, picked[0:32], picked[32:64]) + found)
     sub = lax.broadcasted_iota(I32, (MEMBERS, OBS), 0)
-    blocks.append(jnp.where(sub == 0, masks[0], jnp.where(sub == 1, masks[1], 0.0)))
-    send_ref[...] = jnp.concatenate(blocks, axis=0).T
-
-
-def collect_kernel(recv_ref, send_ref):
-    lane = lax.broadcasted_iota(I32, (LAYERS, CY), 1)
-    total = jnp.zeros((LAYERS, CY), F32)
-    marks = jnp.zeros((LAYERS, CY), F32)
-    for plane in range(PLANES):
-        rows = recv_ref[plane * LAYERS : (plane + 1) * LAYERS, :]
+    blocks.append(jnp.where(sub == 0, masks[0], jnp.where(sub == TILES_Y, masks[1], 0.0)))
+    turned = jnp.concatenate(blocks, axis=0).T
+    lane = lax.broadcasted_iota(I32, (RIM, CY), 1)
+    low = jnp.where(lane < HALF, low[:RIM], pltpu.roll(low[RIM:], HALF, 1))
+    high = jnp.where(lane < HALF, high[:RIM], pltpu.roll(high[RIM:], HALF, 1))
+    for slot in range(TILES_Y):
+        at = slot * SLOT
+        send_ref[at : at + TILES_X, :] = turned[slot * TILES_X : (slot + 1) * TILES_X]
+        after = jnp.where(place_y == slot - 1, 1.0, 0.0).astype(F32)
+        before = jnp.where(place_y == slot + 1, 1.0, 0.0).astype(F32)
+        send_ref[at + TILES_X : at + SLOT, :] = after * high + before * low
+
+
+def collect_kernel(place_ref, recv_ref, tile_ref, own_ref, left_ref, right_ref, send_ref):
+    place_y = place_ref[1]
+    lane = lax.broadcasted_iota(I32, (TILES_X, CY), 1)
+    total = jnp.zeros((TILES_X, CY), F32)
+    for row in range(TILES_Y):
+        rows = recv_ref[row * SLOT : row * SLOT + TILES_X, :]
+        if row:
+            marks = pltpu.roll(jnp.where(lane < VALUES, 0.0, rows), row, 1)
+            rows = jnp.where(lane < VALUES, rows, marks)
         total = total + rows
-        for turn in range(2):
-            at = BATCHES * MEMBERS + turn
-            marks = jnp.where(lane == turn * PLANES + plane, rows[:, at : at + 1], marks)
-    send_ref[pl.ds(0, LAYERS, stride=2), :] = total
-    send_ref[pl.ds(1, LAYERS, stride=2), :] = marks
+    send_ref[...] = total
+
+    def rim(row):
+        start = pl.multiple_of(row * SLOT + TILES_X, RIM)
+        rows = recv_ref[pl.ds(start, RIM), :]
+        return jnp.concatenate([rows, pltpu.roll(rows, HALF, 1)], axis=0)
+
+    below = rim(jnp.maximum(place_y - 1, 0))
+    above = rim(jnp.minimum(place_y + 1, TILES_Y - 1))
+    lane = lax.broadcasted_iota(I32, (MEMBERS, CY), 1)
+    for group in range(GROUPS):
+        for x in range(-2, CX + 2):
+            at = group * 16 + (x + 2) * 2
+            value = tile_ref[group, :, (x + 2) * CY : (x + 3) * CY]
+            first = pltpu.roll(below, CY - at, 1) if at else below
+            value = value + jnp.where(lane < 2, first, 0.0)
+            value = value + jnp.where(lane >= CY - 2, pltpu.roll(above, CY - 2 - at, 1), 0.0)
+            if x < 0:
+                left_ref[group, :, (x + 2) * CY : (x + 3) * CY] = value
+            elif x < CX:
+                own_ref[group, :, x * CY : (x + 1) * CY] = value
+            else:
+                right_ref[group, :, (x - CX) * CY : (x - CX + 1) * CY] = value
 
 
 def merge_kernel(
@@ -196,10 +227,11 @@
     forecast_ref,
     send_ref,
 ):
-    relay = place_ref[2]
+    relay = place_ref[1] * TILES_X + place_ref[0]
     lane = lax.broadcasted_iota(I32, (1, CY), 1)
-    top = jnp.sum(recv_ref[pl.ds(0, LAYERS, stride=2), :], axis=0, keepdims=True)
-    top = jnp.where(lane < BATCHES * MEMBERS, top, 0.0)
+    recv = recv_ref[...]
+    top = jnp.sum(recv, axis=0, keepdims=True)
+    top = jnp.where(lane < VALUES, top, 0.0)
     for group in range(GROUPS):
         own = own_ref[group]
         value = jnp.concatenate(
@@ -215,25 +247,23 @@
         total = jnp.sum(jnp.sum(deviation * deviation, axis=0, keepdims=True), axis=1, keepdims=True)
         top = jnp.where(lane == BATCHES * MEMBERS + group, total, top)
 
-    marks = recv_ref[pl.ds(1, LAYERS, stride=2), :]
-    lanes = lax.broadcasted_iota(I32, (LAYERS, CY), 1)
-    subs = lax.broadcasted_iota(I32, (LAYERS, CY), 0)
-    tile_x = ((lanes >> 3) & 3) * 16 + (subs >> 1) * 2 + ((lanes >> 2) & 1)
+    lanes = lax.broadcasted_iota(I32, (TILES_X, CY), 1)
+    tile_x = lax.broadcasted_iota(I32, (TILES_X, CY), 0)
     first = relay_ref[order_ref[0], relay] >> 3
     second = relay_ref[order_ref[1], relay] >> 3
-    column = jnp.where(lanes < PLANES, first, second)
+    column = jnp.where(lanes < VALUES + TILES_Y, first, second)
     near = ((tile_x - column + REACH) & (TILES_X - 1)) < SPAN
-    marks = jnp.where(near & (lanes < 2 * PLANES), marks, 0.0)
-    marks = marks[:8] + marks[8:]
-    folded = marks
-    for step in (8, 16, 24):
-        folded = folded + pltpu.roll(marks, CY - step, 1)
+    marks = jnp.where(near, recv, 0.0)
+    folded = marks[0:8]
+    for start in range(8, TILES_X, 8):
+        folded = folded + marks[start : start + 8]
     lanes = lax.broadcasted_iota(I32, (8, CY), 1)
     subs = lax.broadcasted_iota(I32, (8, CY), 0)
     bottom = jnp.zeros((8, CY), F32)
     for row in range(8):
         for turn in range(2):
-            moved = pltpu.roll(folded, (turn * PLANES + row * 8) % CY, 1)
+            step = turn * HALF + row * TILES_Y - VALUES - turn * TILES_Y
+            moved = pltpu.roll(folded, step % CY, 1) if step % CY else folded
             there = (subs == row) & ((lanes >> 3) == turn * 8 + row)
             bottom = jnp.where(there, moved, bottom)
     bottom = jnp.sum(bottom, axis=0, keepdims=True)
@@ -261,10 +291,20 @@
     table_ref,
     spots_ref,
     weight_ref,
+    rows_ref,
 ):
     place_x = place_ref[0]
     place_y = place_ref[1]
-    upper = recv_ref[pl.ds(0, TILES, stride=2), :].T
+    for x in range(4):
+        for core in range(2):
+            for y in range(4):
+                for z_hi in range(2):
+                    source = 2 * (x * 128 + core * 64 + y * 16 + z_hi)
+                    target = z_hi * 256 + y * 64 + x * 16 + core
+                    for half in range(2):
+                        rows = recv_ref[pl.ds(source + half, 8, stride=4), :]
+                        rows_ref[pl.ds(half * OBS + target, 8, stride=2), :] = rows
+    upper = rows_ref[:OBS].T
     stretch = []
     for group in range(GROUPS):
         row = BATCHES * MEMBERS + group
@@ -298,8 +338,7 @@
         centre = jnp.sum(prior, axis=0, keepdims=True) * (1.0 / MEMBERS)
         factor = jnp.where(kinds[turn] == 0, stretch[0], stretch[2])
         state_ref[:, AHEAD + turn * OBS : AHEAD + (turn + 1) * OBS] = centre + factor * (prior - centre)
-        strip = ((tile_x >> 1) & 3) * 2 + ((owner >> 2) & 1)
-        spots.append(strip * 8 + (tile_x & 1) * 4 + (owner & 3))
+        spots.append((tile_x & 7) * TILES_Y + (owner & (TILES_Y - 1)))
     for number, (turn, other) in enumerate(PAIRS):
         hot = jnp.where(sub == spots[other] + turn * HALF, 1.0, 0.0)
         spots_ref[:, number * OBS : (number + 1) * OBS] = hot.astype(BF16)
@@ -357,7 +396,7 @@
                 weight_ref[:, x * CY : (x + 1) * CY] = room * room * mask_col
             if later:
                 column = table[:, turn * 4 + 3 : turn * 4 + 4].astype(I32)
-                marks = recv_ref[pl.ds(2 * start + 1, CHUNK, stride=2), :].astype(BF16)
+                marks = rows_ref[pl.ds(OBS + start, CHUNK), :].astype(BF16)
                 for place, other in enumerate(later):
                     number = PAIRS.index((turn, other))
                     allowed = mm(marks, spots_ref[:, number * OBS : (number + 1) * OBS])
@@ -425,45 +464,33 @@
 ):
     place_x = lax.axis_index(GX)
     place_y = lax.axis_index(GY)
-    relay = lax.axis_index(PLANE) * LAYERS + lax.axis_index(LAYER)
-    place = jnp.stack([place_x, place_y, relay]).astype(I32)
+    place = jnp.stack([place_x, place_y]).astype(I32)
     ens = ensemble.reshape(MEMBERS * GROUPS * CX, CY)
     mask = tile_mask.reshape(BATCHES, OBS)
-    low, high = call(edges_kernel, [VMEM], [shape(2, OBS)] * 2)(ens)
-    before = shifted(high, GY, 1, False)
-    behind = shifted(low, GY, -1, False)
+    tile, send = call(
+        spread_kernel,
+        [SMEM] * 3 + [VMEM] * 5,
+        [shape(GROUPS, MEMBERS, WIDE), shape(TILES_Y * SLOT, CY)],
+    )(batch_order, place, courant, ens, obs_owner, obs_cell, obs_kind, mask)
+    recv = lax.all_to_all(send.reshape(TILES_Y, SLOT, CY), GY, 0, 0)
     own, left, right, send = call(
-        spread_kernel,
-        [SMEM] * 3 + [VMEM] * 7,
+        collect_kernel,
+        [SMEM] + [VMEM] * 2,
         [
             shape(GROUPS, MEMBERS, CELLS),
             shape(GROUPS, MEMBERS, 2 * CY),
             shape(GROUPS, MEMBERS, 2 * CY),
-            shape(OBS, CY),
+            shape(TILES_X, CY),
         ],
-        [pltpu.VMEM((MEMBERS * GROUPS * CX, CY), F32)],
-    )(
-        batch_order,
-        place,
-        courant,
-        ens,
-        before,
-        behind,
-        obs_owner,
-        obs_cell,
-        obs_kind,
-        mask,
-    )
+    )(place, recv.reshape(TILES_Y * SLOT, CY), tile)
     from_left = shifted(right, GX, 1, True)
     from_right = shifted(left, GX, -1, True)
-    recv = lax.all_to_all(send.reshape(PLANES, LAYERS, CY), PLANE, 0, 0)
-    send = call(collect_kernel, [VMEM], [shape(2 * LAYERS, CY)])(recv.reshape(TILES, CY))
-    recv = lax.all_to_all(send.reshape(LAYERS, 2, CY), LAYER, 0, 0)
+    recv = lax.all_to_all(send.reshape(TILES_X, 1, CY), GX, 0, 0)
     forecast, send = call(
         merge_kernel,
         [SMEM] * 3 + [VMEM] * 4,
         [shape(GROUPS, MEMBERS, CELLS), shape(2 * LAYERS, CY)],
-    )(batch_order, place, obs_owner, own, from_left, from_right, recv.reshape(2 * LAYERS, CY))
+    )(batch_order, place, obs_owner, own, from_left, from_right, recv.reshape(TILES_X, CY))
     recv = lax.all_to_all(send.reshape(LAYERS, 2, CY), LAYER, 0, 0)
     send = jnp.broadcast_to(recv.reshape(1, 2 * LAYERS, CY), (PLANES, 2 * LAYERS, CY))
     recv = lax.all_to_all(send, PLANE, 0, 0)
@@ -479,6 +506,7 @@
             pltpu.VMEM((OBS, CY), F32),
             pltpu.VMEM((CY, BATCHES * OBS), BF16),
             pltpu.VMEM((CHUNK, BATCHES * OBS), F32),
+            pltpu.VMEM((2 * OBS, CY), F32),
         ],
     )(
         batch_order,

time: 122 us -> 122 us (level)
  blocking collectives: 36.1 us -> 84.6 us
  starting transfers between devices: 47.6 us -> 16.4 us
  waiting for transfers between devices: 17.7 us -> 0.01 us
    all_to_all x0 -> x2, blocking collectives: none -> 55.1 us  [the longest x1 34.4 us: local(): recv = lax.all_to_all(send.reshape(TILES_Y, SLOT, CY), GY, 0, 0)]
    all_to_all x2 -> x0, starting transfers between devices: 37.6 us -> none  [the longest x1 31.7 us: local(): recv = lax.all_to_all(send.reshape(PLANES, LAYERS, CY), PLANE, 0, 0)]
    all_to_all x2 -> x0, waiting for transfers between devices: 15.4 us -> none  [the longest x1 11.3 us: local(): recv = lax.all_to_all(send.reshape(LAYERS, 2, CY), LAYER, 0, 0)]
    all_to_all x1, blocking collectives: 22.3 us -> 15.7 us  [local(): recv = lax.all_to_all(send, PLANE, 0, 0)]
    ppermute x4 -> x2, starting transfers between devices: 10 us -> 16.4 us  [shifted(): return lax.ppermute(value, axis, pairs)]
    ppermute x4 -> x2, waiting for transfers between devices: 2.33 us -> 0.01 us  [shifted(): return lax.ppermute(value, axis, pairs)]
    unnamed x23 -> x21, local copies, waits for them, and re-layouts: 2.25 us -> 3 us
    pallas_call x3 -> x2, Pallas kernels: 3.76 us -> 3.32 us  [the longest x1 2.33 us: local(): call(spread_kernel, [SMEM] * 3 + [VMEM] * 5, [shape(GROUPS, MEMBERS, WIDE...]
  transfers between devices with their start and end apart: 6 -> 2, of which waited for: 3 -> 0; matrix products, arithmetic and copies ran while one was open for 0% -> 0% of each run, Pallas kernels for 1% -> 0%
where the time goes in v3:
time: 122 us; the launch traced here: 121 us
  blocking collectives  84.6 us (69%)
  Pallas kernels  17.1 us (14%)
  starting transfers between devices  16.4 us (13%)
  local copies, waits for them, and re-layouts  3.05 us (2%)
    all_to_all x1, blocking collectives, local(): recv = lax.all_to_all(send.reshape(TILES_Y, SLOT, CY), GY, 0, 0)  34.4 us
    all_to_all x1, blocking collectives, local(): recv = lax.all_to_all(send.reshape(TILES_X, 1, CY), GX, 0, 0)  20.7 us
    ppermute x2, starting transfers between devices, shifted(): return lax.ppermute(value, axis, pairs)  16.4 us
    all_to_all x1, blocking collectives, local(): recv = lax.all_to_all(send, PLANE, 0, 0)  15.7 us
    all_to_all x1, blocking collectives, local(): recv = lax.all_to_all(send.reshape(LAYERS, 2, CY), LAYER, 0, 0)  13.8 us
    pallas_call x1, Pallas kernels, local(): call(assimilate_kernel, [SMEM] * 4 + [VMEM] * 7, [shape(MEMBERS * GROUPS...  12.9 us
    unnamed x21, local copies, waits for them, and re-layouts  3 us
  transfers between devices with their start and end apart: 2, of which 0 were waited for; matrix products, arithmetic and copies ran while one was open for 0% of the time, Pallas kernels for 0%

profile of v3, /device:TPU:1, one launch (start us, length us, event | category | flops | bytes accessed | tf_op | source)
XLA Modules:
  0.0 121.3 jit_solution(7439210727354559211)
XLA Ops:
  0.0 0.0 copy-start.9
  0.0 0.7 copy-done.9
  0.7 0.0 copy-start.3
  0.7 0.0 copy-start.2
  0.7 0.0 copy-start.1
  0.7 0.1 pad_add_fusion.place_ref
  0.8 0.0 copy-start.5
  0.8 0.0 copy-start.7
  0.8 0.6 copy-done.3
  1.4 0.0 copy-done.2
  1.4 0.0 copy-done.1
  1.4 0.0 copy-done.5
  1.4 0.0 copy-done.7
  1.5 0.0 copy-start
  1.5 0.9 copy-done
  2.4 2.3 %shard_map.100 = (f32[4,32,1024]{2,1,0:T(8,128)S(1)}, f32[640,128]{1,0:T(8,128)S(1)}) custom-call(s32[3]{0:T(128)S(1)} %copy-done.5, s32[2]{0:T(128)S(1)} %pad_add_fusion.place_ref, f32[2]{0:T(128)S(1)} %copy-done.7, f32[512,128]{1,0:T(8,128)S(1)} %bitcast.19, s32[3,512]{1,0:T(4,128)S(1)} %copy-done.1, s32[3,512]{1,0:T(4,128)S(1)} %copy-done.2, ...), custom_call_target="tpu_custom_call" | custom-call | tf_op jit(solution)/shard_map/pallas_call | solution.py:470
  4.8 34.4 %all_to_all.20 = f32[8,80,128]{2,1,0:T(8,128)S(1)} all-to-all(f32[8,80,128]{2,1,0:T(8,128)S(1)} %bitcast.18), channel_id=1, replica_groups=mesh['x'=4,'z_lo'=8,'core'=2,'z_hi'=2,'y'=4] {'z_hi','y'}, dimensions={0} | all-to-all | bytes 655360 | tf_op jit(solution)/shard_map/all_to_all | solution.py:475
  39.1 1.0 shard_map.101
  40.1 14.5 %collective-permute-start = (f32[4,32,256]{2,1,0:T(8,128)S(1)}, f32[4,32,256]{2,1,0:T(8,128)S(1)}, u32[]{:S(2)}, u32[]{:S(2)}) collective-permute-start(f32[4,32,256]{2,1,0:T(8,128)S(1)} %get-tuple-element.16), channel_id=1, source_target_pairs={{0,8},{8,16},{16,24},{24,32},{32,40},{40,48},{48,56},{56,64},{64,7... | collective-permute-start | bytes 393224 | tf_op jit(solution)/shard_map/ppermute | solution.py:450
  54.7 1.9 %collective-permute-start.1 = (f32[4,32,256]{2,1,0:T(8,128)S(1)}, f32[4,32,256]{2,1,0:T(8,128)S(1)}, u32[]{:S(2)}, u32[]{:S(2)}) collective-permute-start(f32[4,32,256]{2,1,0:T(8,128)S(1)} %get-tuple-element.17), channel_id=1, source_target_pairs={{0,504},{8,0},{16,8},{24,16},{32,24},{40,32},{48,40},{56,48},{64,5... | collective-permute-start | bytes 393224 | tf_op jit(solution)/shard_map/ppermute | solution.py:450
  56.6 20.7 %all_to_all.21 = f32[64,1,128]{2,1,0:T(1,128)S(1)} all-to-all(f32[64,1,128]{2,1,0:T(1,128)S(1)} %bitcast.23), channel_id=1, replica_groups=mesh['x'=4,'z_lo'=8,'core'=2,'z_hi'=2,'y'=4] {'x','z_lo','core'}, dimensions={0} | all-to-all | bytes 65536 | tf_op jit(solution)/shard_map/all_to_all | solution.py:488
  77.3 0.0 collective-permute-done.from_left_ref
  77.3 0.0 collective-permute-done.1.from_right_ref
  77.3 0.8 shard_map.102
  78.2 13.8 %all_to_all.22 = f32[16,2,128]{2,1,0:T(2,128)S(1)} all-to-all(f32[16,2,128]{2,1,0:T(2,128)S(1)} %bitcast.24), channel_id=1, replica_groups=mesh['x'=4,'z_lo'=8,'core'=2,'z_hi'=2,'y'=4] {'z_lo','z_hi'}, dimensions={0} | all-to-all | bytes 32768 | tf_op jit(solution)/shard_map/all_to_all | solution.py:494
  92.0 0.0 copy-start.4
  92.0 15.7 %all_to_all.23 = f32[32,32,128]{2,1,0:T(8,128)S(1)} all-to-all(f32[32,32,128]{2,1,0:T(8,128)S(1)} %broadcast_in_dim.8), channel_id=1, replica_groups=mesh['x'=4,'z_lo'=8,'core'=2,'z_hi'=2,'y'=4] {'x','core','y'}, dimensions={0} | all-to-all | bytes 1048576 | tf_op jit(solution)/shard_map/all_to_all | solution.py:496
  107.8 0.0 copy-start.6
  107.8 0.0 copy-start.8
  107.8 0.0 copy-done.4
  107.8 0.7 copy-done.6
  108.4 0.0 copy-done.8
  108.4 12.9 %shard_map.103 = f32[512,128]{1,0:T(8,128)} custom-call(s32[3]{0:T(128)S(1)} %copy-done.5, s32[2]{0:T(128)S(1)} %pad_add_fusion.place_ref, f32[2,2]{1,0:T(2,128)S(1)} %copy-done.6, f32[2]{0:T(128)S(1)} %copy-done.8, f32[4,32,512]{2,1,0:T(8,128)S(1)} %get-tuple-element.19.forecast_ref, f32[1024,128]{1,0:T(8,128)S(1)} %bitcast.16, s32[3,512]{1,0:T(4,128)S(1)} %copy-done.1, ...), custom_call_target="tpu_custom_call" | custom-call | tf_op jit(solution)/shard_map/pallas_call | solution.py:497
  (2 shorter events, 0.1 us)
Async XLA Ops:
  0.0 0.7 copy-start.9
  0.7 0.7 copy-start.3
  0.7 0.7 copy-start.2
  0.7 0.7 copy-start.1
  0.8 0.7 copy-start.5
  0.8 0.7 copy-start.7
  1.5 0.9 copy-start
  40.1 37.2 %collective-permute-start = (f32[4,32,256]{2,1,0:T(8,128)S(1)}, f32[4,32,256]{2,1,0:T(8,128)S(1)}, u32[]{:S(2)}, u32[]{:S(2)}) collective-permute-start(f32[4,32,256]{2,1,0:T(8,128)S(1)} %get-tuple-element.16), channel_id=1, source_target_pairs={{0,8},{8,16},{16,24},{24,32},{32,40},{40,48},{48,56},{56,64},{64,7... | collective-permute-start | bytes 393224 | tf_op jit(solution)/shard_map/ppermute | solution.py:450
  54.7 22.7 %collective-permute-start.1 = (f32[4,32,256]{2,1,0:T(8,128)S(1)}, f32[4,32,256]{2,1,0:T(8,128)S(1)}, u32[]{:S(2)}, u32[]{:S(2)}) collective-permute-start(f32[4,32,256]{2,1,0:T(8,128)S(1)} %get-tuple-element.17), channel_id=1, source_target_pairs={{0,504},{8,0},{16,8},{24,16},{32,24},{40,32},{48,40},{56,48},{64,5... | collective-permute-start | bytes 393224 | tf_op jit(solution)/shard_map/ppermute | solution.py:450
  92.0 15.8 %copy-start.4 = (f32[3,512]{1,0:T(4,128)S(1)}, f32[3,512]{1,0:T(4,128)}, u32[]{:S(2)}) copy-start(f32[3,512]{1,0:T(4,128)} %value_ref.1) | copy-start | bytes 18436
  107.8 0.7 copy-start.6
  107.8 0.7 copy-start.8

commit v4 on v2

--- a/solution.py
+++ b/solution.py
@@ -26,6 +26,10 @@
 PLANES = 32
 LAYERS = 16
 HALF = CY // 2
+RIM = 16
+VALUES = BATCHES * MEMBERS
+WIDE = (CX + 4) * CY
+SIDE = 2 * GROUPS * MEMBERS
 GX = ("x", "z_lo", "core")
 GY = ("z_hi", "y")
 PLANE = ("x", "core", "y")
@@ -64,12 +68,6 @@
     rest = value - high.astype(F32)
     middle = rest.astype(BF16)
     return high, middle, (rest - middle.astype(F32)).astype(BF16)
-
-
-def edges_kernel(ens_ref, low_ref, high_ref):
-    turned = ens_ref[...].T
-    low_ref[...] = turned[0:2]
-    high_ref[...] = turned[CY - 2 : CY]
 
 
 def advance(rows, courant_ref, keep):
@@ -102,43 +100,52 @@
     place_ref,
     courant_ref,
     ens_ref,
-    before_ref,
-    behind_ref,
     owner_ref,
     cell_ref,
     kind_ref,
     mask_ref,
     own_ref,
-    left_ref,
-    right_ref,
+    rim_ref,
+    first_ref,
+    second_ref,
     send_ref,
-    outer_ref,
 ):
     place_x = place_ref[0]
     place_y = place_ref[1]
-    rim = jnp.concatenate(
-        [behind_ref[...], jnp.zeros((CY - 4, OBS), F32), before_ref[...]], axis=0
-    )
-    outer_ref[...] = rim.T
     rows = {}
     for group in range(GROUPS):
         for x in range(CX):
-            rows[group, x] = jnp.concatenate(
-                [ens_ref[rows_of(group, x), :], outer_ref[rows_of(group, x), :]], axis=1
-            )
+            own = ens_ref[rows_of(group, x), :]
+            rows[group, x] = jnp.concatenate([own, jnp.zeros_like(own)], axis=1)
     lane = lax.broadcasted_iota(I32, (1, 2 * CY), 1)
     below = (lane >= 3 * CY // 2) & (place_y == 0)
     above = (lane >= CY) & (lane < 3 * CY // 2) & (place_y == TILES_Y - 1)
     keep = jnp.where(below | above, 0.0, 1.0).astype(F32)
     rows = advance(rows, courant_ref, keep)
     rows = advance(rows, courant_ref, None)
-    tile = {at: value[:, :CY] for at, value in rows.items()}
-    for group in range(GROUPS):
-        for x in range(CX):
+    lane = lax.broadcasted_iota(I32, (MEMBERS, CY), 1)
+    low = jnp.zeros((MEMBERS, CY), F32)
+    high = jnp.zeros((MEMBERS, CY), F32)
+    tile = {}
+    for (group, x), value in rows.items():
+        tile[group, x] = value[:, :CY]
+        if 0 <= x < CX:
             own_ref[group, :, x * CY : (x + 1) * CY] = tile[group, x]
+        edge = value[:, CY:]
+        at = group * 16 + (x + 2) * 2
+        there = (lane >> 1) == at // 2
+        low = jnp.where(there, pltpu.roll(edge, at + 2, 1), low)
+        high = jnp.where(there, pltpu.roll(edge, at, 1) if at else edge, high)
+    rim = low + pltpu.roll(high, HALF, 1)
+    rim_ref[...] = rim
+    first_ref[SIDE:] = rim
+    second_ref[SIDE:] = rim
+    even = (place_x & 1) == 0
+    for group in range(GROUPS):
         for x in range(2):
-            left_ref[group, :, x * CY : (x + 1) * CY] = tile[group, x - 2]
-            right_ref[group, :, x * CY : (x + 1) * CY] = tile[group, x + CX]
+            at = (group * 2 + x) * MEMBERS
+            first_ref[at : at + MEMBERS] = jnp.where(even, tile[group, CX + x], tile[group, x - 2])
+            second_ref[at : at + MEMBERS] = jnp.where(even, tile[group, x - 2], tile[group, CX + x])
     ground = jnp.concatenate(
         [
             jnp.concatenate([tile[2 * field, x] for x in range(-2, CX + 2)], axis=1)
@@ -147,6 +154,7 @@
         axis=0,
     )
     parts = jnp.concatenate(thirds(ground), axis=0)
+    rims = jnp.concatenate(thirds(rim), axis=0)
     blocks = []
     masks = []
     for turn in range(BATCHES):
@@ -157,21 +165,58 @@
         masks.append(mask_ref[pl.ds(batch, 1), :].astype(F32))
         at_x = ((owner >> 3) - place_x) * CX + (cell >> 7) + 2
         at_x = at_x & (NX - 1)
-        seen = (at_x < CX + 4) & ((owner & (TILES_Y - 1)) == place_y)
-        index = jnp.where(seen, at_x * CY + (cell & (CY - 1)), -1)
+        at_y = ((owner & (TILES_Y - 1)) - place_y) * CY + (cell & (CY - 1))
+        seen = at_x < CX + 4
+        index = jnp.where(seen & (at_y >= 0) & (at_y < CY), at_x * CY + at_y, -1)
+        corner = kind * 32 + at_x * 2
+        edge = jnp.where(seen & (at_y >= -2) & (at_y < 0), corner + at_y + 2, -1)
+        edge = jnp.where(seen & (at_y >= CY) & (at_y < CY + 2), corner + at_y - CY + HALF, edge)
         picked = jnp.zeros((parts.shape[0], OBS), F32)
-        for start in range(0, (CX + 4) * CY, CHUNK):
+        for start in range(0, WIDE, CHUNK):
             spot = lax.broadcasted_iota(I32, (CHUNK, OBS), 0) + start
             hot = jnp.where(spot == index, 1.0, 0.0).astype(BF16)
             picked = picked + mm(parts[:, start : start + CHUNK], hot)
         picked = picked[0:64] + picked[64:128] + picked[128:192]
-        blocks.append(jnp.where(kind == 0, picked[0:32], picked[32:64]))
+        spot = lax.broadcasted_iota(I32, (CY, OBS), 0)
+        found = mm(rims, jnp.where(spot == edge, 1.0, 0.0).astype(BF16))
+        found = found[0:32] + found[32:64] + found[64:96]
+        blocks.append(jnp.where(kind == 0, picked[0:32], picked[32:64]) + found)
     sub = lax.broadcasted_iota(I32, (MEMBERS, OBS), 0)
     blocks.append(jnp.where(sub == 0, masks[0], jnp.where(sub == 1, masks[1], 0.0)))
     send_ref[...] = jnp.concatenate(blocks, axis=0).T
 
 
-def collect_kernel(recv_ref, send_ref):
+def collect_kernel(
+    place_ref,
+    recv_ref,
+    own_ref,
+    rim_ref,
+    first_ref,
+    second_ref,
+    joined_ref,
+    third_ref,
+    fourth_ref,
+    send_ref,
+):
+    even = (place_ref[0] & 1) == 0
+    for group in range(GROUPS):
+        for x in range(CX):
+            at = (group * 2 + x % 2) * MEMBERS
+            part = slice(at, at + MEMBERS)
+            near = first_ref[part], second_ref[part]
+            other = jnp.where(even, near[1], near[0]) if x < 2 else jnp.where(even, near[0], near[1])
+            cells = slice(x * CY, (x + 1) * CY)
+            joined_ref[group, :, cells] = own_ref[group, :, cells] + other
+    lane = lax.broadcasted_iota(I32, (MEMBERS, CY), 1)
+    from_left = pltpu.roll(jnp.where(even, second_ref[SIDE:], first_ref[SIDE:]), CY - 8, 1)
+    from_right = pltpu.roll(jnp.where(even, first_ref[SIDE:], second_ref[SIDE:]), 8, 1)
+    rim = rim_ref[...] + jnp.where((lane & 15) < 8, from_left, from_right)
+    lane = lax.broadcasted_iota(I32, (RIM, CY), 1)
+    low = jnp.where(lane < HALF, rim[:RIM], pltpu.roll(rim[RIM:], HALF, 1))
+    high = jnp.where(lane < HALF, pltpu.roll(rim[:RIM], HALF, 1), rim[RIM:])
+    even = (place_ref[1] & 1) == 0
+    third_ref[...] = jnp.where(even, high, low)
+    fourth_ref[...] = jnp.where(even, low, high)
     lane = lax.broadcasted_iota(I32, (LAYERS, CY), 1)
     total = jnp.zeros((LAYERS, CY), F32)
     marks = jnp.zeros((LAYERS, CY), F32)
@@ -189,9 +234,9 @@
     order_ref,
     place_ref,
     relay_ref,
-    own_ref,
-    from_left_ref,
-    from_right_ref,
+    joined_ref,
+    third_ref,
+    fourth_ref,
     recv_ref,
     forecast_ref,
     send_ref,
@@ -200,15 +245,21 @@
     lane = lax.broadcasted_iota(I32, (1, CY), 1)
     top = jnp.sum(recv_ref[pl.ds(0, LAYERS, stride=2), :], axis=0, keepdims=True)
     top = jnp.where(lane < BATCHES * MEMBERS, top, 0.0)
-    for group in range(GROUPS):
-        own = own_ref[group]
-        value = jnp.concatenate(
-            [
-                own[:, : 2 * CY] + from_left_ref[group],
-                own[:, 2 * CY :] + from_right_ref[group],
-            ],
-            axis=1,
-        )
+    even = (place_ref[1] & 1) == 0
+    below = jnp.where(even, fourth_ref[...], third_ref[...])
+    above = jnp.where(even, third_ref[...], fourth_ref[...])
+    below = jnp.concatenate([below, pltpu.roll(below, HALF, 1)], axis=0)
+    above = jnp.concatenate([above, pltpu.roll(above, HALF, 1)], axis=0)
+    wide = lax.broadcasted_iota(I32, (MEMBERS, CY), 1)
+    for group in range(GROUPS):
+        pieces = []
+        for x in range(CX):
+            at = group * 16 + (x + 2) * 2
+            piece = joined_ref[group, :, x * CY : (x + 1) * CY]
+            piece = piece + jnp.where(wide < 2, pltpu.roll(below, CY - at, 1), 0.0)
+            piece = piece + jnp.where(wide >= CY - 2, pltpu.roll(above, CY - 2 - at, 1), 0.0)
+            pieces.append(piece)
+        value = jnp.concatenate(pieces, axis=1)
         forecast_ref[group] = value
         centre = jnp.sum(value, axis=0, keepdims=True) * (1.0 / MEMBERS)
         deviation = value - centre
@@ -401,13 +452,13 @@
     return jax.ShapeDtypeStruct(dims, F32)
 
 
-def shifted(value, axis, step, periodic):
+def swapped(value, axis, step, periodic):
     count = lax.axis_size(axis)
-    pairs = [
-        (source, (source + step) % count)
-        for source in range(count)
-        if periodic or 0 <= source + step < count
-    ]
+    pairs = []
+    for source in range(count):
+        target = source + (step if source % 2 == 0 else -step)
+        if periodic or 0 <= target < count:
+            pairs.append((source, target % count))
     return lax.ppermute(value, axis, pairs)
 
 
@@ -429,41 +480,38 @@
     place = jnp.stack([place_x, place_y, relay]).astype(I32)
     ens = ensemble.reshape(MEMBERS * GROUPS * CX, CY)
     mask = tile_mask.reshape(BATCHES, OBS)
-    low, high = call(edges_kernel, [VMEM], [shape(2, OBS)] * 2)(ens)
-    before = shifted(high, GY, 1, False)
-    behind = shifted(low, GY, -1, False)
-    own, left, right, send = call(
+    own, rim, first, second, send = call(
         spread_kernel,
-        [SMEM] * 3 + [VMEM] * 7,
+        [SMEM] * 3 + [VMEM] * 5,
         [
             shape(GROUPS, MEMBERS, CELLS),
-            shape(GROUPS, MEMBERS, 2 * CY),
-            shape(GROUPS, MEMBERS, 2 * CY),
+            shape(MEMBERS, CY),
+            shape(SIDE + MEMBERS, CY),
+            shape(SIDE + MEMBERS, CY),
             shape(OBS, CY),
         ],
-        [pltpu.VMEM((MEMBERS * GROUPS * CX, CY), F32)],
-    )(
-        batch_order,
-        place,
-        courant,
-        ens,
-        before,
-        behind,
-        obs_owner,
-        obs_cell,
-        obs_kind,
-        mask,
-    )
-    from_left = shifted(right, GX, 1, True)
-    from_right = shifted(left, GX, -1, True)
+    )(batch_order, place, courant, ens, obs_owner, obs_cell, obs_kind, mask)
     recv = lax.all_to_all(send.reshape(PLANES, LAYERS, CY), PLANE, 0, 0)
-    send = call(collect_kernel, [VMEM], [shape(2 * LAYERS, CY)])(recv.reshape(TILES, CY))
+    first = swapped(first, GX, 1, True)
+    second = swapped(second, GX, -1, True)
+    joined, third, fourth, send = call(
+        collect_kernel,
+        [SMEM] + [VMEM] * 5,
+        [
+            shape(GROUPS, MEMBERS, CELLS),
+            shape(RIM, CY),
+            shape(RIM, CY),
+            shape(2 * LAYERS, CY),
+        ],
+    )(place, recv.reshape(TILES, CY), own, rim, first, second)
+    third = swapped(third, GY, 1, False)
+    fourth = swapped(fourth, GY, -1, False)
     recv = lax.all_to_all(send.reshape(LAYERS, 2, CY), LAYER, 0, 0)
     forecast, send = call(
         merge_kernel,
         [SMEM] * 3 + [VMEM] * 4,
         [shape(GROUPS, MEMBERS, CELLS), shape(2 * LAYERS, CY)],
-    )(batch_order, place, obs_owner, own, from_left, from_right, recv.reshape(2 * LAYERS, CY))
+    )(batch_order, place, obs_owner, joined, third, fourth, recv.reshape(2 * LAYERS, CY))
     recv = lax.all_to_all(send.reshape(LAYERS, 2, CY), LAYER, 0, 0)
     send = jnp.broadcast_to(recv.reshape(1, 2 * LAYERS, CY), (PLANES, 2 * LAYERS, CY))
     recv = lax.all_to_all(send, PLANE, 0, 0)

time: 122 us -> 122 us (level)
  blocking collectives: 36.1 us -> 51.2 us
  starting transfers between devices: 47.6 us -> 36.3 us
  waiting for transfers between devices: 17.7 us -> 12.1 us
    all_to_all x1, starting transfers between devices: 31.7 us -> 10.4 us  [local(): recv = lax.all_to_all(send.reshape(PLANES, LAYERS, CY), PLANE, 0, 0)]
    all_to_all x1, blocking collectives: 13.8 us -> 29.9 us  [local(): recv = lax.all_to_all(send.reshape(LAYERS, 2, CY), LAYER, 0, 0)]
    all_to_all x1, starting transfers between devices: 5.85 us -> 17.6 us  [local(): recv = lax.all_to_all(send.reshape(LAYERS, 2, CY), LAYER, 0, 0)]
    all_to_all x1, waiting for transfers between devices: 11.3 us -> 6.9 us  [local(): recv = lax.all_to_all(send.reshape(LAYERS, 2, CY), LAYER, 0, 0)]
    all_to_all x1, waiting for transfers between devices: 4.1 us -> 0.01 us  [local(): recv = lax.all_to_all(send.reshape(PLANES, LAYERS, CY), PLANE, 0, 0)]
    ppermute x4, waiting for transfers between devices: 2.33 us -> 5.18 us  [swapped(): return lax.ppermute(value, axis, pairs)]
    ppermute x4, starting transfers between devices: 10 us -> 8.24 us  [swapped(): return lax.ppermute(value, axis, pairs)]
    unnamed x23 -> x21, local copies, waits for them, and re-layouts: 2.25 us -> 3 us
  transfers between devices with their start and end apart: 6 -> 6, of which waited for: 3 -> 3; matrix products, arithmetic and copies ran while one was open for 0% -> 0% of each run, Pallas kernels for 1% -> 0%
where the time goes in v4:
time: 122 us; the launch traced here: 121 us
  blocking collectives  51.2 us (42%)
  starting transfers between devices  36.3 us (30%)
  Pallas kernels  18.5 us (15%)
  waiting for transfers between devices  12.1 us (10%)
  local copies, waits for them, and re-layouts  3.05 us (2%)
    all_to_all x1, blocking collectives, local(): recv = lax.all_to_all(send.reshape(LAYERS, 2, CY), LAYER, 0, 0)  29.9 us
    all_to_all x1, blocking collectives, local(): recv = lax.all_to_all(send, PLANE, 0, 0)  21.3 us
    all_to_all x1, starting transfers between devices, local(): recv = lax.all_to_all(send.reshape(LAYERS, 2, CY), LAYER, 0, 0)  17.6 us
    pallas_call x1, Pallas kernels, local(): call(assimilate_kernel, [SMEM] * 4 + [VMEM] * 7, [shape(MEMBERS * GROUPS...  12.9 us
    all_to_all x1, starting transfers between devices, local(): recv = lax.all_to_all(send.reshape(PLANES, LAYERS, CY), PLANE, 0, 0)  10.4 us
    ppermute x4, starting transfers between devices, swapped(): return lax.ppermute(value, axis, pairs)  8.24 us
    all_to_all x1, waiting for transfers between devices, local(): recv = lax.all_to_all(send.reshape(LAYERS, 2, CY), LAYER, 0, 0)  6.9 us
    ppermute x4, waiting for transfers between devices, swapped(): return lax.ppermute(value, axis, pairs)  5.18 us
  transfers between devices with their start and end apart: 6, of which 3 were waited for; matrix products, arithmetic and copies ran while one was open for 0% of the time, Pallas kernels for 0%

profile of v4, /device:TPU:1, one launch (start us, length us, event | category | flops | bytes accessed | tf_op | source)
XLA Modules:
  0.0 121.3 jit_solution(12083168304358029572)
XLA Ops:
  0.0 0.0 copy-start.9
  0.0 0.7 copy-done.9
  0.7 0.0 copy-start.2
  0.7 0.0 copy-start.3
  0.7 0.0 copy-start.1
  0.7 0.1 pad_add_fusion.place_ref
  0.8 0.0 copy-start.5
  0.8 0.0 copy-start.7
  0.8 0.6 copy-done.2
  1.4 0.0 copy-done.3
  1.4 0.0 copy-done.1
  1.4 0.0 copy-done.5
  1.5 0.0 copy-done.7
  1.5 0.0 copy-start
  1.5 0.9 copy-done
  2.4 3.0 %shard_map.100 = (f32[4,32,512]{2,1,0:T(8,128)S(1)}, f32[32,128]{1,0:T(8,128)S(1)}, f32[288,128]{1,0:T(8,128)S(1)}, f32[288,128]{1,0:T(8,128)S(1)}, f32[512,128]{1,0:T(8,128)}) custom-call(s32[3]{0:T(128)S(1)} %copy-done.5, s32[3]{0:T(128)S(1)} %pad_add_fusion.place_ref, f32[2]{0:T(128)S(1)} %copy-done.7, f32[512,128]{1,0:T(8,128)S(1)} %bitcast.17, ...), custom_call_target="tpu_custom_call" | custom-call | tf_op jit(solution)/shard_map/pallas_call | solution.py:483
  5.5 10.4 %all-to-all-start = ((f32[32,16,128]{2,1,0:T(8,128)}), f32[32,16,128]{2,1,0:T(8,128)S(1)}, u32[]{:S(2)}, u32[]{:S(2)}) async-start(f32[32,16,128]{2,1,0:T(8,128)} %bitcast.4), calls=%async_computation | async-start | bytes 524288 | tf_op jit(solution)/shard_map/all_to_all | solution.py:494
  15.9 2.2 %collective-permute-start = (f32[288,128]{1,0:T(8,128)S(1)}, f32[288,128]{1,0:T(8,128)S(1)}, u32[]{:S(2)}, u32[]{:S(2)}) collective-permute-start(f32[288,128]{1,0:T(8,128)S(1)} %get-tuple-element.19), channel_id=1, source_target_pairs={{0,8},{8,0},{16,24},{24,16},{32,40},{40,32},{48,56},{56,48},{64,72... | collective-permute-start | bytes 442376 | tf_op jit(solution)/shard_map/ppermute | solution.py:462
  18.1 1.9 %collective-permute-start.1 = (f32[288,128]{1,0:T(8,128)S(1)}, f32[288,128]{1,0:T(8,128)S(1)}, u32[]{:S(2)}, u32[]{:S(2)}) collective-permute-start(f32[288,128]{1,0:T(8,128)S(1)} %get-tuple-element.20), channel_id=1, source_target_pairs={{0,504},{8,16},{16,8},{24,32},{32,24},{40,48},{48,40},{56,64},{64,... | collective-permute-start | bytes 442376 | tf_op jit(solution)/shard_map/ppermute | solution.py:462
  20.1 0.0 collective-permute-done.first_ref
  20.1 4.8 %collective-permute-done.1.second_ref = f32[288,128]{1,0:T(8,128)S(1)} collective-permute-done((f32[288,128]{1,0:T(8,128)S(1)}, f32[288,128]{1,0:T(8,128)S(1)}, u32[]{:S(2)}, u32[]{:S(2)}) %collective-permute-start.1) | collective-permute-done | bytes 147488 | tf_op jit(solution)/shard_map/ppermute | solution.py:462
  24.9 0.0 all-to-all-done
  24.9 1.5 %shard_map.101 = (f32[4,32,512]{2,1,0:T(8,128)S(1)}, f32[16,128]{1,0:T(8,128)S(1)}, f32[16,128]{1,0:T(8,128)S(1)}, f32[32,128]{1,0:T(8,128)}) custom-call(s32[3]{0:T(128)S(1)} %pad_add_fusion.place_ref, f32[512,128]{1,0:T(8,128)S(1)} %bitcast.16, f32[4,32,512]{2,1,0:T(8,128)S(1)} %get-tuple-element.17.own_ref, f32[32,128]{1,0:T(8,128)S(1)} %get-tuple-element.18.rim_ref, ...), custom_call_target="tpu_custom_call" | custom-call | tf_op jit(solution)/shard_map/pallas_call | solution.py:497
  26.3 17.6 %all-to-all-start.1 = ((f32[16,2,128]{2,1,0:T(2,128)}), f32[16,2,128]{2,1,0:T(2,128)S(1)}, u32[]{:S(2)}, u32[]{:S(2)}) async-start(f32[16,2,128]{2,1,0:T(2,128)} %bitcast.6), calls=%async_computation.1 | async-start | bytes 32768 | tf_op jit(solution)/shard_map/all_to_all | solution.py:509
  44.0 3.4 %collective-permute-start.2 = (f32[16,128]{1,0:T(8,128)S(1)}, f32[16,128]{1,0:T(8,128)S(1)}, u32[]{:S(2)}, u32[]{:S(2)}) collective-permute-start(f32[16,128]{1,0:T(8,128)S(1)} %get-tuple-element.22), channel_id=1, source_target_pairs={{0,1},{1,0},{2,3},{3,2},{4,5},{5,4},{6,7},{7,6},{8,9},{9,8},{10,11... | collective-permute-start | bytes 24584 | tf_op jit(solution)/shard_map/ppermute | solution.py:462
  47.4 0.7 collective-permute-start.3
  48.1 0.4 collective-permute-done.2.third_ref
  48.4 0.0 collective-permute-done.3.fourth_ref
  48.4 6.9 %all-to-all-done.1 = f32[16,2,128]{2,1,0:T(2,128)S(1)} async-done(((f32[16,2,128]{2,1,0:T(2,128)}), f32[16,2,128]{2,1,0:T(2,128)S(1)}, u32[]{:S(2)}, u32[]{:S(2)}) %all-to-all-start.1) | async-done | bytes 16416 | tf_op jit(solution)/shard_map/all_to_all | solution.py:509
  55.4 1.1 shard_map.102
  56.4 29.9 %all_to_all.20 = f32[16,2,128]{2,1,0:T(2,128)S(1)} all-to-all(f32[16,2,128]{2,1,0:T(2,128)S(1)} %bitcast.21), channel_id=1, replica_groups=mesh['x'=4,'z_lo'=8,'core'=2,'z_hi'=2,'y'=4] {'z_lo','z_hi'}, dimensions={0} | all-to-all | bytes 32768 | tf_op jit(solution)/shard_map/all_to_all | solution.py:515
  86.4 0.0 copy-start.4
  86.4 21.3 %all_to_all.21 = f32[32,32,128]{2,1,0:T(8,128)S(1)} all-to-all(f32[32,32,128]{2,1,0:T(8,128)S(1)} %broadcast_in_dim.8), channel_id=1, replica_groups=mesh['x'=4,'z_lo'=8,'core'=2,'z_hi'=2,'y'=4] {'x','core','y'}, dimensions={0} | all-to-all | bytes 1048576 | tf_op jit(solution)/shard_map/all_to_all | solution.py:517
  107.7 0.0 copy-start.6
  107.7 0.0 copy-start.8
  107.7 0.0 copy-done.4
  107.7 0.7 copy-done.6
  108.4 0.0 copy-done.8
  108.4 12.9 %shard_map.103 = f32[512,128]{1,0:T(8,128)} custom-call(s32[3]{0:T(128)S(1)} %copy-done.5, s32[3]{0:T(128)S(1)} %pad_add_fusion.place_ref, f32[2,2]{1,0:T(2,128)S(1)} %copy-done.6, f32[2]{0:T(128)S(1)} %copy-done.8, f32[4,32,512]{2,1,0:T(8,128)S(1)} %get-tuple-element.25.forecast_ref, f32[1024,128]{1,0:T(8,128)S(1)} %bitcast.15, s32[3,512]{1,0:T(4,128)S(1)} %copy-done.1, ...), custom_call_target="tpu_custom_call" | custom-call | tf_op jit(solution)/shard_map/pallas_call | solution.py:518
  (2 shorter events, 0.1 us)
Async XLA Ops:
  0.0 0.7 copy-start.9
  0.7 0.7 copy-start.2
  0.7 0.7 copy-start.3
  0.7 0.7 copy-start.1
  0.8 0.7 copy-start.5
  0.8 0.7 copy-start.7
  1.5 0.9 copy-start
  5.5 19.4 %all-to-all-start = ((f32[32,16,128]{2,1,0:T(8,128)}), f32[32,16,128]{2,1,0:T(8,128)S(1)}, u32[]{:S(2)}, u32[]{:S(2)}) async-start(f32[32,16,128]{2,1,0:T(8,128)} %bitcast.4), calls=%async_computation | async-start | bytes 524288 | tf_op jit(solution)/shard_map/all_to_all | solution.py:494
  15.9 4.2 %collective-permute-start = (f32[288,128]{1,0:T(8,128)S(1)}, f32[288,128]{1,0:T(8,128)S(1)}, u32[]{:S(2)}, u32[]{:S(2)}) collective-permute-start(f32[288,128]{1,0:T(8,128)S(1)} %get-tuple-element.19), channel_id=1, source_target_pairs={{0,8},{8,0},{16,24},{24,16},{32,40},{40,32},{48,56},{56,48},{64,72... | collective-permute-start | bytes 442376 | tf_op jit(solution)/shard_map/ppermute | solution.py:462
  18.1 6.8 %collective-permute-start.1 = (f32[288,128]{1,0:T(8,128)S(1)}, f32[288,128]{1,0:T(8,128)S(1)}, u32[]{:S(2)}, u32[]{:S(2)}) collective-permute-start(f32[288,128]{1,0:T(8,128)S(1)} %get-tuple-element.20), channel_id=1, source_target_pairs={{0,504},{8,16},{16,8},{24,32},{32,24},{40,48},{48,40},{56,64},{64,... | collective-permute-start | bytes 442376 | tf_op jit(solution)/shard_map/ppermute | solution.py:462
  26.3 29.0 %all-to-all-start.1 = ((f32[16,2,128]{2,1,0:T(2,128)}), f32[16,2,128]{2,1,0:T(2,128)S(1)}, u32[]{:S(2)}, u32[]{:S(2)}) async-start(f32[16,2,128]{2,1,0:T(2,128)} %bitcast.6), calls=%async_computation.1 | async-start | bytes 32768 | tf_op jit(solution)/shard_map/all_to_all | solution.py:509
  44.0 4.5 %collective-permute-start.2 = (f32[16,128]{1,0:T(8,128)S(1)}, f32[16,128]{1,0:T(8,128)S(1)}, u32[]{:S(2)}, u32[]{:S(2)}) collective-permute-start(f32[16,128]{1,0:T(8,128)S(1)} %get-tuple-element.22), channel_id=1, source_target_pairs={{0,1},{1,0},{2,3},{3,2},{4,5},{5,4},{6,7},{7,6},{8,9},{9,8},{10,11... | collective-permute-start | bytes 24584 | tf_op jit(solution)/shard_map/ppermute | solution.py:462
  47.4 1.0 collective-permute-start.3
  86.4 21.3 %copy-start.4 = (f32[3,512]{1,0:T(4,128)S(1)}, f32[3,512]{1,0:T(4,128)}, u32[]{:S(2)}) copy-start(f32[3,512]{1,0:T(4,128)} %value_ref.1) | copy-start | bytes 18436
  107.7 0.7 copy-start.6
  107.7 0.7 copy-start.8

commit v5 on v4

--- a/solution.py
+++ b/solution.py
@@ -28,6 +28,8 @@
 HALF = CY // 2
 RIM = 16
 VALUES = BATCHES * MEMBERS
+PLANE_ROWS = LAYERS + RIM
+LAYER_ROWS = 24
 WIDE = (CX + 4) * CY
 SIDE = 2 * GROUPS * MEMBERS
 GX = ("x", "z_lo", "core")
@@ -56,6 +58,10 @@
 
 def mm(a, b):
     return lax.dot_general(a, b, (((1,), (0,)), ((), ())), preferred_element_type=F32)
+
+
+def flag(condition):
+    return jnp.where(condition, 1.0, 0.0).astype(F32)
 
 
 def halves(value):
@@ -105,7 +111,6 @@
     kind_ref,
     mask_ref,
     own_ref,
-    rim_ref,
     first_ref,
     second_ref,
     send_ref,
@@ -137,9 +142,6 @@
         low = jnp.where(there, pltpu.roll(edge, at + 2, 1), low)
         high = jnp.where(there, pltpu.roll(edge, at, 1) if at else edge, high)
     rim = low + pltpu.roll(high, HALF, 1)
-    rim_ref[...] = rim
-    first_ref[SIDE:] = rim
-    second_ref[SIDE:] = rim
     even = (place_x & 1) == 0
     for group in range(GROUPS):
         for x in range(2):
@@ -183,79 +185,109 @@
         blocks.append(jnp.where(kind == 0, picked[0:32], picked[32:64]) + found)
     sub = lax.broadcasted_iota(I32, (MEMBERS, OBS), 0)
     blocks.append(jnp.where(sub == 0, masks[0], jnp.where(sub == 1, masks[1], 0.0)))
-    send_ref[...] = jnp.concatenate(blocks, axis=0).T
-
-
-def collect_kernel(
-    place_ref,
-    recv_ref,
-    own_ref,
-    rim_ref,
-    first_ref,
-    second_ref,
-    joined_ref,
-    third_ref,
-    fourth_ref,
-    send_ref,
-):
-    even = (place_ref[0] & 1) == 0
-    for group in range(GROUPS):
-        for x in range(CX):
-            at = (group * 2 + x % 2) * MEMBERS
-            part = slice(at, at + MEMBERS)
-            near = first_ref[part], second_ref[part]
-            other = jnp.where(even, near[1], near[0]) if x < 2 else jnp.where(even, near[0], near[1])
-            cells = slice(x * CY, (x + 1) * CY)
-            joined_ref[group, :, cells] = own_ref[group, :, cells] + other
-    lane = lax.broadcasted_iota(I32, (MEMBERS, CY), 1)
-    from_left = pltpu.roll(jnp.where(even, second_ref[SIDE:], first_ref[SIDE:]), CY - 8, 1)
-    from_right = pltpu.roll(jnp.where(even, first_ref[SIDE:], second_ref[SIDE:]), 8, 1)
-    rim = rim_ref[...] + jnp.where((lane & 15) < 8, from_left, from_right)
+    turned = jnp.concatenate(blocks, axis=0).T
     lane = lax.broadcasted_iota(I32, (RIM, CY), 1)
-    low = jnp.where(lane < HALF, rim[:RIM], pltpu.roll(rim[RIM:], HALF, 1))
-    high = jnp.where(lane < HALF, pltpu.roll(rim[:RIM], HALF, 1), rim[RIM:])
-    even = (place_ref[1] & 1) == 0
-    third_ref[...] = jnp.where(even, high, low)
-    fourth_ref[...] = jnp.where(even, low, high)
+    low = jnp.where(lane < HALF, low[:RIM], pltpu.roll(low[RIM:], HALF, 1))
+    high = jnp.where(lane < HALF, high[:RIM], pltpu.roll(high[RIM:], HALF, 1))
+    y = place_y & 3
+    for plane in range(PLANES):
+        at = plane * PLANE_ROWS
+        send_ref[at : at + LAYERS, :] = turned[plane * LAYERS : (plane + 1) * LAYERS]
+        up = flag((y + 1) & 3 == plane & 3)
+        down = flag((y + 3) & 3 == plane & 3)
+        send_ref[at + LAYERS : at + PLANE_ROWS, :] = up * high + down * low
+
+
+def collect_kernel(place_ref, recv_ref, send_ref):
+    place_x = place_ref[0]
+    place_y = place_ref[1]
+    x, z_lo, core = place_x >> 4, (place_x >> 1) & 7, place_x & 1
+    z_hi, y = place_y >> 2, place_y & 3
     lane = lax.broadcasted_iota(I32, (LAYERS, CY), 1)
     total = jnp.zeros((LAYERS, CY), F32)
     marks = jnp.zeros((LAYERS, CY), F32)
     for plane in range(PLANES):
-        rows = recv_ref[plane * LAYERS : (plane + 1) * LAYERS, :]
+        rows = recv_ref[plane * PLANE_ROWS : plane * PLANE_ROWS + LAYERS, :]
         total = total + rows
         for turn in range(2):
-            at = BATCHES * MEMBERS + turn
+            at = VALUES + turn
             marks = jnp.where(lane == turn * PLANES + plane, rows[:, at : at + 1], marks)
-    send_ref[pl.ds(0, LAYERS, stride=2), :] = total
-    send_ref[pl.ds(1, LAYERS, stride=2), :] = marks
+
+    spot = lane & 15
+    hop = jnp.where(core == 0, z_lo == 7, z_lo == 0)
+    side = jnp.where(hop, (x + jnp.where(core == 0, 3, 1)) & 3, x)
+    first = flag(core == 0)
+    second = 1.0 - first
+
+    def rim(column, other, step):
+        plane = (column * 2 + other) * 4 + ((y + step) & 3)
+        start = pl.multiple_of(plane * PLANE_ROWS + LAYERS, RIM)
+        return recv_ref[pl.ds(start, RIM), :]
+
+    def from_left(block):
+        return jnp.where((spot >= 4) & (spot < 8), pltpu.roll(block, CY - 8, 1), 0.0)
+
+    def from_right(block):
+        return jnp.where((spot >= 8) & (spot < 12), pltpu.roll(block, 8, 1), 0.0)
+
+    here, there = [], []
+    for step in (3, 1):
+        mine = jnp.where((spot >= 4) & (spot < 12), rim(x, core, step), 0.0)
+        twin = rim(x, 1 - core, step)
+        far = rim(side, 1 - core, step)
+        block = mine + first * from_right(twin) + second * from_left(twin)
+        other = first * from_left(far) + second * from_right(far)
+        here.append(pltpu.roll(block, 8, 1) if step == 1 else block)
+        there.append(pltpu.roll(other, 8, 1) if step == 1 else other)
+    target = jnp.where(core == 0, z_lo + 1, z_lo + 7) & 7
+    below = jnp.where(y > 0, z_hi, jnp.where(z_hi == 0, 1, -1))
+    above = jnp.where(y < 3, z_hi, jnp.where(z_hi == 1, 0, -1))
+    for layer in range(LAYERS):
+        lower, higher = flag(below == layer % 2), flag(above == layer % 2)
+        same, next_to = flag(z_lo == layer // 2), flag(target == layer // 2)
+        at = layer * LAYER_ROWS
+        send_ref[at : at + RIM, :] = same * (lower * here[0] + higher * here[1]) + next_to * (
+            lower * there[0] + higher * there[1]
+        )
+        pair = jnp.concatenate([total[layer : layer + 1], marks[layer : layer + 1]], axis=0)
+        send_ref[at + RIM : at + RIM + 2, :] = pair
+        send_ref[at + RIM + 2 : at + LAYER_ROWS, :] = jnp.zeros((LAYER_ROWS - RIM - 2, CY), F32)
 
 
 def merge_kernel(
     order_ref,
     place_ref,
     relay_ref,
-    joined_ref,
-    third_ref,
-    fourth_ref,
+    own_ref,
+    first_ref,
+    second_ref,
     recv_ref,
     forecast_ref,
     send_ref,
 ):
     relay = place_ref[2]
     lane = lax.broadcasted_iota(I32, (1, CY), 1)
-    top = jnp.sum(recv_ref[pl.ds(0, LAYERS, stride=2), :], axis=0, keepdims=True)
+    sums = recv_ref[pl.ds(RIM, LAYERS, stride=LAYER_ROWS), :]
+    marks = recv_ref[pl.ds(RIM + 1, LAYERS, stride=LAYER_ROWS), :]
+    top = jnp.sum(sums, axis=0, keepdims=True)
     top = jnp.where(lane < BATCHES * MEMBERS, top, 0.0)
-    even = (place_ref[1] & 1) == 0
-    below = jnp.where(even, fourth_ref[...], third_ref[...])
-    above = jnp.where(even, third_ref[...], fourth_ref[...])
+    below = recv_ref[0:RIM, :]
+    for layer in range(1, LAYERS):
+        below = below + recv_ref[layer * LAYER_ROWS : layer * LAYER_ROWS + RIM, :]
+    above = pltpu.roll(below, CY - 8, 1)
     below = jnp.concatenate([below, pltpu.roll(below, HALF, 1)], axis=0)
     above = jnp.concatenate([above, pltpu.roll(above, HALF, 1)], axis=0)
+    even = (place_ref[0] & 1) == 0
     wide = lax.broadcasted_iota(I32, (MEMBERS, CY), 1)
     for group in range(GROUPS):
         pieces = []
         for x in range(CX):
             at = group * 16 + (x + 2) * 2
-            piece = joined_ref[group, :, x * CY : (x + 1) * CY]
+            part = (group * 2 + x % 2) * MEMBERS
+            part = slice(part, part + MEMBERS)
+            near = first_ref[part], second_ref[part]
+            other = jnp.where(even, near[1], near[0]) if x < 2 else jnp.where(even, near[0], near[1])
+            piece = own_ref[group, :, x * CY : (x + 1) * CY] + other
             piece = piece + jnp.where(wide < 2, pltpu.roll(below, CY - at, 1), 0.0)
             piece = piece + jnp.where(wide >= CY - 2, pltpu.roll(above, CY - 2 - at, 1), 0.0)
             pieces.append(piece)
@@ -266,7 +298,6 @@
         total = jnp.sum(jnp.sum(deviation * deviation, axis=0, keepdims=True), axis=1, keepdims=True)
         top = jnp.where(lane == BATCHES * MEMBERS + group, total, top)
 
-    marks = recv_ref[pl.ds(1, LAYERS, stride=2), :]
     lanes = lax.broadcasted_iota(I32, (LAYERS, CY), 1)
     subs = lax.broadcasted_iota(I32, (LAYERS, CY), 0)
     tile_x = ((lanes >> 3) & 3) * 16 + (subs >> 1) * 2 + ((lanes >> 2) & 1)
@@ -480,38 +511,29 @@
     place = jnp.stack([place_x, place_y, relay]).astype(I32)
     ens = ensemble.reshape(MEMBERS * GROUPS * CX, CY)
     mask = tile_mask.reshape(BATCHES, OBS)
-    own, rim, first, second, send = call(
+    own, first, second, send = call(
         spread_kernel,
         [SMEM] * 3 + [VMEM] * 5,
         [
             shape(GROUPS, MEMBERS, CELLS),
-            shape(MEMBERS, CY),
-            shape(SIDE + MEMBERS, CY),
-            shape(SIDE + MEMBERS, CY),
-            shape(OBS, CY),
+            shape(SIDE, CY),
+            shape(SIDE, CY),
+            shape(PLANES * PLANE_ROWS, CY),
         ],
     )(batch_order, place, courant, ens, obs_owner, obs_cell, obs_kind, mask)
-    recv = lax.all_to_all(send.reshape(PLANES, LAYERS, CY), PLANE, 0, 0)
+    recv = lax.all_to_all(send.reshape(PLANES, PLANE_ROWS, CY), PLANE, 0, 0)
     first = swapped(first, GX, 1, True)
     second = swapped(second, GX, -1, True)
-    joined, third, fourth, send = call(
-        collect_kernel,
-        [SMEM] + [VMEM] * 5,
-        [
-            shape(GROUPS, MEMBERS, CELLS),
-            shape(RIM, CY),
-            shape(RIM, CY),
-            shape(2 * LAYERS, CY),
-        ],
-    )(place, recv.reshape(TILES, CY), own, rim, first, second)
-    third = swapped(third, GY, 1, False)
-    fourth = swapped(fourth, GY, -1, False)
-    recv = lax.all_to_all(send.reshape(LAYERS, 2, CY), LAYER, 0, 0)
+    send = call(collect_kernel, [SMEM, VMEM], [shape(LAYERS * LAYER_ROWS, CY)])(
+        place, recv.reshape(PLANES * PLANE_ROWS, CY)
+    )
+    recv = lax.all_to_all(send.reshape(LAYERS, LAYER_ROWS, CY), LAYER, 0, 0)
+    recv = recv.reshape(LAYERS * LAYER_ROWS, CY)
     forecast, send = call(
         merge_kernel,
         [SMEM] * 3 + [VMEM] * 4,
         [shape(GROUPS, MEMBERS, CELLS), shape(2 * LAYERS, CY)],
-    )(batch_order, place, obs_owner, joined, third, fourth, recv.reshape(2 * LAYERS, CY))
+    )(batch_order, place, obs_owner, own, first, second, recv)
     recv = lax.all_to_all(send.reshape(LAYERS, 2, CY), LAYER, 0, 0)
     send = jnp.broadcast_to(recv.reshape(1, 2 * LAYERS, CY), (PLANES, 2 * LAYERS, CY))
     recv = lax.all_to_all(send, PLANE, 0, 0)

time: 122 us -> 112 us (0.918)
  starting transfers between devices: 36.3 us -> 20.3 us
  blocking collectives: 51.2 us -> 62.5 us
  waiting for transfers between devices: 12.1 us -> 7.81 us
    all_to_all x0 -> x1, blocking collectives: none -> 20.7 us  [local(): recv = lax.all_to_all(send.reshape(PLANES, PLANE_ROWS, CY), PLANE, 0, 0)]
    all_to_all x2 -> x1, starting transfers between devices: 28.1 us -> 13.7 us  [local(): recv = lax.all_to_all(send.reshape(LAYERS, LAYER_ROWS, CY), LAYER, 0, 0)]
    all_to_all x1, blocking collectives: 29.9 us -> 23.3 us  [local(): recv = lax.all_to_all(send.reshape(LAYERS, 2, CY), LAYER, 0, 0)]
    all_to_all x2 -> x1, waiting for transfers between devices: 6.91 us -> 2.98 us  [local(): recv = lax.all_to_all(send.reshape(LAYERS, LAYER_ROWS, CY), LAYER, 0, 0)]
    all_to_all x1, blocking collectives: 21.3 us -> 18.5 us  [local(): recv = lax.all_to_all(send, PLANE, 0, 0)]
    ppermute x4 -> x2, starting transfers between devices: 8.24 us -> 6.61 us  [swapped(): return lax.ppermute(value, axis, pairs)]
    ppermute x4 -> x2, waiting for transfers between devices: 5.18 us -> 4.83 us  [swapped(): return lax.ppermute(value, axis, pairs)]
  transfers between devices with their start and end apart: 6 -> 3, of which waited for: 3 -> 2; matrix products, arithmetic and copies ran while one was open for 0% -> 0% of each run, Pallas kernels for 0% -> 0%
where the time goes in v5:
time: 112 us
  blocking collectives  62.5 us (56%)
  starting transfers between devices  20.3 us (18%)
  Pallas kernels  17.8 us (16%)
  waiting for transfers between devices  7.81 us (7%)
  local copies, waits for them, and re-layouts  3.05 us (3%)
    all_to_all x1, blocking collectives, local(): recv = lax.all_to_all(send.reshape(LAYERS, 2, CY), LAYER, 0, 0)  23.3 us
    all_to_all x1, blocking collectives, local(): recv = lax.all_to_all(send.reshape(PLANES, PLANE_ROWS, CY), PLANE, 0, 0)  20.7 us
    all_to_all x1, blocking collectives, local(): recv = lax.all_to_all(send, PLANE, 0, 0)  18.5 us
    all_to_all x1, starting transfers between devices, local(): recv = lax.all_to_all(send.reshape(LAYERS, LAYER_ROWS, CY), LAYER, 0, 0)  13.7 us
    pallas_call x1, Pallas kernels, local(): call(assimilate_kernel, [SMEM] * 4 + [VMEM] * 7, [shape(MEMBERS * GROUPS...  12.9 us
    ppermute x2, starting transfers between devices, swapped(): return lax.ppermute(value, axis, pairs)  6.61 us
    ppermute x2, waiting for transfers between devices, swapped(): return lax.ppermute(value, axis, pairs)  4.83 us
    unnamed x21, local copies, waits for them, and re-layouts  3 us
  transfers between devices with their start and end apart: 3, of which 2 were waited for; matrix products, arithmetic and copies ran while one was open for 0% of the time, Pallas kernels for 0%

profile of v5, /device:TPU:1, one launch (start us, length us, event | category | flops | bytes accessed | tf_op | source)
XLA Modules:
  0.0 111.6 jit_solution(17115404167731289069)
XLA Ops:
  0.0 0.0 copy-start.9
  0.0 0.7 copy-done.9
  0.7 0.0 copy-start.2
  0.7 0.0 copy-start.3
  0.7 0.0 copy-start.1
  0.7 0.1 pad_add_fusion.place_ref
  0.8 0.0 copy-start.5
  0.8 0.0 copy-start.7
  0.8 0.6 copy-done.2
  1.4 0.0 copy-done.3
  1.4 0.0 copy-done.1
  1.4 0.0 copy-done.5
  1.5 0.0 copy-done.7
  1.5 0.0 copy-start
  1.5 0.9 copy-done
  2.4 2.3 %shard_map.100 = (f32[4,32,512]{2,1,0:T(8,128)S(1)}, f32[256,128]{1,0:T(8,128)S(1)}, f32[256,128]{1,0:T(8,128)S(1)}, f32[1024,128]{1,0:T(8,128)S(1)}) custom-call(s32[3]{0:T(128)S(1)} %copy-done.5, s32[3]{0:T(128)S(1)} %pad_add_fusion.place_ref, f32[2]{0:T(128)S(1)} %copy-done.7, f32[512,128]{1,0:T(8,128)S(1)} %bitcast.19, s32[3,512]{1,0:T(4,128)S(1)} %copy-done.1, ...), custom_call_target="tpu_custom_call" | custom-call | tf_op jit(solution)/shard_map/pallas_call | solution.py:514
  4.8 20.7 %all_to_all.20 = f32[32,32,128]{2,1,0:T(8,128)S(1)} all-to-all(f32[32,32,128]{2,1,0:T(8,128)S(1)} %bitcast.18), channel_id=1, replica_groups=mesh['x'=4,'z_lo'=8,'core'=2,'z_hi'=2,'y'=4] {'x','core','y'}, dimensions={0} | all-to-all | bytes 1048576 | tf_op jit(solution)/shard_map/all_to_all | solution.py:524
  25.4 1.5 %shard_map.101 = f32[384,128]{1,0:T(8,128)} custom-call(s32[3]{0:T(128)S(1)} %pad_add_fusion.place_ref, f32[1024,128]{1,0:T(8,128)S(1)} %bitcast.16), custom_call_target="tpu_custom_call" | custom-call | tf_op jit(solution)/shard_map/pallas_call | solution.py:527
  27.0 13.7 %all-to-all-start.1 = ((f32[16,24,128]{2,1,0:T(8,128)}), f32[16,24,128]{2,1,0:T(8,128)S(1)}, u32[]{:S(2)}, u32[]{:S(2)}) async-start(f32[16,24,128]{2,1,0:T(8,128)} %bitcast.6), calls=%async_computation.1 | async-start | bytes 393216 | tf_op jit(solution)/shard_map/all_to_all | solution.py:530
  40.7 3.2 %collective-permute-start = (f32[256,128]{1,0:T(8,128)S(1)}, f32[256,128]{1,0:T(8,128)S(1)}, u32[]{:S(2)}, u32[]{:S(2)}) collective-permute-start(f32[256,128]{1,0:T(8,128)S(1)} %get-tuple-element.12), channel_id=1, source_target_pairs={{0,8},{8,0},{16,24},{24,16},{32,40},{40,32},{48,56},{56,48},{64,72... | collective-permute-start | bytes 393224 | tf_op jit(solution)/shard_map/ppermute | solution.py:493
  43.8 3.4 %collective-permute-start.1 = (f32[256,128]{1,0:T(8,128)S(1)}, f32[256,128]{1,0:T(8,128)S(1)}, u32[]{:S(2)}, u32[]{:S(2)}) collective-permute-start(f32[256,128]{1,0:T(8,128)S(1)} %get-tuple-element.13), channel_id=1, source_target_pairs={{0,504},{8,16},{16,8},{24,32},{32,24},{40,48},{48,40},{56,64},{64,... | collective-permute-start | bytes 393224 | tf_op jit(solution)/shard_map/ppermute | solution.py:493
  47.3 0.0 collective-permute-done.first_ref
  47.3 4.8 %collective-permute-done.1.second_ref = f32[256,128]{1,0:T(8,128)S(1)} collective-permute-done((f32[256,128]{1,0:T(8,128)S(1)}, f32[256,128]{1,0:T(8,128)S(1)}, u32[]{:S(2)}, u32[]{:S(2)}) %collective-permute-start.1) | collective-permute-done | bytes 131104 | tf_op jit(solution)/shard_map/ppermute | solution.py:493
  52.1 3.0 %all-to-all-done.1 = f32[16,24,128]{2,1,0:T(8,128)S(1)} async-done(((f32[16,24,128]{2,1,0:T(8,128)}), f32[16,24,128]{2,1,0:T(8,128)S(1)}, u32[]{:S(2)}, u32[]{:S(2)}) %all-to-all-start.1) | async-done | bytes 196640 | tf_op jit(solution)/shard_map/all_to_all | solution.py:530
  55.1 1.1 shard_map.102
  56.2 23.3 %all_to_all.21 = f32[16,2,128]{2,1,0:T(2,128)S(1)} all-to-all(f32[16,2,128]{2,1,0:T(2,128)S(1)} %bitcast.22), channel_id=1, replica_groups=mesh['x'=4,'z_lo'=8,'core'=2,'z_hi'=2,'y'=4] {'z_lo','z_hi'}, dimensions={0} | all-to-all | bytes 32768 | tf_op jit(solution)/shard_map/all_to_all | solution.py:537
  79.5 0.0 copy-start.4
  79.5 18.5 %all_to_all.22 = f32[32,32,128]{2,1,0:T(8,128)S(1)} all-to-all(f32[32,32,128]{2,1,0:T(8,128)S(1)} %broadcast_in_dim.8), channel_id=1, replica_groups=mesh['x'=4,'z_lo'=8,'core'=2,'z_hi'=2,'y'=4] {'x','core','y'}, dimensions={0} | all-to-all | bytes 1048576 | tf_op jit(solution)/shard_map/all_to_all | solution.py:539
  98.1 0.0 copy-start.6
  98.1 0.0 copy-start.8
  98.1 0.0 copy-done.4
  98.1 0.7 copy-done.6
  98.7 0.0 copy-done.8
  98.7 12.9 %shard_map.103 = f32[512,128]{1,0:T(8,128)} custom-call(s32[3]{0:T(128)S(1)} %copy-done.5, s32[3]{0:T(128)S(1)} %pad_add_fusion.place_ref, f32[2,2]{1,0:T(2,128)S(1)} %copy-done.6, f32[2]{0:T(128)S(1)} %copy-done.8, f32[4,32,512]{2,1,0:T(8,128)S(1)} %get-tuple-element.15.forecast_ref, f32[1024,128]{1,0:T(8,128)S(1)} %bitcast.15, s32[3,512]{1,0:T(4,128)S(1)} %copy-done.1, ...), custom_call_target="tpu_custom_call" | custom-call | tf_op jit(solution)/shard_map/pallas_call | solution.py:540
  (2 shorter events, 0.1 us)
Async XLA Ops:
  0.0 0.7 copy-start.9
  0.7 0.7 copy-start.2
  0.7 0.7 copy-start.3
  0.7 0.7 copy-start.1
  0.8 0.7 copy-start.5
  0.8 0.7 copy-start.7
  1.5 0.9 copy-start
  27.0 28.1 %all-to-all-start.1 = ((f32[16,24,128]{2,1,0:T(8,128)}), f32[16,24,128]{2,1,0:T(8,128)S(1)}, u32[]{:S(2)}, u32[]{:S(2)}) async-start(f32[16,24,128]{2,1,0:T(8,128)} %bitcast.6), calls=%async_computation.1 | async-start | bytes 393216 | tf_op jit(solution)/shard_map/all_to_all | solution.py:530
  40.7 6.6 %collective-permute-start = (f32[256,128]{1,0:T(8,128)S(1)}, f32[256,128]{1,0:T(8,128)S(1)}, u32[]{:S(2)}, u32[]{:S(2)}) collective-permute-start(f32[256,128]{1,0:T(8,128)S(1)} %get-tuple-element.12), channel_id=1, source_target_pairs={{0,8},{8,0},{16,24},{24,16},{32,40},{40,32},{48,56},{56,48},{64,72... | collective-permute-start | bytes 393224 | tf_op jit(solution)/shard_map/ppermute | solution.py:493
  43.8 8.3 %collective-permute-start.1 = (f32[256,128]{1,0:T(8,128)S(1)}, f32[256,128]{1,0:T(8,128)S(1)}, u32[]{:S(2)}, u32[]{:S(2)}) collective-permute-start(f32[256,128]{1,0:T(8,128)S(1)} %get-tuple-element.13), channel_id=1, source_target_pairs={{0,504},{8,16},{16,8},{24,32},{32,24},{40,48},{48,40},{56,64},{64,... | collective-permute-start | bytes 393224 | tf_op jit(solution)/shard_map/ppermute | solution.py:493
  79.5 18.5 %copy-start.4 = (f32[3,512]{1,0:T(4,128)S(1)}, f32[3,512]{1,0:T(4,128)}, u32[]{:S(2)}) copy-start(f32[3,512]{1,0:T(4,128)} %value_ref.1) | copy-start | bytes 18436
  98.1 0.7 copy-start.6
  98.1 0.7 copy-start.8

commit v6 on v5

--- a/solution.py
+++ b/solution.py
@@ -198,7 +198,16 @@
         send_ref[at + LAYERS : at + PLANE_ROWS, :] = up * high + down * low
 
 
-def collect_kernel(place_ref, recv_ref, send_ref):
+def collect_kernel(place_ref, recv_ref, own_ref, near_ref, far_ref, joined_ref, send_ref):
+    even = (place_ref[0] & 1) == 0
+    for group in range(GROUPS):
+        for column in range(CX):
+            at = (group * 2 + column % 2) * MEMBERS
+            part = slice(at, at + MEMBERS)
+            near, far = near_ref[part], far_ref[part]
+            other = jnp.where(even, far, near) if column < 2 else jnp.where(even, near, far)
+            cells = slice(column * CY, (column + 1) * CY)
+            joined_ref[group, :, cells] = own_ref[group, :, cells] + other
     place_x = place_ref[0]
     place_y = place_ref[1]
     x, z_lo, core = place_x >> 4, (place_x >> 1) & 7, place_x & 1
@@ -258,9 +267,7 @@
     order_ref,
     place_ref,
     relay_ref,
-    own_ref,
-    first_ref,
-    second_ref,
+    joined_ref,
     recv_ref,
     forecast_ref,
     send_ref,
@@ -277,17 +284,12 @@
     above = pltpu.roll(below, CY - 8, 1)
     below = jnp.concatenate([below, pltpu.roll(below, HALF, 1)], axis=0)
     above = jnp.concatenate([above, pltpu.roll(above, HALF, 1)], axis=0)
-    even = (place_ref[0] & 1) == 0
     wide = lax.broadcasted_iota(I32, (MEMBERS, CY), 1)
     for group in range(GROUPS):
         pieces = []
         for x in range(CX):
             at = group * 16 + (x + 2) * 2
-            part = (group * 2 + x % 2) * MEMBERS
-            part = slice(part, part + MEMBERS)
-            near = first_ref[part], second_ref[part]
-            other = jnp.where(even, near[1], near[0]) if x < 2 else jnp.where(even, near[0], near[1])
-            piece = own_ref[group, :, x * CY : (x + 1) * CY] + other
+            piece = joined_ref[group, :, x * CY : (x + 1) * CY]
             piece = piece + jnp.where(wide < 2, pltpu.roll(below, CY - at, 1), 0.0)
             piece = piece + jnp.where(wide >= CY - 2, pltpu.roll(above, CY - 2 - at, 1), 0.0)
             pieces.append(piece)
@@ -524,16 +526,18 @@
     recv = lax.all_to_all(send.reshape(PLANES, PLANE_ROWS, CY), PLANE, 0, 0)
     first = swapped(first, GX, 1, True)
     second = swapped(second, GX, -1, True)
-    send = call(collect_kernel, [SMEM, VMEM], [shape(LAYERS * LAYER_ROWS, CY)])(
-        place, recv.reshape(PLANES * PLANE_ROWS, CY)
-    )
+    joined, send = call(
+        collect_kernel,
+        [SMEM] + [VMEM] * 4,
+        [shape(GROUPS, MEMBERS, CELLS), shape(LAYERS * LAYER_ROWS, CY)],
+    )(place, recv.reshape(PLANES * PLANE_ROWS, CY), own, first, second)
     recv = lax.all_to_all(send.reshape(LAYERS, LAYER_ROWS, CY), LAYER, 0, 0)
     recv = recv.reshape(LAYERS * LAYER_ROWS, CY)
     forecast, send = call(
         merge_kernel,
-        [SMEM] * 3 + [VMEM] * 4,
+        [SMEM] * 3 + [VMEM] * 2,
         [shape(GROUPS, MEMBERS, CELLS), shape(2 * LAYERS, CY)],
-    )(batch_order, place, obs_owner, own, first, second, recv)
+    )(batch_order, place, obs_owner, joined, recv)
     recv = lax.all_to_all(send.reshape(LAYERS, 2, CY), LAYER, 0, 0)
     send = jnp.broadcast_to(recv.reshape(1, 2 * LAYERS, CY), (PLANES, 2 * LAYERS, CY))
     recv = lax.all_to_all(send, PLANE, 0, 0)

time: 112 us -> 112 us (level)
  blocking collectives: 62.5 us -> 68.6 us
  starting transfers between devices: 20.3 us -> 14.6 us
    all_to_all x1, blocking collectives: 23.3 us -> 14.4 us  [local(): recv = lax.all_to_all(send.reshape(LAYERS, 2, CY), LAYER, 0, 0)]
    all_to_all x1, blocking collectives: 20.7 us -> 29.1 us  [local(): recv = lax.all_to_all(send.reshape(LAYERS, LAYER_ROWS, CY), LAYER, 0, 0)]
    all_to_all x1, blocking collectives: 18.5 us -> 25.1 us  [local(): recv = lax.all_to_all(send, PLANE, 0, 0)]
    all_to_all x1, starting transfers between devices: 13.7 us -> 10.4 us  [local(): recv = lax.all_to_all(send.reshape(PLANES, PLANE_ROWS, CY), PLANE, 0, 0)]
    ppermute x2, starting transfers between devices: 6.61 us -> 4.16 us  [swapped(): return lax.ppermute(value, axis, pairs)]
where the time goes in v6:
time: 112 us; the launch traced here: 111 us
  blocking collectives  68.6 us (61%)
  Pallas kernels  18 us (16%)
  starting transfers between devices  14.6 us (13%)
  waiting for transfers between devices  6.94 us (6%)
  local copies, waits for them, and re-layouts  3.05 us (3%)
    all_to_all x1, blocking collectives, local(): recv = lax.all_to_all(send.reshape(LAYERS, LAYER_ROWS, CY), LAYER, 0, 0)  29.1 us
    all_to_all x1, blocking collectives, local(): recv = lax.all_to_all(send, PLANE, 0, 0)  25.1 us
    all_to_all x1, blocking collectives, local(): recv = lax.all_to_all(send.reshape(LAYERS, 2, CY), LAYER, 0, 0)  14.4 us
    pallas_call x1, Pallas kernels, local(): call(assimilate_kernel, [SMEM] * 4 + [VMEM] * 7, [shape(MEMBERS * GROUPS...  12.9 us
    all_to_all x1, starting transfers between devices, local(): recv = lax.all_to_all(send.reshape(PLANES, PLANE_ROWS, CY), PLANE, 0, 0)  10.4 us
    ppermute x2, waiting for transfers between devices, swapped(): return lax.ppermute(value, axis, pairs)  4.65 us
    ppermute x2, starting transfers between devices, swapped(): return lax.ppermute(value, axis, pairs)  4.16 us
    pallas_call x1, Pallas kernels, local(): call(spread_kernel, [SMEM] * 3 + [VMEM] * 5, [shape(GROUPS, MEMBERS, CELL...  3.15 us
  transfers between devices with their start and end apart: 3, of which 2 were waited for; matrix products, arithmetic and copies ran while one was open for 0% of the time, Pallas kernels for 0%

profile of v6, /device:TPU:1, one launch (start us, length us, event | category | flops | bytes accessed | tf_op | source)
XLA Modules:
  0.0 111.3 jit_solution(17247091905753736150)
XLA Ops:
  0.0 0.0 copy-start.9
  0.0 0.7 copy-done.9
  0.7 0.0 copy-start.2
  0.7 0.0 copy-start.3
  0.7 0.0 copy-start.1
  0.7 0.1 pad_add_fusion.place_ref
  0.8 0.0 copy-start.5
  0.8 0.0 copy-start.7
  0.8 0.6 copy-done.2
  1.4 0.0 copy-done.3
  1.4 0.0 copy-done.1
  1.4 0.0 copy-done.5
  1.5 0.0 copy-done.7
  1.5 0.0 copy-start
  1.5 0.9 copy-done
  2.4 3.1 %shard_map.100 = (f32[4,32,512]{2,1,0:T(8,128)S(1)}, f32[256,128]{1,0:T(8,128)S(1)}, f32[256,128]{1,0:T(8,128)S(1)}, f32[1024,128]{1,0:T(8,128)}) custom-call(s32[3]{0:T(128)S(1)} %copy-done.5, s32[3]{0:T(128)S(1)} %pad_add_fusion.place_ref, f32[2]{0:T(128)S(1)} %copy-done.7, f32[512,128]{1,0:T(8,128)S(1)} %bitcast.18, s32[3,512]{1,0:T(4,128)S(1)} %copy-done.1, ...), custom_call_target="tpu_custom_call" | custom-call | tf_op jit(solution)/shard_map/pallas_call | solution.py:516
  5.6 10.4 %all-to-all-start = ((f32[32,32,128]{2,1,0:T(8,128)}), f32[32,32,128]{2,1,0:T(8,128)S(1)}, u32[]{:S(2)}, u32[]{:S(2)}) async-start(f32[32,32,128]{2,1,0:T(8,128)} %bitcast.4), calls=%async_computation | async-start | bytes 1048576 | tf_op jit(solution)/shard_map/all_to_all | solution.py:526
  16.0 2.2 %collective-permute-start = (f32[256,128]{1,0:T(8,128)S(1)}, f32[256,128]{1,0:T(8,128)S(1)}, u32[]{:S(2)}, u32[]{:S(2)}) collective-permute-start(f32[256,128]{1,0:T(8,128)S(1)} %get-tuple-element.15), channel_id=1, source_target_pairs={{0,8},{8,0},{16,24},{24,16},{32,40},{40,32},{48,56},{56,48},{64,72... | collective-permute-start | bytes 393224 | tf_op jit(solution)/shard_map/ppermute | solution.py:495
  18.3 1.9 %collective-permute-start.1 = (f32[256,128]{1,0:T(8,128)S(1)}, f32[256,128]{1,0:T(8,128)S(1)}, u32[]{:S(2)}, u32[]{:S(2)}) collective-permute-start(f32[256,128]{1,0:T(8,128)S(1)} %get-tuple-element.16), channel_id=1, source_target_pairs={{0,504},{8,16},{16,8},{24,32},{32,24},{40,48},{48,40},{56,64},{64,... | collective-permute-start | bytes 393224 | tf_op jit(solution)/shard_map/ppermute | solution.py:495
  20.2 0.0 collective-permute-done.near_ref
  20.2 4.6 %collective-permute-done.1.far_ref = f32[256,128]{1,0:T(8,128)S(1)} collective-permute-done((f32[256,128]{1,0:T(8,128)S(1)}, f32[256,128]{1,0:T(8,128)S(1)}, u32[]{:S(2)}, u32[]{:S(2)}) %collective-permute-start.1) | collective-permute-done | bytes 131104 | tf_op jit(solution)/shard_map/ppermute | solution.py:495
  24.8 2.3 %all-to-all-done = f32[32,32,128]{2,1,0:T(8,128)S(1)} async-done(((f32[32,32,128]{2,1,0:T(8,128)}), f32[32,32,128]{2,1,0:T(8,128)S(1)}, u32[]{:S(2)}, u32[]{:S(2)}) %all-to-all-start) | async-done | bytes 524320 | tf_op jit(solution)/shard_map/all_to_all | solution.py:526
  27.1 0.9 shard_map.101
  28.0 29.1 %all_to_all.20 = f32[16,24,128]{2,1,0:T(8,128)S(1)} all-to-all(f32[16,24,128]{2,1,0:T(8,128)S(1)} %bitcast.19), channel_id=1, replica_groups=mesh['x'=4,'z_lo'=8,'core'=2,'z_hi'=2,'y'=4] {'z_lo','z_hi'}, dimensions={0} | all-to-all | bytes 393216 | tf_op jit(solution)/shard_map/all_to_all | solution.py:534
  57.1 1.1 shard_map.102
  58.2 14.4 %all_to_all.21 = f32[16,2,128]{2,1,0:T(2,128)S(1)} all-to-all(f32[16,2,128]{2,1,0:T(2,128)S(1)} %bitcast.22), channel_id=1, replica_groups=mesh['x'=4,'z_lo'=8,'core'=2,'z_hi'=2,'y'=4] {'z_lo','z_hi'}, dimensions={0} | all-to-all | bytes 32768 | tf_op jit(solution)/shard_map/all_to_all | solution.py:541
  72.6 0.0 copy-start.4
  72.7 25.1 %all_to_all.22 = f32[32,32,128]{2,1,0:T(8,128)S(1)} all-to-all(f32[32,32,128]{2,1,0:T(8,128)S(1)} %broadcast_in_dim.8), channel_id=1, replica_groups=mesh['x'=4,'z_lo'=8,'core'=2,'z_hi'=2,'y'=4] {'x','core','y'}, dimensions={0} | all-to-all | bytes 1048576 | tf_op jit(solution)/shard_map/all_to_all | solution.py:543
  97.8 0.0 copy-start.6
  97.8 0.0 copy-start.8
  97.8 0.0 copy-done.4
  97.8 0.7 copy-done.6
  98.5 0.0 copy-done.8
  98.5 12.9 %shard_map.103 = f32[512,128]{1,0:T(8,128)} custom-call(s32[3]{0:T(128)S(1)} %copy-done.5, s32[3]{0:T(128)S(1)} %pad_add_fusion.place_ref, f32[2,2]{1,0:T(2,128)S(1)} %copy-done.6, f32[2]{0:T(128)S(1)} %copy-done.8, f32[4,32,512]{2,1,0:T(8,128)S(1)} %get-tuple-element.19.forecast_ref, f32[1024,128]{1,0:T(8,128)S(1)} %bitcast.16, s32[3,512]{1,0:T(4,128)S(1)} %copy-done.1, ...), custom_call_target="tpu_custom_call" | custom-call | tf_op jit(solution)/shard_map/pallas_call | solution.py:544
  (2 shorter events, 0.1 us)
Async XLA Ops:
  0.0 0.7 copy-start.9
  0.7 0.7 copy-start.2
  0.7 0.7 copy-start.3
  0.7 0.7 copy-start.1
  0.8 0.7 copy-start.5
  0.8 0.7 copy-start.7
  1.5 0.9 copy-start
  5.6 21.6 %all-to-all-start = ((f32[32,32,128]{2,1,0:T(8,128)}), f32[32,32,128]{2,1,0:T(8,128)S(1)}, u32[]{:S(2)}, u32[]{:S(2)}) async-start(f32[32,32,128]{2,1,0:T(8,128)} %bitcast.4), calls=%async_computation | async-start | bytes 1048576 | tf_op jit(solution)/shard_map/all_to_all | solution.py:526
  16.0 4.2 %collective-permute-start = (f32[256,128]{1,0:T(8,128)S(1)}, f32[256,128]{1,0:T(8,128)S(1)}, u32[]{:S(2)}, u32[]{:S(2)}) collective-permute-start(f32[256,128]{1,0:T(8,128)S(1)} %get-tuple-element.15), channel_id=1, source_target_pairs={{0,8},{8,0},{16,24},{24,16},{32,40},{40,32},{48,56},{56,48},{64,72... | collective-permute-start | bytes 393224 | tf_op jit(solution)/shard_map/ppermute | solution.py:495
  18.3 6.6 %collective-permute-start.1 = (f32[256,128]{1,0:T(8,128)S(1)}, f32[256,128]{1,0:T(8,128)S(1)}, u32[]{:S(2)}, u32[]{:S(2)}) collective-permute-start(f32[256,128]{1,0:T(8,128)S(1)} %get-tuple-element.16), channel_id=1, source_target_pairs={{0,504},{8,16},{16,8},{24,32},{32,24},{40,48},{48,40},{56,64},{64,... | collective-permute-start | bytes 393224 | tf_op jit(solution)/shard_map/ppermute | solution.py:495
  72.6 25.1 %copy-start.4 = (f32[3,512]{1,0:T(4,128)S(1)}, f32[3,512]{1,0:T(4,128)}, u32[]{:S(2)}) copy-start(f32[3,512]{1,0:T(4,128)} %value_ref.1) | copy-start | bytes 18436
  97.8 0.7 copy-start.6
  97.8 0.7 copy-start.8

commit v7 on v6

--- a/solution.py
+++ b/solution.py
@@ -37,6 +37,7 @@
 PLANE = ("x", "core", "y")
 LAYER = ("z_lo", "z_hi")
 CHUNK = 256
+GATHER = 128
 AHEAD = GROUPS * CELLS
 PAIRS = ((0, 1), (0, 2), (1, 2))
 
@@ -340,9 +341,9 @@
     out_ref,
     state_ref,
     pack_ref,
-    left_ref,
+    sheet_ref,
     drive_ref,
-    table_ref,
+    order_of_ref,
     spots_ref,
     weight_ref,
 ):
@@ -362,8 +363,8 @@
 
     kinds, xs, ys, values = [], [], [], []
     sub = lax.broadcasted_iota(I32, (CY, OBS), 0)
-    table_ref[...] = jnp.zeros_like(table_ref)
     table = jnp.zeros((CY, OBS), F32)
+    near = []
     columns, spots = [], []
     for turn in range(BATCHES):
         batch = order_ref[turn]
@@ -376,8 +377,17 @@
         ys.append(((owner & (TILES_Y - 1)) * CY + (cell & (CY - 1))).astype(F32))
         tile_x = owner >> 3
         columns.append(tile_x + REACH)
-        for row, value in enumerate((xs[turn], ys[turn], mask, tile_x.astype(F32))):
-            table = jnp.where(sub == turn * 4 + row, value, table)
+        reach = REACH * (BATCHES - turn)
+        near.append(flag(((tile_x - place_x + reach) & (TILES_X - 1)) <= 2 * reach))
+        facts = (
+            xs[turn],
+            (owner & (TILES_Y - 1)).astype(F32),
+            (cell & (CY - 1)).astype(F32),
+            mask,
+            tile_x.astype(F32),
+        )
+        for row, value in enumerate(facts):
+            table = jnp.where(sub == turn * 8 + row, value, table)
         prior = upper[turn * MEMBERS : (turn + 1) * MEMBERS]
         centre = jnp.sum(prior, axis=0, keepdims=True) * (1.0 / MEMBERS)
         factor = jnp.where(kinds[turn] == 0, stretch[0], stretch[2])
@@ -387,7 +397,14 @@
     for number, (turn, other) in enumerate(PAIRS):
         hot = jnp.where(sub == spots[other] + turn * HALF, 1.0, 0.0)
         spots_ref[:, number * OBS : (number + 1) * OBS] = hot.astype(BF16)
-    table_ref[...] = table.T
+    sheet_ref[:, CY : 2 * CY] = table.T.astype(BF16)
+    sheet_ref[:, 2 * CY : 3 * CY] = recv_ref[pl.ds(1, TILES, stride=2), :].astype(BF16)
+    ahead = lax.broadcasted_iota(I32, (OBS, OBS), 0) <= lax.broadcasted_iota(I32, (OBS, OBS), 1)
+    counts = jnp.concatenate([*near, jnp.zeros((8 - BATCHES, OBS), F32)], axis=0)
+    counts = mm(counts.astype(BF16), jnp.where(ahead, 1.0, 0.0).astype(BF16))
+    for turn in range(BATCHES):
+        slot = jnp.where(near[turn] > 0.0, counts[turn : turn + 1] - 1.0, -1.0)
+        order_of_ref[turn : turn + 1] = slot.astype(I32)
 
     lane = lax.broadcasted_iota(I32, (1, CY), 1)
     cell_x = (place_x * CX).astype(F32)
@@ -410,7 +427,7 @@
         packed = jnp.concatenate(
             [scaled_high, scaled_high, scaled_low, jnp.zeros_like(scaled)], axis=0
         )
-        left_ref[...] = packed.T.astype(BF16)
+        sheet_ref[:, :CY] = packed.T.astype(BF16)
 
         later = list(range(turn + 1, BATCHES))
         blocks = [slice(group * CELLS, (group + 1) * CELLS) for group in range(GROUPS)]
@@ -424,14 +441,26 @@
             pack_ref[64:96, cols] = high
             pack_ref[96:128, cols] = jnp.zeros_like(high)
 
-        @pl.loop(0, OBS // CHUNK)
+        total = jnp.sum(near[turn])
+        trips = jnp.int32(0)
+        for start in range(0, OBS, GATHER):
+            trips = trips + jnp.where(total > float(start), 1, 0)
+        slot = order_of_ref[turn : turn + 1]
+
+        @pl.loop(0, trips)
         def _(step):
-            start = pl.multiple_of(step * CHUNK, CHUNK)
-            part = pl.ds(start, CHUNK)
-            table = table_ref[part, :]
-            x_col = table[:, turn * 4 : turn * 4 + 1]
-            y_col = table[:, turn * 4 + 1 : turn * 4 + 2]
-            mask_col = table[:, turn * 4 + 2 : turn * 4 + 3]
+            place = lax.broadcasted_iota(I32, (GATHER, OBS), 0) + step * GATHER
+            hot = jnp.where(place == slot, 1.0, 0.0).astype(BF16)
+            sheet = mm(hot, sheet_ref[...])
+            left = sheet[:, :CY].astype(BF16)
+            table = sheet[:, CY : 2 * CY]
+            marks = sheet[:, 2 * CY :].astype(BF16)
+            drive = lax.dot_general(
+                drive_ref[...], hot, (((1,), (1,)), ((), ())), preferred_element_type=F32
+            ).astype(BF16)
+            x_col = table[:, turn * 8 : turn * 8 + 1]
+            y_col = table[:, turn * 8 + 1 : turn * 8 + 2] * CY + table[:, turn * 8 + 2 : turn * 8 + 3]
+            mask_col = table[:, turn * 8 + 3 : turn * 8 + 4]
             gap_y = y_col - cell_y
             drop_y = gap_y * gap_y * (1.0 / (LOC_Y * LOC_Y))
             for x in range(CX):
@@ -440,9 +469,8 @@
                 room = jnp.maximum((1.0 - gap_x * gap_x * (1.0 / (LOC_X * LOC_X))) - drop_y, 0.0)
                 weight_ref[:, x * CY : (x + 1) * CY] = room * room * mask_col
             if later:
-                column = table[:, turn * 4 + 3 : turn * 4 + 4].astype(I32)
-                marks = recv_ref[pl.ds(2 * start + 1, CHUNK, stride=2), :].astype(BF16)
-                for place, other in enumerate(later):
+                column = table[:, turn * 8 + 4 : turn * 8 + 5].astype(I32)
+                for index, other in enumerate(later):
                     number = PAIRS.index((turn, other))
                     allowed = mm(marks, spots_ref[:, number * OBS : (number + 1) * OBS])
                     apart = (columns[other] - column) & (TILES_X - 1)
@@ -452,10 +480,8 @@
                     gap_y = y_col - ys[other]
                     room = 1.0 - gap_x * gap_x * (1.0 / (LOC_X * LOC_X))
                     room = jnp.maximum(room - gap_y * gap_y * (1.0 / (LOC_Y * LOC_Y)), 0.0)
-                    weight_ref[:, (place + 1) * OBS : (place + 2) * OBS] = room * room * allowed
-
-            left = left_ref[part, :]
-            drive = drive_ref[:, part]
+                    weight_ref[:, (index + 1) * OBS : (index + 2) * OBS] = room * room * allowed
+
             for number, cols in enumerate(blocks):
                 at = max(0, number - GROUPS + 1) * OBS
                 covariance = mm(left, pack_ref[:, cols]) * weight_ref[:, at : at + OBS]
@@ -548,11 +574,11 @@
         [
             pltpu.VMEM((MEMBERS, AHEAD + BATCHES * OBS), F32),
             pltpu.VMEM((CY, AHEAD + BATCHES * OBS), BF16),
-            pltpu.VMEM((OBS, CY), BF16),
+            pltpu.VMEM((OBS, 3 * CY), BF16),
             pltpu.VMEM((2 * MEMBERS, OBS), BF16),
-            pltpu.VMEM((OBS, CY), F32),
+            pltpu.VMEM((8, OBS), I32),
             pltpu.VMEM((CY, BATCHES * OBS), BF16),
-            pltpu.VMEM((CHUNK, BATCHES * OBS), F32),
+            pltpu.VMEM((GATHER, BATCHES * OBS), F32),
         ],
     )(
         batch_order,

time: 112 us -> 105 us (0.938)
  Pallas kernels: 18 us -> 11 us
    pallas_call x1, Pallas kernels: 12.9 us -> 5.88 us  [local(): call(assimilate_kernel, [SMEM] * 4 + [VMEM] * 7, [shape(MEMBERS * GROUPS...]
where the time goes in v7:
time: 105 us; the launch traced here: 104 us
  blocking collectives  68.6 us (65%)
  starting transfers between devices  14.6 us (14%)
  Pallas kernels  11 us (10%)
  waiting for transfers between devices  6.94 us (7%)
  local copies, waits for them, and re-layouts  3.05 us (3%)
    all_to_all x1, blocking collectives, local(): recv = lax.all_to_all(send.reshape(LAYERS, LAYER_ROWS, CY), LAYER, 0, 0)  29.1 us
    all_to_all x1, blocking collectives, local(): recv = lax.all_to_all(send, PLANE, 0, 0)  25.1 us
    all_to_all x1, blocking collectives, local(): recv = lax.all_to_all(send.reshape(LAYERS, 2, CY), LAYER, 0, 0)  14.4 us
    all_to_all x1, starting transfers between devices, local(): recv = lax.all_to_all(send.reshape(PLANES, PLANE_ROWS, CY), PLANE, 0, 0)  10.4 us
    pallas_call x1, Pallas kernels, local(): call(assimilate_kernel, [SMEM] * 4 + [VMEM] * 7, [shape(MEMBERS * GROUPS...  5.88 us
    ppermute x2, waiting for transfers between devices, swapped(): return lax.ppermute(value, axis, pairs)  4.65 us
    ppermute x2, starting transfers between devices, swapped(): return lax.ppermute(value, axis, pairs)  4.16 us
    pallas_call x1, Pallas kernels, local(): call(spread_kernel, [SMEM] * 3 + [VMEM] * 5, [shape(GROUPS, MEMBERS, CELL...  3.15 us
  transfers between devices with their start and end apart: 3, of which 2 were waited for; matrix products, arithmetic and copies ran while one was open for 0% of the time, Pallas kernels for 0%

profile of v7, /device:TPU:1, one launch (start us, length us, event | category | flops | bytes accessed | tf_op | source)
XLA Modules:
  0.0 104.3 jit_solution(16091854208311151449)
XLA Ops:
  0.0 0.0 copy-start.9
  0.0 0.7 copy-done.9
  0.7 0.0 copy-start.2
  0.7 0.0 copy-start.3
  0.7 0.0 copy-start.1
  0.7 0.1 pad_add_fusion.place_ref
  0.8 0.0 copy-start.5
  0.8 0.0 copy-start.7
  0.8 0.6 copy-done.2
  1.4 0.0 copy-done.3
  1.4 0.0 copy-done.1
  1.4 0.0 copy-done.5
  1.5 0.0 copy-done.7
  1.5 0.0 copy-start
  1.5 0.9 copy-done
  2.4 3.1 %shard_map.100 = (f32[4,32,512]{2,1,0:T(8,128)S(1)}, f32[256,128]{1,0:T(8,128)S(1)}, f32[256,128]{1,0:T(8,128)S(1)}, f32[1024,128]{1,0:T(8,128)}) custom-call(s32[3]{0:T(128)S(1)} %copy-done.5, s32[3]{0:T(128)S(1)} %pad_add_fusion.place_ref, f32[2]{0:T(128)S(1)} %copy-done.7, f32[512,128]{1,0:T(8,128)S(1)} %bitcast.18, s32[3,512]{1,0:T(4,128)S(1)} %copy-done.1, ...), custom_call_target="tpu_custom_call" | custom-call | tf_op jit(solution)/shard_map/pallas_call | solution.py:542
  5.6 10.4 %all-to-all-start = ((f32[32,32,128]{2,1,0:T(8,128)}), f32[32,32,128]{2,1,0:T(8,128)S(1)}, u32[]{:S(2)}, u32[]{:S(2)}) async-start(f32[32,32,128]{2,1,0:T(8,128)} %bitcast.4), calls=%async_computation | async-start | bytes 1048576 | tf_op jit(solution)/shard_map/all_to_all | solution.py:552
  16.0 2.2 %collective-permute-start = (f32[256,128]{1,0:T(8,128)S(1)}, f32[256,128]{1,0:T(8,128)S(1)}, u32[]{:S(2)}, u32[]{:S(2)}) collective-permute-start(f32[256,128]{1,0:T(8,128)S(1)} %get-tuple-element.15), channel_id=1, source_target_pairs={{0,8},{8,0},{16,24},{24,16},{32,40},{40,32},{48,56},{56,48},{64,72... | collective-permute-start | bytes 393224 | tf_op jit(solution)/shard_map/ppermute | solution.py:521
  18.3 1.9 %collective-permute-start.1 = (f32[256,128]{1,0:T(8,128)S(1)}, f32[256,128]{1,0:T(8,128)S(1)}, u32[]{:S(2)}, u32[]{:S(2)}) collective-permute-start(f32[256,128]{1,0:T(8,128)S(1)} %get-tuple-element.16), channel_id=1, source_target_pairs={{0,504},{8,16},{16,8},{24,32},{32,24},{40,48},{48,40},{56,64},{64,... | collective-permute-start | bytes 393224 | tf_op jit(solution)/shard_map/ppermute | solution.py:521
  20.2 0.0 collective-permute-done.near_ref
  20.2 4.6 %collective-permute-done.1.far_ref = f32[256,128]{1,0:T(8,128)S(1)} collective-permute-done((f32[256,128]{1,0:T(8,128)S(1)}, f32[256,128]{1,0:T(8,128)S(1)}, u32[]{:S(2)}, u32[]{:S(2)}) %collective-permute-start.1) | collective-permute-done | bytes 131104 | tf_op jit(solution)/shard_map/ppermute | solution.py:521
  24.8 2.3 %all-to-all-done = f32[32,32,128]{2,1,0:T(8,128)S(1)} async-done(((f32[32,32,128]{2,1,0:T(8,128)}), f32[32,32,128]{2,1,0:T(8,128)S(1)}, u32[]{:S(2)}, u32[]{:S(2)}) %all-to-all-start) | async-done | bytes 524320 | tf_op jit(solution)/shard_map/all_to_all | solution.py:552
  27.1 0.9 shard_map.101
  28.0 29.1 %all_to_all.20 = f32[16,24,128]{2,1,0:T(8,128)S(1)} all-to-all(f32[16,24,128]{2,1,0:T(8,128)S(1)} %bitcast.19), channel_id=1, replica_groups=mesh['x'=4,'z_lo'=8,'core'=2,'z_hi'=2,'y'=4] {'z_lo','z_hi'}, dimensions={0} | all-to-all | bytes 393216 | tf_op jit(solution)/shard_map/all_to_all | solution.py:560
  57.1 1.1 %shard_map.102 = (f32[4,32,512]{2,1,0:T(8,128)S(1)}, f32[32,128]{1,0:T(8,128)S(1)}) custom-call(s32[3]{0:T(128)S(1)} %copy-done.5, s32[3]{0:T(128)S(1)} %pad_add_fusion.place_ref, s32[3,512]{1,0:T(4,128)S(1)} %copy-done.1, f32[4,32,512]{2,1,0:T(8,128)S(1)} %get-tuple-element.17.joined_ref, f32[384,128]{1,0:T(8,128)S(1)} %bitcast.17), custom_call_target="tpu_custom_call" | custom-call | tf_op jit(solution)/shard_map/pallas_call | solution.py:562
  58.2 14.4 %all_to_all.21 = f32[16,2,128]{2,1,0:T(2,128)S(1)} all-to-all(f32[16,2,128]{2,1,0:T(2,128)S(1)} %bitcast.22), channel_id=1, replica_groups=mesh['x'=4,'z_lo'=8,'core'=2,'z_hi'=2,'y'=4] {'z_lo','z_hi'}, dimensions={0} | all-to-all | bytes 32768 | tf_op jit(solution)/shard_map/all_to_all | solution.py:567
  72.6 0.0 copy-start.4
  72.7 25.1 %all_to_all.22 = f32[32,32,128]{2,1,0:T(8,128)S(1)} all-to-all(f32[32,32,128]{2,1,0:T(8,128)S(1)} %broadcast_in_dim.8), channel_id=1, replica_groups=mesh['x'=4,'z_lo'=8,'core'=2,'z_hi'=2,'y'=4] {'x','core','y'}, dimensions={0} | all-to-all | bytes 1048576 | tf_op jit(solution)/shard_map/all_to_all | solution.py:569
  97.8 0.0 copy-start.6
  97.8 0.0 copy-start.8
  97.8 0.0 copy-done.4
  97.8 0.7 copy-done.6
  98.5 0.0 copy-done.8
  98.5 5.9 %shard_map.103 = f32[512,128]{1,0:T(8,128)} custom-call(s32[3]{0:T(128)S(1)} %copy-done.5, s32[3]{0:T(128)S(1)} %pad_add_fusion.place_ref, f32[2,2]{1,0:T(2,128)S(1)} %copy-done.6, f32[2]{0:T(128)S(1)} %copy-done.8, f32[4,32,512]{2,1,0:T(8,128)S(1)} %get-tuple-element.19.forecast_ref, f32[1024,128]{1,0:T(8,128)S(1)} %bitcast.16, s32[3,512]{1,0:T(4,128)S(1)} %copy-done.1, ...), custom_call_target="tpu_custom_call" | custom-call | tf_op jit(solution)/shard_map/pallas_call | solution.py:570
  (2 shorter events, 0.1 us)
Async XLA Ops:
  0.0 0.7 copy-start.9
  0.7 0.7 copy-start.2
  0.7 0.7 copy-start.3
  0.7 0.7 copy-start.1
  0.8 0.7 copy-start.5
  0.8 0.7 copy-start.7
  1.5 0.9 copy-start
  5.6 21.6 %all-to-all-start = ((f32[32,32,128]{2,1,0:T(8,128)}), f32[32,32,128]{2,1,0:T(8,128)S(1)}, u32[]{:S(2)}, u32[]{:S(2)}) async-start(f32[32,32,128]{2,1,0:T(8,128)} %bitcast.4), calls=%async_computation | async-start | bytes 1048576 | tf_op jit(solution)/shard_map/all_to_all | solution.py:552
  16.0 4.2 %collective-permute-start = (f32[256,128]{1,0:T(8,128)S(1)}, f32[256,128]{1,0:T(8,128)S(1)}, u32[]{:S(2)}, u32[]{:S(2)}) collective-permute-start(f32[256,128]{1,0:T(8,128)S(1)} %get-tuple-element.15), channel_id=1, source_target_pairs={{0,8},{8,0},{16,24},{24,16},{32,40},{40,32},{48,56},{56,48},{64,72... | collective-permute-start | bytes 393224 | tf_op jit(solution)/shard_map/ppermute | solution.py:521
  18.3 6.6 %collective-permute-start.1 = (f32[256,128]{1,0:T(8,128)S(1)}, f32[256,128]{1,0:T(8,128)S(1)}, u32[]{:S(2)}, u32[]{:S(2)}) collective-permute-start(f32[256,128]{1,0:T(8,128)S(1)} %get-tuple-element.16), channel_id=1, source_target_pairs={{0,504},{8,16},{16,8},{24,32},{32,24},{40,48},{48,40},{56,64},{64,... | collective-permute-start | bytes 393224 | tf_op jit(solution)/shard_map/ppermute | solution.py:521
  72.6 25.1 %copy-start.4 = (f32[3,512]{1,0:T(4,128)S(1)}, f32[3,512]{1,0:T(4,128)}, u32[]{:S(2)}) copy-start(f32[3,512]{1,0:T(4,128)} %value_ref.1) | copy-start | bytes 18436
  97.8 0.7 copy-start.6
  97.8 0.7 copy-start.8

commit v8 on v7

--- a/solution.py
+++ b/solution.py
@@ -36,6 +36,7 @@
 GY = ("z_hi", "y")
 PLANE = ("x", "core", "y")
 LAYER = ("z_lo", "z_hi")
+CHIP = ("x", "y")
 CHUNK = 256
 GATHER = 128
 AHEAD = GROUPS * CELLS
@@ -332,7 +333,8 @@
     spread_ref,
     error_ref,
     forecast_ref,
-    recv_ref,
+    mine_ref,
+    twin_ref,
     owner_ref,
     cell_ref,
     kind_ref,
@@ -346,9 +348,17 @@
     order_of_ref,
     spots_ref,
     weight_ref,
+    recv_ref,
 ):
     place_x = place_ref[0]
     place_y = place_ref[1]
+    first = (place_x & 1) == 0
+    for plane in range(PLANES):
+        source = (plane // 8 * 4 + plane % 4) * 2 * LAYERS
+        source = slice(source, source + 2 * LAYERS)
+        mine, twin = mine_ref[source], twin_ref[source]
+        rows = jnp.where(first, twin, mine) if plane // 4 % 2 else jnp.where(first, mine, twin)
+        recv_ref[plane * 2 * LAYERS : (plane + 1) * 2 * LAYERS] = rows
     upper = recv_ref[pl.ds(0, TILES, stride=2), :].T
     stretch = []
     for group in range(GROUPS):
@@ -565,11 +575,13 @@
         [shape(GROUPS, MEMBERS, CELLS), shape(2 * LAYERS, CY)],
     )(batch_order, place, obs_owner, joined, recv)
     recv = lax.all_to_all(send.reshape(LAYERS, 2, CY), LAYER, 0, 0)
-    send = jnp.broadcast_to(recv.reshape(1, 2 * LAYERS, CY), (PLANES, 2 * LAYERS, CY))
-    recv = lax.all_to_all(send, PLANE, 0, 0)
+    chips = PLANES // 2
+    send = jnp.broadcast_to(recv.reshape(1, 2 * LAYERS, CY), (chips, 2 * LAYERS, CY))
+    mine = lax.all_to_all(send, CHIP, 0, 0).reshape(TILES, CY)
+    twin = lax.ppermute(mine, "core", [(0, 1), (1, 0)])
     out = call(
         assimilate_kernel,
-        [SMEM] * 4 + [VMEM] * 7,
+        [SMEM] * 4 + [VMEM] * 8,
         [shape(MEMBERS * GROUPS * CX, CY)],
         [
             pltpu.VMEM((MEMBERS, AHEAD + BATCHES * OBS), F32),
@@ -579,6 +591,7 @@
             pltpu.VMEM((8, OBS), I32),
             pltpu.VMEM((CY, BATCHES * OBS), BF16),
             pltpu.VMEM((GATHER, BATCHES * OBS), F32),
+            pltpu.VMEM((2 * TILES, CY), F32),
         ],
     )(
         batch_order,
@@ -586,7 +599,8 @@
         target_spread,
         obs_error,
         forecast,
-        recv.reshape(2 * TILES, CY),
+        mine,
+        twin,
         obs_owner,
         obs_cell,
         obs_kind,

time: 105 us -> 105 us (level)
  blocking collectives: 68.6 us -> 61.8 us
  starting transfers between devices: 14.6 us -> 20.9 us
  waiting for transfers between devices: 6.94 us -> 8.08 us
    all_to_all x1, blocking collectives: 25.1 us -> 18.2 us  [local(): mine = lax.all_to_all(send, CHIP, 0, 0).reshape(TILES, CY)]
    ppermute x0 -> x1, starting transfers between devices: none -> 6.28 us  [local(): twin = lax.ppermute(mine, 'core', [(0, 1), (1, 0)])]
    ppermute x0 -> x1, waiting for transfers between devices: none -> 1.14 us  [local(): twin = lax.ppermute(mine, 'core', [(0, 1), (1, 0)])]
  transfers between devices with their start and end apart: 3 -> 4, of which waited for: 2 -> 3; matrix products, arithmetic and copies ran while one was open for 0% -> 0% of each run, Pallas kernels for 0% -> 0%
where the time goes in v8:
time: 105 us; the launch traced here: 104 us
  blocking collectives  61.8 us (59%)
  starting transfers between devices  20.9 us (20%)
  Pallas kernels  11 us (10%)
  waiting for transfers between devices  8.08 us (8%)
  local copies, waits for them, and re-layouts  2.35 us (2%)
    all_to_all x1, blocking collectives, local(): recv = lax.all_to_all(send.reshape(LAYERS, LAYER_ROWS, CY), LAYER, 0, 0)  29.1 us
    all_to_all x1, blocking collectives, local(): mine = lax.all_to_all(send, CHIP, 0, 0).reshape(TILES, CY)  18.2 us
    all_to_all x1, blocking collectives, local(): recv = lax.all_to_all(send.reshape(LAYERS, 2, CY), LAYER, 0, 0)  14.4 us
    all_to_all x1, starting transfers between devices, local(): recv = lax.all_to_all(send.reshape(PLANES, PLANE_ROWS, CY), PLANE, 0, 0)  10.4 us
    ppermute x1, starting transfers between devices, local(): twin = lax.ppermute(mine, 'core', [(0, 1), (1, 0)])  6.28 us
    pallas_call x1, Pallas kernels, local(): call(assimilate_kernel, [SMEM] * 4 + [VMEM] * 8, [shape(MEMBERS * GROUPS...  5.92 us
    ppermute x2, waiting for transfers between devices, swapped(): return lax.ppermute(value, axis, pairs)  4.65 us
    ppermute x2, starting transfers between devices, swapped(): return lax.ppermute(value, axis, pairs)  4.16 us
  transfers between devices with their start and end apart: 4, of which 3 were waited for; matrix products, arithmetic and copies ran while one was open for 0% of the time, Pallas kernels for 0%

profile of v8, /device:TPU:1, one launch (start us, length us, event | category | flops | bytes accessed | tf_op | source)
XLA Modules:
  0.0 104.2 jit_solution(10866024647389444644)
XLA Ops:
  0.0 0.0 copy-start.9
  0.0 0.7 copy-done.9
  0.7 0.0 copy-start.2
  0.7 0.0 copy-start.3
  0.7 0.0 copy-start.1
  0.7 0.1 pad_add_fusion.place_ref
  0.8 0.0 copy-start.5
  0.8 0.0 copy-start.7
  0.8 0.6 copy-done.2
  1.4 0.0 copy-done.3
  1.4 0.0 copy-done.1
  1.4 0.0 copy-done.5
  1.5 0.0 copy-done.7
  1.5 0.0 copy-start
  1.5 0.9 copy-done
  2.4 3.1 %shard_map.100 = (f32[4,32,512]{2,1,0:T(8,128)S(1)}, f32[256,128]{1,0:T(8,128)S(1)}, f32[256,128]{1,0:T(8,128)S(1)}, f32[1024,128]{1,0:T(8,128)}) custom-call(s32[3]{0:T(128)S(1)} %copy-done.5, s32[3]{0:T(128)S(1)} %pad_add_fusion.place_ref, f32[2]{0:T(128)S(1)} %copy-done.7, f32[512,128]{1,0:T(8,128)S(1)} %bitcast.19, s32[3,512]{1,0:T(4,128)S(1)} %copy-done.1, ...), custom_call_target="tpu_custom_call" | custom-call | tf_op jit(solution)/shard_map/pallas_call | solution.py:552
  5.6 10.4 %all-to-all-start = ((f32[32,32,128]{2,1,0:T(8,128)}), f32[32,32,128]{2,1,0:T(8,128)S(1)}, u32[]{:S(2)}, u32[]{:S(2)}) async-start(f32[32,32,128]{2,1,0:T(8,128)} %bitcast.4), calls=%async_computation | async-start | bytes 1048576 | tf_op jit(solution)/shard_map/all_to_all | solution.py:562
  16.0 2.2 %collective-permute-start = (f32[256,128]{1,0:T(8,128)S(1)}, f32[256,128]{1,0:T(8,128)S(1)}, u32[]{:S(2)}, u32[]{:S(2)}) collective-permute-start(f32[256,128]{1,0:T(8,128)S(1)} %get-tuple-element.15), channel_id=1, source_target_pairs={{0,8},{8,0},{16,24},{24,16},{32,40},{40,32},{48,56},{56,48},{64,72... | collective-permute-start | bytes 393224 | tf_op jit(solution)/shard_map/ppermute | solution.py:531
  18.3 1.9 %collective-permute-start.1 = (f32[256,128]{1,0:T(8,128)S(1)}, f32[256,128]{1,0:T(8,128)S(1)}, u32[]{:S(2)}, u32[]{:S(2)}) collective-permute-start(f32[256,128]{1,0:T(8,128)S(1)} %get-tuple-element.16), channel_id=1, source_target_pairs={{0,504},{8,16},{16,8},{24,32},{32,24},{40,48},{48,40},{56,64},{64,... | collective-permute-start | bytes 393224 | tf_op jit(solution)/shard_map/ppermute | solution.py:531
  20.2 0.0 collective-permute-done.near_ref
  20.2 4.6 %collective-permute-done.1.far_ref = f32[256,128]{1,0:T(8,128)S(1)} collective-permute-done((f32[256,128]{1,0:T(8,128)S(1)}, f32[256,128]{1,0:T(8,128)S(1)}, u32[]{:S(2)}, u32[]{:S(2)}) %collective-permute-start.1) | collective-permute-done | bytes 131104 | tf_op jit(solution)/shard_map/ppermute | solution.py:531
  24.8 2.3 %all-to-all-done = f32[32,32,128]{2,1,0:T(8,128)S(1)} async-done(((f32[32,32,128]{2,1,0:T(8,128)}), f32[32,32,128]{2,1,0:T(8,128)S(1)}, u32[]{:S(2)}, u32[]{:S(2)}) %all-to-all-start) | async-done | bytes 524320 | tf_op jit(solution)/shard_map/all_to_all | solution.py:562
  27.1 0.9 shard_map.101
  28.0 29.1 %all_to_all.20 = f32[16,24,128]{2,1,0:T(8,128)S(1)} all-to-all(f32[16,24,128]{2,1,0:T(8,128)S(1)} %bitcast.20), channel_id=1, replica_groups=mesh['x'=4,'z_lo'=8,'core'=2,'z_hi'=2,'y'=4] {'z_lo','z_hi'}, dimensions={0} | all-to-all | bytes 393216 | tf_op jit(solution)/shard_map/all_to_all | solution.py:570
  57.1 1.1 %shard_map.102 = (f32[4,32,512]{2,1,0:T(8,128)S(1)}, f32[32,128]{1,0:T(8,128)S(1)}) custom-call(s32[3]{0:T(128)S(1)} %copy-done.5, s32[3]{0:T(128)S(1)} %pad_add_fusion.place_ref, s32[3,512]{1,0:T(4,128)S(1)} %copy-done.1, f32[4,32,512]{2,1,0:T(8,128)S(1)} %get-tuple-element.17.joined_ref, f32[384,128]{1,0:T(8,128)S(1)} %bitcast.18), custom_call_target="tpu_custom_call" | custom-call | tf_op jit(solution)/shard_map/pallas_call | solution.py:572
  58.2 14.4 %all_to_all.21 = f32[16,2,128]{2,1,0:T(2,128)S(1)} all-to-all(f32[16,2,128]{2,1,0:T(2,128)S(1)} %bitcast.23), channel_id=1, replica_groups=mesh['x'=4,'z_lo'=8,'core'=2,'z_hi'=2,'y'=4] {'z_lo','z_hi'}, dimensions={0} | all-to-all | bytes 32768 | tf_op jit(solution)/shard_map/all_to_all | solution.py:577
  72.6 0.0 copy-start.4
  72.6 18.2 %all_to_all.22 = f32[16,32,128]{2,1,0:T(8,128)S(1)} all-to-all(f32[16,32,128]{2,1,0:T(8,128)S(1)} %broadcast_in_dim.8), channel_id=1, replica_groups=mesh['x'=4,'z_lo'=8,'core'=2,'z_hi'=2,'y'=4] {'x','y'}, dimensions={0} | all-to-all | bytes 524288 | tf_op jit(solution)/shard_map/all_to_all | solution.py:580
  90.9 0.0 copy-start.6
  90.9 0.0 copy-start.8
  90.9 6.3 %collective-permute-start.2 = (f32[512,128]{1,0:T(8,128)S(1)}, f32[512,128]{1,0:T(8,128)S(1)}, u32[]{:S(2)}, u32[]{:S(2)}) collective-permute-start(f32[512,128]{1,0:T(8,128)S(1)} %bitcast.16), channel_id=1, source_target_pairs={{0,8},{8,0},{1,9},{9,1},{2,10},{10,2},{3,11},{11,3},{4,12},{12,4},... | collective-permute-start | bytes 786440 | tf_op jit(solution)/shard_map/ppermute | solution.py:581
  97.2 1.1 %collective-permute-done.2.twin_ref = f32[512,128]{1,0:T(8,128)S(1)} collective-permute-done((f32[512,128]{1,0:T(8,128)S(1)}, f32[512,128]{1,0:T(8,128)S(1)}, u32[]{:S(2)}, u32[]{:S(2)}) %collective-permute-start.2) | collective-permute-done | bytes 262176 | tf_op jit(solution)/shard_map/ppermute | solution.py:581
  98.3 0.0 copy-done.4
  98.3 0.0 copy-done.6
  98.3 0.0 copy-done.8
  98.3 5.9 %shard_map.103 = f32[512,128]{1,0:T(8,128)} custom-call(s32[3]{0:T(128)S(1)} %copy-done.5, s32[3]{0:T(128)S(1)} %pad_add_fusion.place_ref, f32[2,2]{1,0:T(2,128)S(1)} %copy-done.6, f32[2]{0:T(128)S(1)} %copy-done.8, f32[4,32,512]{2,1,0:T(8,128)S(1)} %get-tuple-element.19.forecast_ref, f32[512,128]{1,0:T(8,128)S(1)} %bitcast.17, ...), custom_call_target="tpu_custom_call" | custom-call | tf_op jit(solution)/shard_map/pallas_call | solution.py:582
  (2 shorter events, 0.0 us)
Async XLA Ops:
  0.0 0.7 copy-start.9
  0.7 0.7 copy-start.2
  0.7 0.7 copy-start.3
  0.7 0.7 copy-start.1
  0.8 0.7 copy-start.5
  0.8 0.7 copy-start.7
  1.5 0.9 copy-start
  5.6 21.6 %all-to-all-start = ((f32[32,32,128]{2,1,0:T(8,128)}), f32[32,32,128]{2,1,0:T(8,128)S(1)}, u32[]{:S(2)}, u32[]{:S(2)}) async-start(f32[32,32,128]{2,1,0:T(8,128)} %bitcast.4), calls=%async_computation | async-start | bytes 1048576 | tf_op jit(solution)/shard_map/all_to_all | solution.py:562
  16.0 4.2 %collective-permute-start = (f32[256,128]{1,0:T(8,128)S(1)}, f32[256,128]{1,0:T(8,128)S(1)}, u32[]{:S(2)}, u32[]{:S(2)}) collective-permute-start(f32[256,128]{1,0:T(8,128)S(1)} %get-tuple-element.15), channel_id=1, source_target_pairs={{0,8},{8,0},{16,24},{24,16},{32,40},{40,32},{48,56},{56,48},{64,72... | collective-permute-start | bytes 393224 | tf_op jit(solution)/shard_map/ppermute | solution.py:531
  18.3 6.6 %collective-permute-start.1 = (f32[256,128]{1,0:T(8,128)S(1)}, f32[256,128]{1,0:T(8,128)S(1)}, u32[]{:S(2)}, u32[]{:S(2)}) collective-permute-start(f32[256,128]{1,0:T(8,128)S(1)} %get-tuple-element.16), channel_id=1, source_target_pairs={{0,504},{8,16},{16,8},{24,32},{32,24},{40,48},{48,40},{56,64},{64,... | collective-permute-start | bytes 393224 | tf_op jit(solution)/shard_map/ppermute | solution.py:531
  72.6 25.7 %copy-start.4 = (f32[3,512]{1,0:T(4,128)S(1)}, f32[3,512]{1,0:T(4,128)}, u32[]{:S(2)}) copy-start(f32[3,512]{1,0:T(4,128)} %value_ref.1) | copy-start | bytes 18436
  90.9 7.4 %copy-start.6 = (f32[2,2]{1,0:T(2,128)S(1)}, f32[2,2]{1,0:T(2,128)}, u32[]{:S(2)}) copy-start(f32[2,2]{1,0:T(2,128)} %spread_ref.1) | copy-start | bytes 52
  90.9 7.4 %copy-start.8 = (f32[2]{0:T(128)S(1)}, f32[2]{0:T(128)}, u32[]{:S(2)}) copy-start(f32[2]{0:T(128)} %error_ref.1) | copy-start | bytes 28
  90.9 7.4 %collective-permute-start.2 = (f32[512,128]{1,0:T(8,128)S(1)}, f32[512,128]{1,0:T(8,128)S(1)}, u32[]{:S(2)}, u32[]{:S(2)}) collective-permute-start(f32[512,128]{1,0:T(8,128)S(1)} %bitcast.16), channel_id=1, source_target_pairs={{0,8},{8,0},{1,9},{9,1},{2,10},{10,2},{3,11},{11,3},{4,12},{12,4},... | collective-permute-start | bytes 786440 | tf_op jit(solution)/shard_map/ppermute | solution.py:581

commit v9 on v8

--- a/solution.py
+++ b/solution.py
@@ -29,9 +29,10 @@
 RIM = 16
 VALUES = BATCHES * MEMBERS
 PLANE_ROWS = LAYERS + RIM
-LAYER_ROWS = 24
+LAYER_ROWS = RIM + 2
 WIDE = (CX + 4) * CY
 SIDE = 2 * GROUPS * MEMBERS
+PAD = 128
 GX = ("x", "z_lo", "core")
 GY = ("z_hi", "y")
 PLANE = ("x", "core", "y")
@@ -144,6 +145,8 @@
         low = jnp.where(there, pltpu.roll(edge, at + 2, 1), low)
         high = jnp.where(there, pltpu.roll(edge, at, 1) if at else edge, high)
     rim = low + pltpu.roll(high, HALF, 1)
+    first_ref[SIDE:] = jnp.zeros((PAD, CY), F32)
+    second_ref[SIDE:] = jnp.zeros((PAD, CY), F32)
     even = (place_x & 1) == 0
     for group in range(GROUPS):
         for x in range(2):
@@ -200,16 +203,7 @@
         send_ref[at + LAYERS : at + PLANE_ROWS, :] = up * high + down * low
 
 
-def collect_kernel(place_ref, recv_ref, own_ref, near_ref, far_ref, joined_ref, send_ref):
-    even = (place_ref[0] & 1) == 0
-    for group in range(GROUPS):
-        for column in range(CX):
-            at = (group * 2 + column % 2) * MEMBERS
-            part = slice(at, at + MEMBERS)
-            near, far = near_ref[part], far_ref[part]
-            other = jnp.where(even, far, near) if column < 2 else jnp.where(even, near, far)
-            cells = slice(column * CY, (column + 1) * CY)
-            joined_ref[group, :, cells] = own_ref[group, :, cells] + other
+def collect_kernel(place_ref, recv_ref, send_ref):
     place_x = place_ref[0]
     place_y = place_ref[1]
     x, z_lo, core = place_x >> 4, (place_x >> 1) & 7, place_x & 1
@@ -262,14 +256,15 @@
         )
         pair = jnp.concatenate([total[layer : layer + 1], marks[layer : layer + 1]], axis=0)
         send_ref[at + RIM : at + RIM + 2, :] = pair
-        send_ref[at + RIM + 2 : at + LAYER_ROWS, :] = jnp.zeros((LAYER_ROWS - RIM - 2, CY), F32)
 
 
 def merge_kernel(
     order_ref,
     place_ref,
     relay_ref,
-    joined_ref,
+    own_ref,
+    near_ref,
+    far_ref,
     recv_ref,
     forecast_ref,
     send_ref,
@@ -286,12 +281,16 @@
     above = pltpu.roll(below, CY - 8, 1)
     below = jnp.concatenate([below, pltpu.roll(below, HALF, 1)], axis=0)
     above = jnp.concatenate([above, pltpu.roll(above, HALF, 1)], axis=0)
+    even = (place_ref[0] & 1) == 0
     wide = lax.broadcasted_iota(I32, (MEMBERS, CY), 1)
     for group in range(GROUPS):
         pieces = []
         for x in range(CX):
             at = group * 16 + (x + 2) * 2
-            piece = joined_ref[group, :, x * CY : (x + 1) * CY]
+            part = (group * 2 + x % 2) * MEMBERS
+            near, far = near_ref[part : part + MEMBERS], far_ref[part : part + MEMBERS]
+            other = jnp.where(even, far, near) if x < 2 else jnp.where(even, near, far)
+            piece = own_ref[group, :, x * CY : (x + 1) * CY] + other
             piece = piece + jnp.where(wide < 2, pltpu.roll(below, CY - at, 1), 0.0)
             piece = piece + jnp.where(wide >= CY - 2, pltpu.roll(above, CY - 2 - at, 1), 0.0)
             pieces.append(piece)
@@ -554,26 +553,24 @@
         [SMEM] * 3 + [VMEM] * 5,
         [
             shape(GROUPS, MEMBERS, CELLS),
-            shape(SIDE, CY),
-            shape(SIDE, CY),
+            shape(SIDE + PAD, CY),
+            shape(SIDE + PAD, CY),
             shape(PLANES * PLANE_ROWS, CY),
         ],
     )(batch_order, place, courant, ens, obs_owner, obs_cell, obs_kind, mask)
     recv = lax.all_to_all(send.reshape(PLANES, PLANE_ROWS, CY), PLANE, 0, 0)
     first = swapped(first, GX, 1, True)
     second = swapped(second, GX, -1, True)
-    joined, send = call(
-        collect_kernel,
-        [SMEM] + [VMEM] * 4,
-        [shape(GROUPS, MEMBERS, CELLS), shape(LAYERS * LAYER_ROWS, CY)],
-    )(place, recv.reshape(PLANES * PLANE_ROWS, CY), own, first, second)
-    recv = lax.all_to_all(send.reshape(LAYERS, LAYER_ROWS, CY), LAYER, 0, 0)
+    send = call(collect_kernel, [SMEM, VMEM], [shape(LAYERS * LAYER_ROWS, CY)])(
+        place, recv.reshape(PLANES * PLANE_ROWS, CY)
+    )
+    recv = lax.all_to_all(send.reshape(LAYERS, LAYER_ROWS // 2, 2, CY), LAYER, 0, 0)
     recv = recv.reshape(LAYERS * LAYER_ROWS, CY)
     forecast, send = call(
         merge_kernel,
-        [SMEM] * 3 + [VMEM] * 2,
+        [SMEM] * 3 + [VMEM] * 4,
         [shape(GROUPS, MEMBERS, CELLS), shape(2 * LAYERS, CY)],
-    )(batch_order, place, obs_owner, joined, recv)
+    )(batch_order, place, obs_owner, own, first, second, recv)
     recv = lax.all_to_all(send.reshape(LAYERS, 2, CY), LAYER, 0, 0)
     chips = PLANES // 2
     send = jnp.broadcast_to(recv.reshape(1, 2 * LAYERS, CY), (chips, 2 * LAYERS, CY))

time: 105 us -> 106 us (level)
  starting transfers between devices: 20.9 us -> 26.9 us
  blocking collectives: 61.8 us -> 56.6 us
    all_to_all x1, blocking collectives: 14.4 us -> 24.7 us  [local(): recv = lax.all_to_all(send.reshape(LAYERS, 2, CY), LAYER, 0, 0)]
    all_to_all x1, blocking collectives: 29.1 us -> 20.7 us  [local(): recv = lax.all_to_all(send.reshape(PLANES, PLANE_ROWS, CY), PLANE, 0, 0)]
    all_to_all x1, blocking collectives: 18.2 us -> 11.3 us  [local(): mine = lax.all_to_all(send, CHIP, 0, 0).reshape(TILES, CY)]
    all_to_all x1, starting transfers between devices: 10.4 us -> 13.7 us  [local(): lax.all_to_all(send.reshape(LAYERS, LAYER_ROWS // 2, 2, CY), LAYER, 0, 0)]
    ppermute x2, starting transfers between devices: 4.16 us -> 6.61 us  [swapped(): return lax.ppermute(value, axis, pairs)]
where the time goes in v9:
time: 106 us; the launch traced here: 105 us
  blocking collectives  56.6 us (53%)
  starting transfers between devices  26.9 us (25%)
  Pallas kernels  10.9 us (10%)
  waiting for transfers between devices  8.26 us (8%)
  local copies, waits for them, and re-layouts  2.35 us (2%)
    all_to_all x1, blocking collectives, local(): recv = lax.all_to_all(send.reshape(LAYERS, 2, CY), LAYER, 0, 0)  24.7 us
    all_to_all x1, blocking collectives, local(): recv = lax.all_to_all(send.reshape(PLANES, PLANE_ROWS, CY), PLANE, 0, 0)  20.7 us
    all_to_all x1, starting transfers between devices, local(): lax.all_to_all(send.reshape(LAYERS, LAYER_ROWS // 2, 2, CY), LAYER, 0, 0)  13.7 us
    all_to_all x1, blocking collectives, local(): mine = lax.all_to_all(send, CHIP, 0, 0).reshape(TILES, CY)  11.3 us
    ppermute x2, starting transfers between devices, swapped(): return lax.ppermute(value, axis, pairs)  6.61 us
    ppermute x1, starting transfers between devices, local(): twin = lax.ppermute(mine, 'core', [(0, 1), (1, 0)])  6.6 us
    pallas_call x1, Pallas kernels, local(): call(assimilate_kernel, [SMEM] * 4 + [VMEM] * 8, [shape(MEMBERS * GROUPS...  5.92 us
    ppermute x2, waiting for transfers between devices, swapped(): return lax.ppermute(value, axis, pairs)  5.19 us
  transfers between devices with their start and end apart: 4, of which 3 were waited for; matrix products, arithmetic and copies ran while one was open for 0% of the time, Pallas kernels for 0%

profile of v9, /device:TPU:1, one launch (start us, length us, event | category | flops | bytes accessed | tf_op | source)
XLA Modules:
  0.0 105.1 jit_solution(14960561712232218033)
XLA Ops:
  0.0 0.0 copy-start.9
  0.0 0.7 copy-done.9
  0.7 0.0 copy-start.2
  0.7 0.0 copy-start.3
  0.7 0.0 copy-start.1
  0.7 0.1 pad_add_fusion.place_ref
  0.8 0.0 copy-start.5
  0.8 0.0 copy-start.7
  0.8 0.6 copy-done.2
  1.4 0.0 copy-done.3
  1.4 0.0 copy-done.1
  1.4 0.0 copy-done.5
  1.5 0.0 copy-done.7
  1.5 0.0 copy-start
  1.5 0.9 copy-done
  2.4 2.3 %shard_map.100 = (f32[4,32,512]{2,1,0:T(8,128)S(1)}, f32[384,128]{1,0:T(8,128)S(1)}, f32[384,128]{1,0:T(8,128)S(1)}, f32[1024,128]{1,0:T(8,128)S(1)}) custom-call(s32[3]{0:T(128)S(1)} %copy-done.5, s32[3]{0:T(128)S(1)} %pad_add_fusion.place_ref, f32[2]{0:T(128)S(1)} %copy-done.7, f32[512,128]{1,0:T(8,128)S(1)} %bitcast.20, s32[3,512]{1,0:T(4,128)S(1)} %copy-done.1, ...), custom_call_target="tpu_custom_call" | custom-call | tf_op jit(solution)/shard_map/pallas_call | solution.py:551
  4.8 20.7 %all_to_all.20 = f32[32,32,128]{2,1,0:T(8,128)S(1)} all-to-all(f32[32,32,128]{2,1,0:T(8,128)S(1)} %bitcast.19), channel_id=1, replica_groups=mesh['x'=4,'z_lo'=8,'core'=2,'z_hi'=2,'y'=4] {'x','core','y'}, dimensions={0} | all-to-all | bytes 1048576 | tf_op jit(solution)/shard_map/all_to_all | solution.py:561
  25.4 1.5 %shard_map.101 = f32[288,128]{1,0:T(8,128)} custom-call(s32[3]{0:T(128)S(1)} %pad_add_fusion.place_ref, f32[1024,128]{1,0:T(8,128)S(1)} %bitcast.15), custom_call_target="tpu_custom_call" | custom-call | tf_op jit(solution)/shard_map/pallas_call | solution.py:564
  27.0 13.7 %all-to-all-start.1 = ((f32[16,9,2,128]{3,2,1,0:T(2,128)}), f32[16,9,2,128]{3,2,1,0:T(2,128)S(1)}, u32[]{:S(2)}, u32[]{:S(2)}) async-start(f32[16,9,2,128]{3,2,1,0:T(2,128)} %bitcast.6), calls=%async_computation.1 | async-start | bytes 294912 | tf_op jit(solution)/shard_map/all_to_all | solution.py:567
  40.7 3.2 %collective-permute-start = (f32[384,128]{1,0:T(8,128)S(1)}, f32[384,128]{1,0:T(8,128)S(1)}, u32[]{:S(2)}, u32[]{:S(2)}) collective-permute-start(f32[384,128]{1,0:T(8,128)S(1)} %get-tuple-element.12), channel_id=1, source_target_pairs={{0,8},{8,0},{16,24},{24,16},{32,40},{40,32},{48,56},{56,48},{64,72... | collective-permute-start | bytes 589832 | tf_op jit(solution)/shard_map/ppermute | solution.py:530
  43.8 3.4 %collective-permute-start.1 = (f32[384,128]{1,0:T(8,128)S(1)}, f32[384,128]{1,0:T(8,128)S(1)}, u32[]{:S(2)}, u32[]{:S(2)}) collective-permute-start(f32[384,128]{1,0:T(8,128)S(1)} %get-tuple-element.13), channel_id=1, source_target_pairs={{0,504},{8,16},{16,8},{24,32},{32,24},{40,48},{48,40},{56,64},{64,... | collective-permute-start | bytes 589832 | tf_op jit(solution)/shard_map/ppermute | solution.py:530
  47.3 0.0 collective-permute-done.near_ref
  47.3 5.2 %collective-permute-done.1.far_ref = f32[384,128]{1,0:T(8,128)S(1)} collective-permute-done((f32[384,128]{1,0:T(8,128)S(1)}, f32[384,128]{1,0:T(8,128)S(1)}, u32[]{:S(2)}, u32[]{:S(2)}) %collective-permute-start.1) | collective-permute-done | bytes 196640 | tf_op jit(solution)/shard_map/ppermute | solution.py:530
  52.5 1.9 %all-to-all-done.1 = f32[16,9,2,128]{3,2,1,0:T(2,128)S(1)} async-done(((f32[16,9,2,128]{3,2,1,0:T(2,128)}), f32[16,9,2,128]{3,2,1,0:T(2,128)S(1)}, u32[]{:S(2)}, u32[]{:S(2)}) %all-to-all-start.1) | async-done | bytes 147488 | tf_op jit(solution)/shard_map/all_to_all | solution.py:567
  54.4 1.1 %shard_map.102 = (f32[4,32,512]{2,1,0:T(8,128)S(1)}, f32[32,128]{1,0:T(8,128)S(1)}) custom-call(s32[3]{0:T(128)S(1)} %copy-done.5, s32[3]{0:T(128)S(1)} %pad_add_fusion.place_ref, s32[3,512]{1,0:T(4,128)S(1)} %copy-done.1, f32[4,32,512]{2,1,0:T(8,128)S(1)} %get-tuple-element.11.own_ref, f32[384,128]{1,0:T(8,128)S(1)} %collective-permute-done.near_ref, ...), custom_call_target="tpu_custom_call" | custom-call | tf_op jit(solution)/shard_map/pallas_call | solution.py:569
  55.5 24.7 %all_to_all.21 = f32[16,2,128]{2,1,0:T(2,128)S(1)} all-to-all(f32[16,2,128]{2,1,0:T(2,128)S(1)} %bitcast.23), channel_id=1, replica_groups=mesh['x'=4,'z_lo'=8,'core'=2,'z_hi'=2,'y'=4] {'z_lo','z_hi'}, dimensions={0} | all-to-all | bytes 32768 | tf_op jit(solution)/shard_map/all_to_all | solution.py:574
  80.2 0.0 copy-start.4
  80.2 11.3 %all_to_all.22 = f32[16,32,128]{2,1,0:T(8,128)S(1)} all-to-all(f32[16,32,128]{2,1,0:T(8,128)S(1)} %broadcast_in_dim.8), channel_id=1, replica_groups=mesh['x'=4,'z_lo'=8,'core'=2,'z_hi'=2,'y'=4] {'x','y'}, dimensions={0} | all-to-all | bytes 524288 | tf_op jit(solution)/shard_map/all_to_all | solution.py:577
  91.4 0.0 copy-start.6
  91.4 0.0 copy-start.8
  91.4 6.6 %collective-permute-start.2 = (f32[512,128]{1,0:T(8,128)S(1)}, f32[512,128]{1,0:T(8,128)S(1)}, u32[]{:S(2)}, u32[]{:S(2)}) collective-permute-start(f32[512,128]{1,0:T(8,128)S(1)} %bitcast.16), channel_id=1, source_target_pairs={{0,8},{8,0},{1,9},{9,1},{2,10},{10,2},{3,11},{11,3},{4,12},{12,4},... | collective-permute-start | bytes 786440 | tf_op jit(solution)/shard_map/ppermute | solution.py:578
  98.0 1.1 %collective-permute-done.2.twin_ref = f32[512,128]{1,0:T(8,128)S(1)} collective-permute-done((f32[512,128]{1,0:T(8,128)S(1)}, f32[512,128]{1,0:T(8,128)S(1)}, u32[]{:S(2)}, u32[]{:S(2)}) %collective-permute-start.2) | collective-permute-done | bytes 262176 | tf_op jit(solution)/shard_map/ppermute | solution.py:578
  99.2 0.0 copy-done.4
  99.2 0.0 copy-done.6
  99.2 0.0 copy-done.8
  99.2 5.9 %shard_map.103 = f32[512,128]{1,0:T(8,128)} custom-call(s32[3]{0:T(128)S(1)} %copy-done.5, s32[3]{0:T(128)S(1)} %pad_add_fusion.place_ref, f32[2,2]{1,0:T(2,128)S(1)} %copy-done.6, f32[2]{0:T(128)S(1)} %copy-done.8, f32[4,32,512]{2,1,0:T(8,128)S(1)} %get-tuple-element.15.forecast_ref, f32[512,128]{1,0:T(8,128)S(1)} %bitcast.17, ...), custom_call_target="tpu_custom_call" | custom-call | tf_op jit(solution)/shard_map/pallas_call | solution.py:579
  (2 shorter events, 0.0 us)
Async XLA Ops:
  0.0 0.7 copy-start.9
  0.7 0.7 copy-start.2
  0.7 0.7 copy-start.3
  0.7 0.7 copy-start.1
  0.8 0.7 copy-start.5
  0.8 0.7 copy-start.7
  1.5 0.9 copy-start
  27.0 27.4 %all-to-all-start.1 = ((f32[16,9,2,128]{3,2,1,0:T(2,128)}), f32[16,9,2,128]{3,2,1,0:T(2,128)S(1)}, u32[]{:S(2)}, u32[]{:S(2)}) async-start(f32[16,9,2,128]{3,2,1,0:T(2,128)} %bitcast.6), calls=%async_computation.1 | async-start | bytes 294912 | tf_op jit(solution)/shard_map/all_to_all | solution.py:567
  40.7 6.6 %collective-permute-start = (f32[384,128]{1,0:T(8,128)S(1)}, f32[384,128]{1,0:T(8,128)S(1)}, u32[]{:S(2)}, u32[]{:S(2)}) collective-permute-start(f32[384,128]{1,0:T(8,128)S(1)} %get-tuple-element.12), channel_id=1, source_target_pairs={{0,8},{8,0},{16,24},{24,16},{32,40},{40,32},{48,56},{56,48},{64,72... | collective-permute-start | bytes 589832 | tf_op jit(solution)/shard_map/ppermute | solution.py:530
  43.8 8.6 %collective-permute-start.1 = (f32[384,128]{1,0:T(8,128)S(1)}, f32[384,128]{1,0:T(8,128)S(1)}, u32[]{:S(2)}, u32[]{:S(2)}) collective-permute-start(f32[384,128]{1,0:T(8,128)S(1)} %get-tuple-element.13), channel_id=1, source_target_pairs={{0,504},{8,16},{16,8},{24,32},{32,24},{40,48},{48,40},{56,64},{64,... | collective-permute-start | bytes 589832 | tf_op jit(solution)/shard_map/ppermute | solution.py:530
  80.2 19.0 %copy-start.4 = (f32[3,512]{1,0:T(4,128)S(1)}, f32[3,512]{1,0:T(4,128)}, u32[]{:S(2)}) copy-start(f32[3,512]{1,0:T(4,128)} %value_ref.1) | copy-start | bytes 18436
  91.4 7.8 %copy-start.6 = (f32[2,2]{1,0:T(2,128)S(1)}, f32[2,2]{1,0:T(2,128)}, u32[]{:S(2)}) copy-start(f32[2,2]{1,0:T(2,128)} %spread_ref.1) | copy-start | bytes 52
  91.4 7.8 %copy-start.8 = (f32[2]{0:T(128)S(1)}, f32[2]{0:T(128)}, u32[]{:S(2)}) copy-start(f32[2]{0:T(128)} %error_ref.1) | copy-start | bytes 28
  91.4 7.8 %collective-permute-start.2 = (f32[512,128]{1,0:T(8,128)S(1)}, f32[512,128]{1,0:T(8,128)S(1)}, u32[]{:S(2)}, u32[]{:S(2)}) collective-permute-start(f32[512,128]{1,0:T(8,128)S(1)} %bitcast.16), channel_id=1, source_target_pairs={{0,8},{8,0},{1,9},{9,1},{2,10},{10,2},{3,11},{11,3},{4,12},{12,4},... | collective-permute-start | bytes 786440 | tf_op jit(solution)/shard_map/ppermute | solution.py:578

commit v10 on v8

--- a/solution.py
+++ b/solution.py
@@ -29,7 +29,7 @@
 RIM = 16
 VALUES = BATCHES * MEMBERS
 PLANE_ROWS = LAYERS + RIM
-LAYER_ROWS = 24
+LAYER_ROWS = RIM + 2
 WIDE = (CX + 4) * CY
 SIDE = 2 * GROUPS * MEMBERS
 GX = ("x", "z_lo", "core")
@@ -166,7 +166,7 @@
         owner = owner_ref[pl.ds(batch, 1), :]
         cell = cell_ref[pl.ds(batch, 1), :]
         kind = kind_ref[pl.ds(batch, 1), :]
-        masks.append(mask_ref[pl.ds(batch, 1), :].astype(F32))
+        masks.append(mask_ref[batch].astype(F32))
         at_x = ((owner >> 3) - place_x) * CX + (cell >> 7) + 2
         at_x = at_x & (NX - 1)
         at_y = ((owner & (TILES_Y - 1)) - place_y) * CY + (cell & (CY - 1))
@@ -262,7 +262,6 @@
         )
         pair = jnp.concatenate([total[layer : layer + 1], marks[layer : layer + 1]], axis=0)
         send_ref[at + RIM : at + RIM + 2, :] = pair
-        send_ref[at + RIM + 2 : at + LAYER_ROWS, :] = jnp.zeros((LAYER_ROWS - RIM - 2, CY), F32)
 
 
 def merge_kernel(
@@ -382,7 +381,7 @@
         cell = cell_ref[pl.ds(batch, 1), :]
         kinds.append(kind_ref[pl.ds(batch, 1), :])
         values.append(value_ref[pl.ds(batch, 1), :])
-        mask = mask_ref[pl.ds(batch, 1), :].astype(F32)
+        mask = mask_ref[batch].astype(F32)
         xs.append(((owner >> 3) * CX + (cell >> 7)).astype(F32))
         ys.append(((owner & (TILES_Y - 1)) * CY + (cell & (CY - 1))).astype(F32))
         tile_x = owner >> 3
@@ -548,7 +547,7 @@
     relay = lax.axis_index(PLANE) * LAYERS + lax.axis_index(LAYER)
     place = jnp.stack([place_x, place_y, relay]).astype(I32)
     ens = ensemble.reshape(MEMBERS * GROUPS * CX, CY)
-    mask = tile_mask.reshape(BATCHES, OBS)
+    mask = tile_mask.reshape(BATCHES, 1, OBS)
     own, first, second, send = call(
         spread_kernel,
         [SMEM] * 3 + [VMEM] * 5,
@@ -567,7 +566,7 @@
         [SMEM] + [VMEM] * 4,
         [shape(GROUPS, MEMBERS, CELLS), shape(LAYERS * LAYER_ROWS, CY)],
     )(place, recv.reshape(PLANES * PLANE_ROWS, CY), own, first, second)
-    recv = lax.all_to_all(send.reshape(LAYERS, LAYER_ROWS, CY), LAYER, 0, 0)
+    recv = lax.all_to_all(send.reshape(LAYERS, LAYER_ROWS // 2, 2, CY), LAYER, 0, 0)
     recv = recv.reshape(LAYERS * LAYER_ROWS, CY)
     forecast, send = call(
         merge_kernel,

time: 105 us -> 102 us (0.971)
  blocking collectives: 61.8 us -> 59.6 us
    all_to_all x1, blocking collectives: 18.2 us -> 17.1 us  [local(): mine = lax.all_to_all(send, CHIP, 0, 0).reshape(TILES, CY)]
    unnamed x21 -> x20, local copies, waits for them, and re-layouts: 2.33 us -> 1.63 us
where the time goes in v10:
time: 102 us; the launch traced here: 101 us
  blocking collectives  59.6 us (58%)
  starting transfers between devices  20.9 us (20%)
  Pallas kernels  11 us (11%)
  waiting for transfers between devices  8.08 us (8%)
  local copies, waits for them, and re-layouts  1.65 us (2%)
    all_to_all x1, blocking collectives, local(): lax.all_to_all(send.reshape(LAYERS, LAYER_ROWS // 2, 2, CY), LAYER, 0, 0)  28.4 us
    all_to_all x1, blocking collectives, local(): mine = lax.all_to_all(send, CHIP, 0, 0).reshape(TILES, CY)  17.1 us
    all_to_all x1, blocking collectives, local(): recv = lax.all_to_all(send.reshape(LAYERS, 2, CY), LAYER, 0, 0)  14.1 us
    all_to_all x1, starting transfers between devices, local(): recv = lax.all_to_all(send.reshape(PLANES, PLANE_ROWS, CY), PLANE, 0, 0)  10.4 us
    ppermute x1, starting transfers between devices, local(): twin = lax.ppermute(mine, 'core', [(0, 1), (1, 0)])  6.3 us
    pallas_call x1, Pallas kernels, local(): call(assimilate_kernel, [SMEM] * 4 + [VMEM] * 8, [shape(MEMBERS * GROUPS...  5.92 us
    ppermute x2, waiting for transfers between devices, swapped(): return lax.ppermute(value, axis, pairs)  4.65 us
    ppermute x2, starting transfers between devices, swapped(): return lax.ppermute(value, axis, pairs)  4.16 us
  transfers between devices with their start and end apart: 4, of which 3 were waited for; matrix products, arithmetic and copies ran while one was open for 0% of the time, Pallas kernels for 0%

profile of v10, /device:TPU:1, one launch (start us, length us, event | category | flops | bytes accessed | tf_op | source)
XLA Modules:
  0.0 101.4 jit_solution(1752719466754664654)
XLA Ops:
  0.0 0.0 copy-start.6
  0.0 0.0 copy-start.8
  0.0 0.0 copy-start.4
  0.0 0.0 copy-start.3
  0.0 0.0 copy-start.2
  0.0 0.0 copy-start.1
  0.0 0.1 pad_add_fusion.place_ref
  0.1 0.5 copy-done.6
  0.7 0.0 copy-done.8
  0.7 0.1 copy-done.4
  0.7 0.0 copy-done.3
  0.7 0.0 copy-done.2
  0.8 0.0 copy-done.1
  0.8 0.0 copy-start
  0.8 0.9 copy-done
  1.7 3.1 %shard_map.100 = (f32[4,32,512]{2,1,0:T(8,128)S(1)}, f32[256,128]{1,0:T(8,128)S(1)}, f32[256,128]{1,0:T(8,128)S(1)}, f32[1024,128]{1,0:T(8,128)}) custom-call(s32[3]{0:T(128)S(1)} %copy-done.6, s32[3]{0:T(128)S(1)} %pad_add_fusion.place_ref, f32[2]{0:T(128)S(1)} %copy-done.8, f32[512,128]{1,0:T(8,128)S(1)} %bitcast.17, s32[3,512]{1,0:T(4,128)S(1)} %copy-done.1, ...), custom_call_target="tpu_custom_call" | custom-call | tf_op jit(solution)/shard_map/pallas_call | solution.py:551
  4.9 10.4 %all-to-all-start = ((f32[32,32,128]{2,1,0:T(8,128)}), f32[32,32,128]{2,1,0:T(8,128)S(1)}, u32[]{:S(2)}, u32[]{:S(2)}) async-start(f32[32,32,128]{2,1,0:T(8,128)} %bitcast.5), calls=%async_computation | async-start | bytes 1048576 | tf_op jit(solution)/shard_map/all_to_all | solution.py:561
  15.3 2.2 %collective-permute-start = (f32[256,128]{1,0:T(8,128)S(1)}, f32[256,128]{1,0:T(8,128)S(1)}, u32[]{:S(2)}, u32[]{:S(2)}) collective-permute-start(f32[256,128]{1,0:T(8,128)S(1)} %get-tuple-element.15), channel_id=1, source_target_pairs={{0,8},{8,0},{16,24},{24,16},{32,40},{40,32},{48,56},{56,48},{64,72... | collective-permute-start | bytes 393224 | tf_op jit(solution)/shard_map/ppermute | solution.py:530
  17.6 1.9 %collective-permute-start.1 = (f32[256,128]{1,0:T(8,128)S(1)}, f32[256,128]{1,0:T(8,128)S(1)}, u32[]{:S(2)}, u32[]{:S(2)}) collective-permute-start(f32[256,128]{1,0:T(8,128)S(1)} %get-tuple-element.16), channel_id=1, source_target_pairs={{0,504},{8,16},{16,8},{24,32},{32,24},{40,48},{48,40},{56,64},{64,... | collective-permute-start | bytes 393224 | tf_op jit(solution)/shard_map/ppermute | solution.py:530
  19.5 0.0 collective-permute-done.near_ref
  19.5 4.6 %collective-permute-done.1.far_ref = f32[256,128]{1,0:T(8,128)S(1)} collective-permute-done((f32[256,128]{1,0:T(8,128)S(1)}, f32[256,128]{1,0:T(8,128)S(1)}, u32[]{:S(2)}, u32[]{:S(2)}) %collective-permute-start.1) | collective-permute-done | bytes 131104 | tf_op jit(solution)/shard_map/ppermute | solution.py:530
  24.1 2.3 %all-to-all-done = f32[32,32,128]{2,1,0:T(8,128)S(1)} async-done(((f32[32,32,128]{2,1,0:T(8,128)}), f32[32,32,128]{2,1,0:T(8,128)S(1)}, u32[]{:S(2)}, u32[]{:S(2)}) %all-to-all-start) | async-done | bytes 524320 | tf_op jit(solution)/shard_map/all_to_all | solution.py:561
  26.4 0.9 shard_map.101
  27.3 28.4 %all_to_all.20 = f32[16,9,2,128]{3,2,1,0:T(2,128)S(1)} all-to-all(f32[16,9,2,128]{3,2,1,0:T(2,128)S(1)} %bitcast.18), channel_id=1, replica_groups=mesh['x'=4,'z_lo'=8,'core'=2,'z_hi'=2,'y'=4] {'z_lo','z_hi'}, dimensions={0} | all-to-all | bytes 294912 | tf_op jit(solution)/shard_map/all_to_all | solution.py:569
  55.7 1.1 %shard_map.102 = (f32[4,32,512]{2,1,0:T(8,128)S(1)}, f32[32,128]{1,0:T(8,128)S(1)}) custom-call(s32[3]{0:T(128)S(1)} %copy-done.6, s32[3]{0:T(128)S(1)} %pad_add_fusion.place_ref, s32[3,512]{1,0:T(4,128)S(1)} %copy-done.1, f32[4,32,512]{2,1,0:T(8,128)S(1)} %get-tuple-element.17.joined_ref, f32[288,128]{1,0:T(8,128)S(1)} %bitcast.16), custom_call_target="tpu_custom_call" | custom-call | tf_op jit(solution)/shard_map/pallas_call | solution.py:571
  56.7 14.1 %all_to_all.21 = f32[16,2,128]{2,1,0:T(2,128)S(1)} all-to-all(f32[16,2,128]{2,1,0:T(2,128)S(1)} %bitcast.21), channel_id=1, replica_groups=mesh['x'=4,'z_lo'=8,'core'=2,'z_hi'=2,'y'=4] {'z_lo','z_hi'}, dimensions={0} | all-to-all | bytes 32768 | tf_op jit(solution)/shard_map/all_to_all | solution.py:576
  70.9 0.0 copy-start.5
  70.9 17.1 %all_to_all.22 = f32[16,32,128]{2,1,0:T(8,128)S(1)} all-to-all(f32[16,32,128]{2,1,0:T(8,128)S(1)} %broadcast_in_dim.8), channel_id=1, replica_groups=mesh['x'=4,'z_lo'=8,'core'=2,'z_hi'=2,'y'=4] {'x','y'}, dimensions={0} | all-to-all | bytes 524288 | tf_op jit(solution)/shard_map/all_to_all | solution.py:579
  88.1 0.0 copy-start.7
  88.1 0.0 copy-start.9
  88.1 6.3 %collective-permute-start.2 = (f32[512,128]{1,0:T(8,128)S(1)}, f32[512,128]{1,0:T(8,128)S(1)}, u32[]{:S(2)}, u32[]{:S(2)}) collective-permute-start(f32[512,128]{1,0:T(8,128)S(1)} %bitcast.14), channel_id=1, source_target_pairs={{0,8},{8,0},{1,9},{9,1},{2,10},{10,2},{3,11},{11,3},{4,12},{12,4},... | collective-permute-start | bytes 786440 | tf_op jit(solution)/shard_map/ppermute | solution.py:580
  94.4 1.1 %collective-permute-done.2.twin_ref = f32[512,128]{1,0:T(8,128)S(1)} collective-permute-done((f32[512,128]{1,0:T(8,128)S(1)}, f32[512,128]{1,0:T(8,128)S(1)}, u32[]{:S(2)}, u32[]{:S(2)}) %collective-permute-start.2) | collective-permute-done | bytes 262176 | tf_op jit(solution)/shard_map/ppermute | solution.py:580
  95.5 0.0 copy-done.5
  95.5 0.0 copy-done.7
  95.5 0.0 copy-done.9
  95.5 5.9 %shard_map.103 = f32[512,128]{1,0:T(8,128)} custom-call(s32[3]{0:T(128)S(1)} %copy-done.6, s32[3]{0:T(128)S(1)} %pad_add_fusion.place_ref, f32[2,2]{1,0:T(2,128)S(1)} %copy-done.7, f32[2]{0:T(128)S(1)} %copy-done.9, f32[4,32,512]{2,1,0:T(8,128)S(1)} %get-tuple-element.19.forecast_ref, f32[512,128]{1,0:T(8,128)S(1)} %bitcast.15, ...), custom_call_target="tpu_custom_call" | custom-call | tf_op jit(solution)/shard_map/pallas_call | solution.py:581
  (1 shorter events, 0.0 us)
Async XLA Ops:
  0.0 0.7 copy-start.6
  0.0 0.7 copy-start.8
  0.0 0.7 copy-start.4
  0.0 0.7 copy-start.3
  0.0 0.7 copy-start.2
  0.0 0.7 copy-start.1
  0.8 0.9 copy-start
  4.9 21.6 %all-to-all-start = ((f32[32,32,128]{2,1,0:T(8,128)}), f32[32,32,128]{2,1,0:T(8,128)S(1)}, u32[]{:S(2)}, u32[]{:S(2)}) async-start(f32[32,32,128]{2,1,0:T(8,128)} %bitcast.5), calls=%async_computation | async-start | bytes 1048576 | tf_op jit(solution)/shard_map/all_to_all | solution.py:561
  15.3 4.2 %collective-permute-start = (f32[256,128]{1,0:T(8,128)S(1)}, f32[256,128]{1,0:T(8,128)S(1)}, u32[]{:S(2)}, u32[]{:S(2)}) collective-permute-start(f32[256,128]{1,0:T(8,128)S(1)} %get-tuple-element.15), channel_id=1, source_target_pairs={{0,8},{8,0},{16,24},{24,16},{32,40},{40,32},{48,56},{56,48},{64,72... | collective-permute-start | bytes 393224 | tf_op jit(solution)/shard_map/ppermute | solution.py:530
  17.6 6.6 %collective-permute-start.1 = (f32[256,128]{1,0:T(8,128)S(1)}, f32[256,128]{1,0:T(8,128)S(1)}, u32[]{:S(2)}, u32[]{:S(2)}) collective-permute-start(f32[256,128]{1,0:T(8,128)S(1)} %get-tuple-element.16), channel_id=1, source_target_pairs={{0,504},{8,16},{16,8},{24,32},{32,24},{40,48},{48,40},{56,64},{64,... | collective-permute-start | bytes 393224 | tf_op jit(solution)/shard_map/ppermute | solution.py:530
  70.9 24.6 %copy-start.5 = (f32[3,512]{1,0:T(4,128)S(1)}, f32[3,512]{1,0:T(4,128)}, u32[]{:S(2)}) copy-start(f32[3,512]{1,0:T(4,128)} %value_ref.1) | copy-start | bytes 18436
  88.1 7.5 %copy-start.7 = (f32[2,2]{1,0:T(2,128)S(1)}, f32[2,2]{1,0:T(2,128)}, u32[]{:S(2)}) copy-start(f32[2,2]{1,0:T(2,128)} %spread_ref.1) | copy-start | bytes 52
  88.1 7.5 %copy-start.9 = (f32[2]{0:T(128)S(1)}, f32[2]{0:T(128)}, u32[]{:S(2)}) copy-start(f32[2]{0:T(128)} %error_ref.1) | copy-start | bytes 28
  88.1 7.4 %collective-permute-start.2 = (f32[512,128]{1,0:T(8,128)S(1)}, f32[512,128]{1,0:T(8,128)S(1)}, u32[]{:S(2)}, u32[]{:S(2)}) collective-permute-start(f32[512,128]{1,0:T(8,128)S(1)} %bitcast.14), channel_id=1, source_target_pairs={{0,8},{8,0},{1,9},{9,1},{2,10},{10,2},{3,11},{11,3},{4,12},{12,4},... | collective-permute-start | bytes 786440 | tf_op jit(solution)/shard_map/ppermute | solution.py:580

commit v11 on v10

--- a/solution.py
+++ b/solution.py
@@ -112,6 +112,9 @@
     cell_ref,
     kind_ref,
     mask_ref,
+    target_ref,
+    error_ref,
+    value_ref,
     own_ref,
     first_ref,
     second_ref,
@@ -200,7 +203,7 @@
         send_ref[at + LAYERS : at + PLANE_ROWS, :] = up * high + down * low
 
 
-def collect_kernel(place_ref, recv_ref, own_ref, near_ref, far_ref, joined_ref, send_ref):
+def collect_kernel(place_ref, far_ref, near_ref, recv_ref, own_ref, joined_ref, send_ref):
     even = (place_ref[0] & 1) == 0
     for group in range(GROUPS):
         for column in range(CX):
@@ -550,22 +553,34 @@
     mask = tile_mask.reshape(BATCHES, 1, OBS)
     own, first, second, send = call(
         spread_kernel,
-        [SMEM] * 3 + [VMEM] * 5,
+        [SMEM] * 3 + [VMEM] * 8,
         [
             shape(GROUPS, MEMBERS, CELLS),
             shape(SIDE, CY),
             shape(SIDE, CY),
             shape(PLANES * PLANE_ROWS, CY),
         ],
-    )(batch_order, place, courant, ens, obs_owner, obs_cell, obs_kind, mask)
+    )(
+        batch_order,
+        place,
+        courant,
+        ens,
+        obs_owner,
+        obs_cell,
+        obs_kind,
+        mask,
+        target_spread,
+        obs_error,
+        obs_value,
+    )
     recv = lax.all_to_all(send.reshape(PLANES, PLANE_ROWS, CY), PLANE, 0, 0)
+    second = swapped(second, GX, -1, True)
     first = swapped(first, GX, 1, True)
-    second = swapped(second, GX, -1, True)
     joined, send = call(
         collect_kernel,
         [SMEM] + [VMEM] * 4,
         [shape(GROUPS, MEMBERS, CELLS), shape(LAYERS * LAYER_ROWS, CY)],
-    )(place, recv.reshape(PLANES * PLANE_ROWS, CY), own, first, second)
+    )(place, second, first, recv.reshape(PLANES * PLANE_ROWS, CY), own)
     recv = lax.all_to_all(send.reshape(LAYERS, LAYER_ROWS // 2, 2, CY), LAYER, 0, 0)
     recv = recv.reshape(LAYERS * LAYER_ROWS, CY)
     forecast, send = call(

time: 102 us -> 99.5 us (0.975)
  starting transfers between devices: 20.9 us -> 32.5 us
  blocking collectives: 59.6 us -> 51.7 us
  waiting for transfers between devices: 8.08 us -> 2.1 us
    ppermute x2, starting transfers between devices: 4.16 us -> 15.7 us  [swapped(): return lax.ppermute(value, axis, pairs)]
    all_to_all x1, blocking collectives: 28.4 us -> 20.6 us  [local(): lax.all_to_all(send.reshape(LAYERS, LAYER_ROWS // 2, 2, CY), LAYER, 0, 0)]
    ppermute x2, waiting for transfers between devices: 4.65 us -> 0.96 us  [swapped(): return lax.ppermute(value, axis, pairs)]
    all_to_all x1, waiting for transfers between devices: 2.3 us -> 0.01 us  [local(): recv = lax.all_to_all(send.reshape(PLANES, PLANE_ROWS, CY), PLANE, 0, 0)]
  transfers between devices with their start and end apart: 4 -> 4, of which waited for: 3 -> 2; matrix products, arithmetic and copies ran while one was open for 0% -> 0% of each run, Pallas kernels for 0% -> 0%
where the time goes in v11:
time: 99.5 us; the launch traced here: 99.1 us
  blocking collectives  51.7 us (52%)
  starting transfers between devices  32.5 us (33%)
  Pallas kernels  11 us (11%)
  waiting for transfers between devices  2.1 us (2%)
  local copies, waits for them, and re-layouts  1.65 us (2%)
    all_to_all x1, blocking collectives, local(): lax.all_to_all(send.reshape(LAYERS, LAYER_ROWS // 2, 2, CY), LAYER, 0, 0)  20.6 us
    all_to_all x1, blocking collectives, local(): mine = lax.all_to_all(send, CHIP, 0, 0).reshape(TILES, CY)  16.9 us
    ppermute x2, starting transfers between devices, swapped(): return lax.ppermute(value, axis, pairs)  15.7 us
    all_to_all x1, blocking collectives, local(): recv = lax.all_to_all(send.reshape(LAYERS, 2, CY), LAYER, 0, 0)  14.1 us
    all_to_all x1, starting transfers between devices, local(): recv = lax.all_to_all(send.reshape(PLANES, PLANE_ROWS, CY), PLANE, 0, 0)  10.4 us
    ppermute x1, starting transfers between devices, local(): twin = lax.ppermute(mine, 'core', [(0, 1), (1, 0)])  6.32 us
    pallas_call x1, Pallas kernels, local(): call(assimilate_kernel, [SMEM] * 4 + [VMEM] * 8, [shape(MEMBERS * GROUPS...  5.92 us
    pallas_call x1, Pallas kernels, local(): call(spread_kernel, [SMEM] * 3 + [VMEM] * 8, [shape(GROUPS, MEMBERS, CELL...  3.14 us
  transfers between devices with their start and end apart: 4, of which 2 were waited for; matrix products, arithmetic and copies ran while one was open for 0% of the time, Pallas kernels for 0%

profile of v11, /device:TPU:1, one launch (start us, length us, event | category | flops | bytes accessed | tf_op | source)
XLA Modules:
  0.0 99.1 jit_solution(5053482790982459215)
XLA Ops:
  0.0 0.0 copy-start.8
  0.0 0.0 copy-start.9
  0.0 0.0 copy-start.5
  0.0 0.0 copy-start.6
  0.0 0.0 copy-start.7
  0.0 0.0 copy-start.4
  0.0 0.0 copy-start.3
  0.1 0.0 copy-start.2
  0.1 0.0 copy-start.1
  0.1 0.1 pad_add_fusion.place_ref
  0.2 0.5 copy-done.8
  0.7 0.0 copy-done.9
  0.7 0.1 copy-done.5
  0.7 0.0 copy-done.6
  0.7 0.0 copy-done.7
  0.7 0.0 copy-done.4
  0.8 0.0 copy-done.3
  0.8 0.0 copy-done.2
  0.8 0.0 copy-done.1
  0.8 0.0 copy-start
  0.8 0.9 copy-done
  1.8 3.1 %shard_map.100 = (f32[4,32,512]{2,1,0:T(8,128)S(1)}, f32[256,128]{1,0:T(8,128)S(1)}, f32[256,128]{1,0:T(8,128)S(1)}, f32[1024,128]{1,0:T(8,128)}) custom-call(s32[3]{0:T(128)S(1)} %copy-done.6, s32[3]{0:T(128)S(1)} %pad_add_fusion.place_ref, f32[2]{0:T(128)S(1)} %copy-done.9, f32[512,128]{1,0:T(8,128)S(1)} %bitcast.17, s32[3,512]{1,0:T(4,128)S(1)} %copy-done.1, ...), custom_call_target="tpu_custom_call" | custom-call | tf_op jit(solution)/shard_map/pallas_call | solution.py:554
  4.9 10.4 %all-to-all-start = ((f32[32,32,128]{2,1,0:T(8,128)}), f32[32,32,128]{2,1,0:T(8,128)S(1)}, u32[]{:S(2)}, u32[]{:S(2)}) async-start(f32[32,32,128]{2,1,0:T(8,128)} %bitcast.5), calls=%async_computation | async-start | bytes 1048576 | tf_op jit(solution)/shard_map/all_to_all | solution.py:576
  15.4 1.9 %collective-permute-start = (f32[256,128]{1,0:T(8,128)S(1)}, f32[256,128]{1,0:T(8,128)S(1)}, u32[]{:S(2)}, u32[]{:S(2)}) collective-permute-start(f32[256,128]{1,0:T(8,128)S(1)} %get-tuple-element.13), channel_id=1, source_target_pairs={{0,504},{8,16},{16,8},{24,32},{32,24},{40,48},{48,40},{56,64},{64,... | collective-permute-start | bytes 393224 | tf_op jit(solution)/shard_map/ppermute | solution.py:533
  17.3 13.8 %collective-permute-start.1 = (f32[256,128]{1,0:T(8,128)S(1)}, f32[256,128]{1,0:T(8,128)S(1)}, u32[]{:S(2)}, u32[]{:S(2)}) collective-permute-start(f32[256,128]{1,0:T(8,128)S(1)} %get-tuple-element.14), channel_id=1, source_target_pairs={{0,8},{8,0},{16,24},{24,16},{32,40},{40,32},{48,56},{56,48},{64,72... | collective-permute-start | bytes 393224 | tf_op jit(solution)/shard_map/ppermute | solution.py:533
  31.1 0.0 collective-permute-done.far_ref
  31.1 1.0 collective-permute-done.1.near_ref
  32.0 0.0 all-to-all-done
  32.0 0.9 shard_map.101
  32.9 20.6 %all_to_all.20 = f32[16,9,2,128]{3,2,1,0:T(2,128)S(1)} all-to-all(f32[16,9,2,128]{3,2,1,0:T(2,128)S(1)} %bitcast.18), channel_id=1, replica_groups=mesh['x'=4,'z_lo'=8,'core'=2,'z_hi'=2,'y'=4] {'z_lo','z_hi'}, dimensions={0} | all-to-all | bytes 294912 | tf_op jit(solution)/shard_map/all_to_all | solution.py:584
  53.6 1.1 %shard_map.102 = (f32[4,32,512]{2,1,0:T(8,128)S(1)}, f32[32,128]{1,0:T(8,128)S(1)}) custom-call(s32[3]{0:T(128)S(1)} %copy-done.6, s32[3]{0:T(128)S(1)} %pad_add_fusion.place_ref, s32[3,512]{1,0:T(4,128)S(1)} %copy-done.1, f32[4,32,512]{2,1,0:T(8,128)S(1)} %get-tuple-element.17.joined_ref, f32[288,128]{1,0:T(8,128)S(1)} %bitcast.16), custom_call_target="tpu_custom_call" | custom-call | tf_op jit(solution)/shard_map/pallas_call | solution.py:586
  54.6 14.1 %all_to_all.21 = f32[16,2,128]{2,1,0:T(2,128)S(1)} all-to-all(f32[16,2,128]{2,1,0:T(2,128)S(1)} %bitcast.21), channel_id=1, replica_groups=mesh['x'=4,'z_lo'=8,'core'=2,'z_hi'=2,'y'=4] {'z_lo','z_hi'}, dimensions={0} | all-to-all | bytes 32768 | tf_op jit(solution)/shard_map/all_to_all | solution.py:591
  68.8 16.9 %all_to_all.22 = f32[16,32,128]{2,1,0:T(8,128)S(1)} all-to-all(f32[16,32,128]{2,1,0:T(8,128)S(1)} %broadcast_in_dim.8), channel_id=1, replica_groups=mesh['x'=4,'z_lo'=8,'core'=2,'z_hi'=2,'y'=4] {'x','y'}, dimensions={0} | all-to-all | bytes 524288 | tf_op jit(solution)/shard_map/all_to_all | solution.py:594
  85.7 6.3 %collective-permute-start.2 = (f32[512,128]{1,0:T(8,128)S(1)}, f32[512,128]{1,0:T(8,128)S(1)}, u32[]{:S(2)}, u32[]{:S(2)}) collective-permute-start(f32[512,128]{1,0:T(8,128)S(1)} %bitcast.14), channel_id=1, source_target_pairs={{0,8},{8,0},{1,9},{9,1},{2,10},{10,2},{3,11},{11,3},{4,12},{12,4},... | collective-permute-start | bytes 786440 | tf_op jit(solution)/shard_map/ppermute | solution.py:595
  92.0 1.1 %collective-permute-done.2.twin_ref = f32[512,128]{1,0:T(8,128)S(1)} collective-permute-done((f32[512,128]{1,0:T(8,128)S(1)}, f32[512,128]{1,0:T(8,128)S(1)}, u32[]{:S(2)}, u32[]{:S(2)}) %collective-permute-start.2) | collective-permute-done | bytes 262176 | tf_op jit(solution)/shard_map/ppermute | solution.py:595
  93.1 5.9 %shard_map.103 = f32[512,128]{1,0:T(8,128)} custom-call(s32[3]{0:T(128)S(1)} %copy-done.6, s32[3]{0:T(128)S(1)} %pad_add_fusion.place_ref, f32[2,2]{1,0:T(2,128)S(1)} %copy-done.7, f32[2]{0:T(128)S(1)} %copy-done.8, f32[4,32,512]{2,1,0:T(8,128)S(1)} %get-tuple-element.19.forecast_ref, f32[512,128]{1,0:T(8,128)S(1)} %bitcast.15, ...), custom_call_target="tpu_custom_call" | custom-call | tf_op jit(solution)/shard_map/pallas_call | solution.py:596
  (1 shorter events, 0.0 us)
Async XLA Ops:
  0.0 0.7 copy-start.8
  0.0 0.7 copy-start.9
  0.0 0.7 copy-start.5
  0.0 0.7 copy-start.6
  0.0 0.7 copy-start.7
  0.0 0.7 copy-start.4
  0.0 0.8 copy-start.3
  0.1 0.8 copy-start.2
  0.1 0.8 copy-start.1
  0.8 0.9 copy-start
  4.9 27.1 %all-to-all-start = ((f32[32,32,128]{2,1,0:T(8,128)}), f32[32,32,128]{2,1,0:T(8,128)S(1)}, u32[]{:S(2)}, u32[]{:S(2)}) async-start(f32[32,32,128]{2,1,0:T(8,128)} %bitcast.5), calls=%async_computation | async-start | bytes 1048576 | tf_op jit(solution)/shard_map/all_to_all | solution.py:576
  15.4 15.7 %collective-permute-start = (f32[256,128]{1,0:T(8,128)S(1)}, f32[256,128]{1,0:T(8,128)S(1)}, u32[]{:S(2)}, u32[]{:S(2)}) collective-permute-start(f32[256,128]{1,0:T(8,128)S(1)} %get-tuple-element.13), channel_id=1, source_target_pairs={{0,504},{8,16},{16,8},{24,32},{32,24},{40,48},{48,40},{56,64},{64,... | collective-permute-start | bytes 393224 | tf_op jit(solution)/shard_map/ppermute | solution.py:533
  17.3 14.7 %collective-permute-start.1 = (f32[256,128]{1,0:T(8,128)S(1)}, f32[256,128]{1,0:T(8,128)S(1)}, u32[]{:S(2)}, u32[]{:S(2)}) collective-permute-start(f32[256,128]{1,0:T(8,128)S(1)} %get-tuple-element.14), channel_id=1, source_target_pairs={{0,8},{8,0},{16,24},{24,16},{32,40},{40,32},{48,56},{56,48},{64,72... | collective-permute-start | bytes 393224 | tf_op jit(solution)/shard_map/ppermute | solution.py:533
  85.7 7.5 %collective-permute-start.2 = (f32[512,128]{1,0:T(8,128)S(1)}, f32[512,128]{1,0:T(8,128)S(1)}, u32[]{:S(2)}, u32[]{:S(2)}) collective-permute-start(f32[512,128]{1,0:T(8,128)S(1)} %bitcast.14), channel_id=1, source_target_pairs={{0,8},{8,0},{1,9},{9,1},{2,10},{10,2},{3,11},{11,3},{4,12},{12,4},... | collective-permute-start | bytes 786440 | tf_op jit(solution)/shard_map/ppermute | solution.py:595

commit v12 on v11

--- a/solution.py
+++ b/solution.py
@@ -203,14 +203,14 @@
         send_ref[at + LAYERS : at + PLANE_ROWS, :] = up * high + down * low
 
 
-def collect_kernel(place_ref, far_ref, near_ref, recv_ref, own_ref, joined_ref, send_ref):
+def collect_kernel(place_ref, far_ref, recv_ref, own_ref, joined_ref, send_ref):
     even = (place_ref[0] & 1) == 0
     for group in range(GROUPS):
         for column in range(CX):
             at = (group * 2 + column % 2) * MEMBERS
             part = slice(at, at + MEMBERS)
-            near, far = near_ref[part], far_ref[part]
-            other = jnp.where(even, far, near) if column < 2 else jnp.where(even, near, far)
+            far = far_ref[part]
+            other = jnp.where(even, far, 0.0) if column < 2 else jnp.where(even, 0.0, far)
             cells = slice(column * CY, (column + 1) * CY)
             joined_ref[group, :, cells] = own_ref[group, :, cells] + other
     place_x = place_ref[0]
@@ -272,6 +272,7 @@
     place_ref,
     relay_ref,
     joined_ref,
+    near_ref,
     recv_ref,
     forecast_ref,
     send_ref,
@@ -288,12 +289,16 @@
     above = pltpu.roll(below, CY - 8, 1)
     below = jnp.concatenate([below, pltpu.roll(below, HALF, 1)], axis=0)
     above = jnp.concatenate([above, pltpu.roll(above, HALF, 1)], axis=0)
+    even = (place_ref[0] & 1) == 0
     wide = lax.broadcasted_iota(I32, (MEMBERS, CY), 1)
     for group in range(GROUPS):
         pieces = []
         for x in range(CX):
             at = group * 16 + (x + 2) * 2
-            piece = joined_ref[group, :, x * CY : (x + 1) * CY]
+            part = (group * 2 + x % 2) * MEMBERS
+            near = near_ref[part : part + MEMBERS]
+            near = jnp.where(even, 0.0, near) if x < 2 else jnp.where(even, near, 0.0)
+            piece = joined_ref[group, :, x * CY : (x + 1) * CY] + near
             piece = piece + jnp.where(wide < 2, pltpu.roll(below, CY - at, 1), 0.0)
             piece = piece + jnp.where(wide >= CY - 2, pltpu.roll(above, CY - 2 - at, 1), 0.0)
             pieces.append(piece)
@@ -578,16 +583,16 @@
     first = swapped(first, GX, 1, True)
     joined, send = call(
         collect_kernel,
-        [SMEM] + [VMEM] * 4,
+        [SMEM] + [VMEM] * 3,
         [shape(GROUPS, MEMBERS, CELLS), shape(LAYERS * LAYER_ROWS, CY)],
-    )(place, second, first, recv.reshape(PLANES * PLANE_ROWS, CY), own)
+    )(place, second, recv.reshape(PLANES * PLANE_ROWS, CY), own)
     recv = lax.all_to_all(send.reshape(LAYERS, LAYER_ROWS // 2, 2, CY), LAYER, 0, 0)
     recv = recv.reshape(LAYERS * LAYER_ROWS, CY)
     forecast, send = call(
         merge_kernel,
-        [SMEM] * 3 + [VMEM] * 2,
+        [SMEM] * 3 + [VMEM] * 3,
         [shape(GROUPS, MEMBERS, CELLS), shape(2 * LAYERS, CY)],
-    )(batch_order, place, obs_owner, joined, recv)
+    )(batch_order, place, obs_owner, joined, first, recv)
     recv = lax.all_to_all(send.reshape(LAYERS, 2, CY), LAYER, 0, 0)
     chips = PLANES // 2
     send = jnp.broadcast_to(recv.reshape(1, 2 * LAYERS, CY), (chips, 2 * LAYERS, CY))

time: 99.5 us -> 100 us (level)
  blocking collectives: 51.7 us -> 31 us
  waiting for transfers between devices: 2.1 us -> 17.4 us
  starting transfers between devices: 32.5 us -> 38 us
    all_to_all x1 -> x0, blocking collectives: 20.6 us -> none  [local(): lax.all_to_all(send.reshape(LAYERS, LAYER_ROWS // 2, 2, CY), LAYER, 0, 0)]
    all_to_all x0 -> x1, starting transfers between devices: none -> 13.2 us  [local(): lax.all_to_all(send.reshape(LAYERS, LAYER_ROWS // 2, 2, CY), LAYER, 0, 0)]
    ppermute x2, starting transfers between devices: 15.7 us -> 8.12 us  [swapped(): return lax.ppermute(value, axis, pairs)]
    all_to_all x0 -> x1, waiting for transfers between devices: none -> 6.06 us  [local(): lax.all_to_all(send.reshape(LAYERS, LAYER_ROWS // 2, 2, CY), LAYER, 0, 0)]
    ppermute x2, waiting for transfers between devices: 0.96 us -> 5.62 us  [swapped(): return lax.ppermute(value, axis, pairs)]
    all_to_all x1, waiting for transfers between devices: 0.01 us -> 4.54 us  [local(): recv = lax.all_to_all(send.reshape(PLANES, PLANE_ROWS, CY), PLANE, 0, 0)]
    all_to_all x1, blocking collectives: 16.9 us -> 14.2 us  [local(): mine = lax.all_to_all(send, CHIP, 0, 0).reshape(TILES, CY)]
    all_to_all x1, blocking collectives: 14.1 us -> 16.8 us  [local(): recv = lax.all_to_all(send.reshape(LAYERS, 2, CY), LAYER, 0, 0)]
  transfers between devices with their start and end apart: 4 -> 5, of which waited for: 2 -> 5; matrix products, arithmetic and copies ran while one was open for 0% -> 0% of each run, Pallas kernels for 0% -> 0%
where the time goes in v12:
time: 100 us; the launch traced here: 99.9 us
  starting transfers between devices  38 us (38%)
  blocking collectives  31 us (31%)
  waiting for transfers between devices  17.4 us (17%)
  Pallas kernels  11.7 us (12%)
  local copies, waits for them, and re-layouts  1.65 us (2%)
    all_to_all x1, blocking collectives, local(): recv = lax.all_to_all(send.reshape(LAYERS, 2, CY), LAYER, 0, 0)  16.8 us
    all_to_all x1, blocking collectives, local(): mine = lax.all_to_all(send, CHIP, 0, 0).reshape(TILES, CY)  14.2 us
    all_to_all x1, starting transfers between devices, local(): lax.all_to_all(send.reshape(LAYERS, LAYER_ROWS // 2, 2, CY), LAYER, 0, 0)  13.2 us
    all_to_all x1, starting transfers between devices, local(): recv = lax.all_to_all(send.reshape(PLANES, PLANE_ROWS, CY), PLANE, 0, 0)  10.4 us
    ppermute x2, starting transfers between devices, swapped(): return lax.ppermute(value, axis, pairs)  8.12 us
    ppermute x1, starting transfers between devices, local(): twin = lax.ppermute(mine, 'core', [(0, 1), (1, 0)])  6.32 us
    all_to_all x1, waiting for transfers between devices, local(): lax.all_to_all(send.reshape(LAYERS, LAYER_ROWS // 2, 2, CY), LAYER, 0, 0)  6.06 us
    pallas_call x1, Pallas kernels, local(): call(assimilate_kernel, [SMEM] * 4 + [VMEM] * 8, [shape(MEMBERS * GROUPS...  5.91 us
  transfers between devices with their start and end apart: 5, of which 5 were waited for; matrix products, arithmetic and copies ran while one was open for 0% of the time, Pallas kernels for 0%

profile of v12, /device:TPU:1, one launch (start us, length us, event | category | flops | bytes accessed | tf_op | source)
XLA Modules:
  0.0 99.9 jit_solution(2939336557388538028)
XLA Ops:
  0.0 0.0 copy-start.8
  0.0 0.0 copy-start.9
  0.0 0.0 copy-start.5
  0.0 0.0 copy-start.6
  0.0 0.0 copy-start.7
  0.0 0.0 copy-start.4
  0.0 0.0 copy-start.3
  0.1 0.0 copy-start.2
  0.1 0.0 copy-start.1
  0.1 0.1 pad_add_fusion.place_ref
  0.2 0.5 copy-done.8
  0.7 0.0 copy-done.9
  0.7 0.1 copy-done.5
  0.7 0.0 copy-done.6
  0.7 0.0 copy-done.7
  0.7 0.0 copy-done.4
  0.8 0.0 copy-done.3
  0.8 0.0 copy-done.2
  0.8 0.0 copy-done.1
  0.8 0.0 copy-start
  0.8 0.9 copy-done
  1.8 3.2 %shard_map.100 = (f32[4,32,512]{2,1,0:T(8,128)S(1)}, f32[256,128]{1,0:T(8,128)S(1)}, f32[256,128]{1,0:T(8,128)S(1)}, f32[1024,128]{1,0:T(8,128)}) custom-call(s32[3]{0:T(128)S(1)} %copy-done.6, s32[3]{0:T(128)S(1)} %pad_add_fusion.place_ref, f32[2]{0:T(128)S(1)} %copy-done.9, f32[512,128]{1,0:T(8,128)S(1)} %bitcast.17, s32[3,512]{1,0:T(4,128)S(1)} %copy-done.1, ...), custom_call_target="tpu_custom_call" | custom-call | tf_op jit(solution)/shard_map/pallas_call | solution.py:559
  4.9 10.4 %all-to-all-start = ((f32[32,32,128]{2,1,0:T(8,128)}), f32[32,32,128]{2,1,0:T(8,128)S(1)}, u32[]{:S(2)}, u32[]{:S(2)}) async-start(f32[32,32,128]{2,1,0:T(8,128)} %bitcast.5), calls=%async_computation | async-start | bytes 1048576 | tf_op jit(solution)/shard_map/all_to_all | solution.py:581
  15.4 1.9 %collective-permute-start = (f32[256,128]{1,0:T(8,128)S(1)}, f32[256,128]{1,0:T(8,128)S(1)}, u32[]{:S(2)}, u32[]{:S(2)}) collective-permute-start(f32[256,128]{1,0:T(8,128)S(1)} %get-tuple-element.13), channel_id=1, source_target_pairs={{0,504},{8,16},{16,8},{24,32},{32,24},{40,48},{48,40},{56,64},{64,... | collective-permute-start | bytes 393224 | tf_op jit(solution)/shard_map/ppermute | solution.py:538
  17.3 4.7 %collective-permute-done.far_ref = f32[256,128]{1,0:T(8,128)S(1)} collective-permute-done((f32[256,128]{1,0:T(8,128)S(1)}, f32[256,128]{1,0:T(8,128)S(1)}, u32[]{:S(2)}, u32[]{:S(2)}) %collective-permute-start) | collective-permute-done | bytes 131104 | tf_op jit(solution)/shard_map/ppermute | solution.py:538
  22.0 4.5 %all-to-all-done = f32[32,32,128]{2,1,0:T(8,128)S(1)} async-done(((f32[32,32,128]{2,1,0:T(8,128)}), f32[32,32,128]{2,1,0:T(8,128)S(1)}, u32[]{:S(2)}, u32[]{:S(2)}) %all-to-all-start) | async-done | bytes 524320 | tf_op jit(solution)/shard_map/all_to_all | solution.py:581
  26.5 1.5 %shard_map.101 = (f32[4,32,512]{2,1,0:T(8,128)S(1)}, f32[288,128]{1,0:T(8,128)}) custom-call(s32[3]{0:T(128)S(1)} %pad_add_fusion.place_ref, f32[256,128]{1,0:T(8,128)S(1)} %collective-permute-done.far_ref, f32[1024,128]{1,0:T(8,128)S(1)} %bitcast.13, f32[4,32,512]{2,1,0:T(8,128)S(1)} %get-tuple-element.15.own_ref), custom_call_target="tpu_custom_call" | custom-call | tf_op jit(solution)/shard_map/pallas_call | solution.py:584
  28.0 13.2 %all-to-all-start.1 = ((f32[16,9,2,128]{3,2,1,0:T(2,128)}), f32[16,9,2,128]{3,2,1,0:T(2,128)S(1)}, u32[]{:S(2)}, u32[]{:S(2)}) async-start(f32[16,9,2,128]{3,2,1,0:T(2,128)} %bitcast.7), calls=%async_computation.1 | async-start | bytes 294912 | tf_op jit(solution)/shard_map/all_to_all | solution.py:589
  41.2 6.2 %collective-permute-start.1 = (f32[256,128]{1,0:T(8,128)S(1)}, f32[256,128]{1,0:T(8,128)S(1)}, u32[]{:S(2)}, u32[]{:S(2)}) collective-permute-start(f32[256,128]{1,0:T(8,128)S(1)} %get-tuple-element.17), channel_id=1, source_target_pairs={{0,8},{8,0},{16,24},{24,16},{32,40},{40,32},{48,56},{56,48},{64,72... | collective-permute-start | bytes 393224 | tf_op jit(solution)/shard_map/ppermute | solution.py:538
  47.4 1.0 collective-permute-done.1.near_ref
  48.4 6.1 %all-to-all-done.1 = f32[16,9,2,128]{3,2,1,0:T(2,128)S(1)} async-done(((f32[16,9,2,128]{3,2,1,0:T(2,128)}), f32[16,9,2,128]{3,2,1,0:T(2,128)S(1)}, u32[]{:S(2)}, u32[]{:S(2)}) %all-to-all-start.1) | async-done | bytes 147488 | tf_op jit(solution)/shard_map/all_to_all | solution.py:589
  54.4 1.1 %shard_map.102 = (f32[4,32,512]{2,1,0:T(8,128)S(1)}, f32[32,128]{1,0:T(8,128)S(1)}) custom-call(s32[3]{0:T(128)S(1)} %copy-done.6, s32[3]{0:T(128)S(1)} %pad_add_fusion.place_ref, s32[3,512]{1,0:T(4,128)S(1)} %copy-done.1, f32[4,32,512]{2,1,0:T(8,128)S(1)} %get-tuple-element.16.joined_ref, f32[256,128]{1,0:T(8,128)S(1)} %collective-permute-done.1.near_ref, ...), custom_call_target="tpu_custom_call" | custom-call | tf_op jit(solution)/shard_map/pallas_call | solution.py:591
  55.5 16.8 %all_to_all.20 = f32[16,2,128]{2,1,0:T(2,128)S(1)} all-to-all(f32[16,2,128]{2,1,0:T(2,128)S(1)} %bitcast.20), channel_id=1, replica_groups=mesh['x'=4,'z_lo'=8,'core'=2,'z_hi'=2,'y'=4] {'z_lo','z_hi'}, dimensions={0} | all-to-all | bytes 32768 | tf_op jit(solution)/shard_map/all_to_all | solution.py:596
  72.3 14.2 %all_to_all.21 = f32[16,32,128]{2,1,0:T(8,128)S(1)} all-to-all(f32[16,32,128]{2,1,0:T(8,128)S(1)} %broadcast_in_dim.8), channel_id=1, replica_groups=mesh['x'=4,'z_lo'=8,'core'=2,'z_hi'=2,'y'=4] {'x','y'}, dimensions={0} | all-to-all | bytes 524288 | tf_op jit(solution)/shard_map/all_to_all | solution.py:599
  86.5 6.3 %collective-permute-start.2 = (f32[512,128]{1,0:T(8,128)S(1)}, f32[512,128]{1,0:T(8,128)S(1)}, u32[]{:S(2)}, u32[]{:S(2)}) collective-permute-start(f32[512,128]{1,0:T(8,128)S(1)} %bitcast.14), channel_id=1, source_target_pairs={{0,8},{8,0},{1,9},{9,1},{2,10},{10,2},{3,11},{11,3},{4,12},{12,4},... | collective-permute-start | bytes 786440 | tf_op jit(solution)/shard_map/ppermute | solution.py:600
  92.9 1.1 %collective-permute-done.2.twin_ref = f32[512,128]{1,0:T(8,128)S(1)} collective-permute-done((f32[512,128]{1,0:T(8,128)S(1)}, f32[512,128]{1,0:T(8,128)S(1)}, u32[]{:S(2)}, u32[]{:S(2)}) %collective-permute-start.2) | collective-permute-done | bytes 262176 | tf_op jit(solution)/shard_map/ppermute | solution.py:600
  94.0 5.9 %shard_map.103 = f32[512,128]{1,0:T(8,128)} custom-call(s32[3]{0:T(128)S(1)} %copy-done.6, s32[3]{0:T(128)S(1)} %pad_add_fusion.place_ref, f32[2,2]{1,0:T(2,128)S(1)} %copy-done.7, f32[2]{0:T(128)S(1)} %copy-done.8, f32[4,32,512]{2,1,0:T(8,128)S(1)} %get-tuple-element.19.forecast_ref, f32[512,128]{1,0:T(8,128)S(1)} %bitcast.15, ...), custom_call_target="tpu_custom_call" | custom-call | tf_op jit(solution)/shard_map/pallas_call | solution.py:601
  (1 shorter events, 0.0 us)
Async XLA Ops:
  0.0 0.7 copy-start.8
  0.0 0.7 copy-start.9
  0.0 0.7 copy-start.5
  0.0 0.7 copy-start.6
  0.0 0.7 copy-start.7
  0.0 0.7 copy-start.4
  0.0 0.8 copy-start.3
  0.1 0.8 copy-start.2
  0.1 0.8 copy-start.1
  0.8 0.9 copy-start
  4.9 21.6 %all-to-all-start = ((f32[32,32,128]{2,1,0:T(8,128)}), f32[32,32,128]{2,1,0:T(8,128)S(1)}, u32[]{:S(2)}, u32[]{:S(2)}) async-start(f32[32,32,128]{2,1,0:T(8,128)} %bitcast.5), calls=%async_computation | async-start | bytes 1048576 | tf_op jit(solution)/shard_map/all_to_all | solution.py:581
  15.4 6.6 %collective-permute-start = (f32[256,128]{1,0:T(8,128)S(1)}, f32[256,128]{1,0:T(8,128)S(1)}, u32[]{:S(2)}, u32[]{:S(2)}) collective-permute-start(f32[256,128]{1,0:T(8,128)S(1)} %get-tuple-element.13), channel_id=1, source_target_pairs={{0,504},{8,16},{16,8},{24,32},{32,24},{40,48},{48,40},{56,64},{64,... | collective-permute-start | bytes 393224 | tf_op jit(solution)/shard_map/ppermute | solution.py:538
  28.0 26.4 %all-to-all-start.1 = ((f32[16,9,2,128]{3,2,1,0:T(2,128)}), f32[16,9,2,128]{3,2,1,0:T(2,128)S(1)}, u32[]{:S(2)}, u32[]{:S(2)}) async-start(f32[16,9,2,128]{3,2,1,0:T(2,128)} %bitcast.7), calls=%async_computation.1 | async-start | bytes 294912 | tf_op jit(solution)/shard_map/all_to_all | solution.py:589
  41.2 7.2 %collective-permute-start.1 = (f32[256,128]{1,0:T(8,128)S(1)}, f32[256,128]{1,0:T(8,128)S(1)}, u32[]{:S(2)}, u32[]{:S(2)}) collective-permute-start(f32[256,128]{1,0:T(8,128)S(1)} %get-tuple-element.17), channel_id=1, source_target_pairs={{0,8},{8,0},{16,24},{24,16},{32,40},{40,32},{48,56},{56,48},{64,72... | collective-permute-start | bytes 393224 | tf_op jit(solution)/shard_map/ppermute | solution.py:538
  86.5 7.5 %collective-permute-start.2 = (f32[512,128]{1,0:T(8,128)S(1)}, f32[512,128]{1,0:T(8,128)S(1)}, u32[]{:S(2)}, u32[]{:S(2)}) collective-permute-start(f32[512,128]{1,0:T(8,128)S(1)} %bitcast.14), channel_id=1, source_target_pairs={{0,8},{8,0},{1,9},{9,1},{2,10},{10,2},{3,11},{11,3},{4,12},{12,4},... | collective-permute-start | bytes 786440 | tf_op jit(solution)/shard_map/ppermute | solution.py:600
